TPU v7x, 32 devices: a whole 2x2x4 slice. The times are simulated.
32 devices in a mesh: tower: 2 (over core), batch: 16 (over z, y, x).
Axes of the slice: x: 2, y: 2, z: 4, core: 2. Of those that a mesh axis runs over, the one named last changes fastest.
Arguments:
- tokens: bfloat16 [2, 32, 512, 768], P('tower', 'batch'), may hold values from -7 to 7
- lengths: int32 [2, 32], P('tower', 'batch'), may hold values from 128 to 512, as said below
- doc_groups: int32 [32], replicated, may hold values from 0 to 7, never falling along the last dimension, each value on 1 to 16 neighbouring positions
- positives: int32 [32], replicated, may hold values from 0 to 31, each once
- cotangent: bfloat16 [2, 32, 512, 768], P('tower', 'batch'), may hold values from -6 to 6
- w_query: bfloat16 [768, 768], replicated, may hold values from -0.0546875 to 0.0546875
- w_key: bfloat16 [768, 768], replicated, may hold values from -0.21875 to 0.21875
- w_value: bfloat16 [768, 768], replicated, may hold values from -0.21875 to 0.21875
- w_mixed: bfloat16 [768, 768], replicated, may hold values from -0.625 to 0.625
- w_inner: bfloat16 [768, 3072], replicated, may hold values from -0.21875 to 0.21875
- w_outer: bfloat16 [3072, 768], replicated, may hold values from -0.109375 to 0.109375
- gain_attn: float32 [768], replicated, may hold values from 0.25 to 1.75
- gain_ffn: float32 [768], replicated, may hold values from 0.25 to 1.75
- rel_table: float32 [32, 12], replicated, may hold values from -4 to 4
Outputs:
- activations: bfloat16 [2, 32, 512, 768], P('tower', 'batch')
- pooled: float32 [2, 32, 768], P('tower', 'batch')
- loss: float32 [], replicated
- tokens_grad: bfloat16 [2, 32, 512, 768], P('tower', 'batch')
- w_query_grad: float32 [768, 768], replicated
- w_key_grad: float32 [768, 768], replicated
- w_value_grad: float32 [768, 768], replicated
- w_mixed_grad: float32 [768, 768], replicated
- w_inner_grad: float32 [768, 3072], replicated
- w_outer_grad: float32 [3072, 768], replicated
- gain_attn_grad: float32 [768], replicated
- gain_ffn_grad: float32 [768], replicated
- rel_table_grad: float32 [32, 12], replicated
Inputs may be any that keep to these rules, and one draw needn't show every extreme that they name: `doc_groups`: group numbers never fall along the rows; each group holds 1 to 16 documents. `positives`: each document row is named once. `lengths`: each tower has at least one row whose length is exactly 512.
All inputs are finite; a program needn't handle non-finite values.
Results may differ from a plain program's by a relative error of at most 0.014.
The roundings to bfloat16 on the way count: a program that leaves them out, or rounds other values in their place, can miss the bound.
Values sent between devices are 32-bit elements; how exact they have to be, the bound alone decides.
A program may use at most 320 MiB of HBM per device.

v0:
```python
import jax
import jax.numpy as jnp
from jax import lax
from jax.sharding import PartitionSpec as P

EPSILON = 1e-06
SCALE = 50.0
NEGATIVE = -1000000000.0
THRESHOLDS = (12, 16, 23, 32, 46, 64, 91)
HIGHEST = lax.Precision.HIGHEST


def bucket_ids(length):
    places = jnp.arange(length, dtype=jnp.int32)
    offsets = places[None, :] - places[:, None]
    distance = jnp.abs(offsets)
    distant = 8 + sum(((distance >= limit).astype(jnp.int32) for limit in THRESHOLDS))
    buckets = jnp.where(distance < 8, distance, distant)
    return buckets + 16 * (offsets > 0).astype(jnp.int32)


def bucket_onehot(length, count_buckets):
    ids = bucket_ids(length)
    return (ids[:, :, None] == jnp.arange(count_buckets, dtype=jnp.int32)[None, None, :]).astype(
        jnp.float32
    )


def normalize(values, gain_vec):
    return values * lax.rsqrt(jnp.mean(values * values, -1, keepdims=True) + EPSILON) * gain_vec


def contrast(stacked, doc_groups, positives):
    unit_vecs = stacked * lax.rsqrt(jnp.sum(stacked * stacked, -1, keepdims=True) + EPSILON)
    scores = SCALE * jnp.dot(
        unit_vecs[0], unit_vecs[1].T, precision=HIGHEST, preferred_element_type=jnp.float32
    )
    indices = jnp.arange(doc_groups.shape[0], dtype=jnp.int32)
    chosen = positives[:, None] == indices[None, :]
    query_groups = jnp.sum(jnp.where(chosen, doc_groups[None, :], 0), 1)
    same_group = query_groups[:, None] == doc_groups[None, :]
    masked = jnp.where(same_group, scores, NEGATIVE)
    highest = jnp.max(masked, 1, keepdims=True)
    log_total = highest[:, 0] + jnp.log(jnp.sum(jnp.exp(masked - highest), 1))
    matched = jnp.sum(jnp.where(chosen, scores, 0.0), 1)
    return jnp.sum(log_total - matched)


def smooth(values):
    return jax.nn.gelu(values, approximate=False)


def matmul(left, right):
    return jnp.dot(left, right, preferred_element_type=jnp.float32)


def left_product(left, right):
    return lax.dot_general(
        left, right, (((0,), (0,)), ((), ())), preferred_element_type=jnp.float32
    )


def right_product(left, right):
    return lax.dot_general(
        left, right, (((1,), (1,)), ((), ())), preferred_element_type=jnp.float32
    )


def padded(matrix, slots):
    extra = -matrix.shape[0] % slots
    return jnp.pad(matrix, ((0, extra),) + ((0, 0),) * (matrix.ndim - 1))


def shards(
    tokens,
    lengths,
    doc_groups,
    positives,
    cotangent,
    w_query,
    w_key,
    w_value,
    w_mixed,
    w_inner,
    w_outer,
    gain_attn,
    gain_ffn,
    rel_table,
):
    rows_dev = tokens.shape[1]
    seq_len = tokens.shape[2]
    width = tokens.shape[3]
    heads = rel_table.shape[1]
    head_size = width // heads
    count = rows_dev * seq_len
    inputs = tokens.reshape(count, width).astype(jnp.float32)
    row_lengths = lengths.reshape(rows_dev)
    length_f = row_lengths.astype(jnp.float32)
    present = jnp.arange(seq_len, dtype=jnp.int32)[None, :] < row_lengths[:, None]
    onehot = bucket_onehot(seq_len, rel_table.shape[0])
    bias = jnp.einsum("qkb,bh->hqk", onehot, rel_table, precision=HIGHEST)

    def split_heads(matrix):
        return matrix.reshape(rows_dev, seq_len, heads, head_size)

    normed1, norm_back1 = jax.vjp(normalize, inputs, gain_attn)
    normed1 = normed1.astype(jnp.bfloat16)
    queries = matmul(normed1, w_query).astype(jnp.bfloat16)
    keys_all = matmul(normed1, w_key).astype(jnp.bfloat16)
    values_all = matmul(normed1, w_value).astype(jnp.bfloat16)

    def score_of():
        raw = (
            jnp.einsum(
                "rqhd,rkhd->rhqk",
                split_heads(queries),
                split_heads(keys_all),
                preferred_element_type=jnp.float32,
            )
            + bias[None]
        )
        return jnp.where(present[:, None, None, :], raw, NEGATIVE)

    scores = score_of()
    highest = jnp.max(scores, -1, keepdims=True)
    log_sums = highest + jnp.log(jnp.sum(jnp.exp(scores - highest), -1, keepdims=True))
    weights_soft = jnp.exp(scores - log_sums)
    heads_out = jnp.einsum(
        "rhqk,rkhd->rqhd",
        weights_soft.astype(jnp.bfloat16),
        split_heads(values_all),
        preferred_element_type=jnp.float32,
    )
    heads_out = heads_out.reshape(count, width).astype(jnp.bfloat16)
    hidden1 = inputs + matmul(heads_out, w_mixed)
    normed2, norm_back2 = jax.vjp(normalize, hidden1, gain_ffn)
    normed2 = normed2.astype(jnp.bfloat16)
    inner_pre = matmul(normed2, w_inner)
    activated, smooth_back = jax.vjp(smooth, inner_pre)
    activated = activated.astype(jnp.bfloat16)
    output = hidden1 + matmul(activated, w_outer)
    activations = output.astype(jnp.bfloat16).reshape(tokens.shape)
    row_outputs = output.reshape(rows_dev, seq_len, width)
    pooled = jnp.sum(jnp.where(present[:, :, None], row_outputs, 0.0), 1) / length_f[:, None]
    gathered = lax.all_gather(pooled[None], ("tower", "batch"), axis=1, tiled=True)[0]
    position = lax.axis_index(("tower", "batch"))

    def summed_loss(every):
        return contrast(every.reshape(2, -1, width), doc_groups, positives)

    summed_ce, loss_back = jax.vjp(summed_loss, gathered)
    grad_every = loss_back(jnp.ones((), jnp.float32))[0]
    loss = summed_ce / doc_groups.shape[0]
    grad_pooled = lax.dynamic_slice_in_dim(grad_every, position * rows_dev, rows_dev, 0)
    spread_grad = jnp.where(
        present[:, :, None], grad_pooled[:, None, :] / length_f[:, None, None], 0.0
    )
    grad_output = cotangent.reshape(count, width).astype(jnp.float32) + spread_grad.reshape(
        count, width
    )
    grad_out_b = grad_output.astype(jnp.bfloat16)
    w_outer_grad = left_product(activated, grad_out_b)
    grad_act = right_product(grad_out_b, w_outer)
    grad_inner = smooth_back(grad_act)[0].astype(jnp.bfloat16)
    w_inner_grad = left_product(normed2, grad_inner)
    grad_normed2 = right_product(grad_inner, w_inner)
    grad_hid_norm, gain_ffn_grad = norm_back2(grad_normed2)
    grad_hidden1 = grad_output + grad_hid_norm
    grad_attn_b = grad_hidden1.astype(jnp.bfloat16)
    w_mixed_grad = left_product(heads_out, grad_attn_b)
    grad_heads = right_product(grad_attn_b, w_mixed).astype(jnp.bfloat16)
    again = jnp.exp(score_of() - log_sums)
    grad_soft = jnp.einsum(
        "rqhd,rkhd->rhqk",
        split_heads(grad_heads),
        split_heads(values_all),
        preferred_element_type=jnp.float32,
    )
    row_delta = jnp.sum(again * grad_soft, -1, keepdims=True)
    grad_scores = (again * (grad_soft - row_delta)).astype(jnp.bfloat16)
    grad_query = (
        jnp.einsum(
            "rhqk,rkhd->rqhd",
            grad_scores,
            split_heads(keys_all),
            preferred_element_type=jnp.float32,
        )
        .reshape(count, width)
        .astype(jnp.bfloat16)
    )
    grad_key = (
        jnp.einsum(
            "rhqk,rqhd->rkhd", grad_scores, split_heads(queries), preferred_element_type=jnp.float32
        )
        .reshape(count, width)
        .astype(jnp.bfloat16)
    )
    grad_value = (
        jnp.einsum(
            "rhqk,rqhd->rkhd",
            again.astype(jnp.bfloat16),
            split_heads(grad_heads),
            preferred_element_type=jnp.float32,
        )
        .reshape(count, width)
        .astype(jnp.bfloat16)
    )
    bias_grad = jnp.sum(grad_scores.astype(jnp.float32), 0)
    table_grad = jnp.einsum("qkb,hqk->bh", onehot, bias_grad, precision=HIGHEST)
    w_query_grad = left_product(normed1, grad_query)
    w_key_grad = left_product(normed1, grad_key)
    w_value_grad = left_product(normed1, grad_value)
    grad_normed1 = (
        right_product(grad_query, w_query)
        + right_product(grad_key, w_key)
        + right_product(grad_value, w_value)
    )
    grad_in_norm, gain_attn_grad = norm_back1(grad_normed1)
    tokens_grad = (grad_hidden1 + grad_in_norm).astype(jnp.bfloat16).reshape(tokens.shape)
    slots = lax.axis_size(("tower", "batch"))
    locals_list = [
        w_query_grad,
        w_key_grad,
        w_value_grad,
        w_mixed_grad,
        w_inner_grad,
        w_outer_grad,
        gain_attn_grad,
        gain_ffn_grad,
        table_grad,
    ]
    members = [padded(member, slots) for member in locals_list]
    shares = (
        lax.psum_scatter(members[0], ("tower", "batch"), scatter_dimension=0, tiled=True),
        lax.psum_scatter(members[1], ("tower", "batch"), scatter_dimension=0, tiled=True),
        lax.psum_scatter(members[2], ("tower", "batch"), scatter_dimension=0, tiled=True),
        lax.psum_scatter(members[3], ("tower", "batch"), scatter_dimension=0, tiled=True),
        lax.psum_scatter(members[4], ("tower", "batch"), scatter_dimension=0, tiled=True),
        lax.psum_scatter(members[5], ("tower", "batch"), scatter_dimension=0, tiled=True),
        lax.psum_scatter(members[6], ("tower", "batch"), scatter_dimension=0, tiled=True),
        lax.psum_scatter(members[7], ("tower", "batch"), scatter_dimension=0, tiled=True),
        lax.psum_scatter(members[8], ("tower", "batch"), scatter_dimension=0, tiled=True),
    )
    summed = (
        lax.all_gather(shares[0], ("tower", "batch"), axis=0, tiled=True),
        lax.all_gather(shares[1], ("tower", "batch"), axis=0, tiled=True),
        lax.all_gather(shares[2], ("tower", "batch"), axis=0, tiled=True),
        lax.all_gather(shares[3], ("tower", "batch"), axis=0, tiled=True),
        lax.all_gather(shares[4], ("tower", "batch"), axis=0, tiled=True),
        lax.all_gather(shares[5], ("tower", "batch"), axis=0, tiled=True),
        lax.all_gather(shares[6], ("tower", "batch"), axis=0, tiled=True),
        lax.all_gather(shares[7], ("tower", "batch"), axis=0, tiled=True),
        lax.all_gather(shares[8], ("tower", "batch"), axis=0, tiled=True),
    )
    results = [whole[: member.shape[0]] for whole, member in zip(summed, locals_list)]
    return (
        activations,
        pooled[None],
        loss,
        tokens_grad,
        results[0],
        results[1],
        results[2],
        results[3],
        results[4],
        results[5],
        results[6],
        results[7],
        results[8],
    )


def solution(mesh):
    return jax.shard_map(
        shards,
        mesh=mesh,
        in_specs=(
            P("tower", "batch", None, None),
            P("tower", "batch"),
            P(),
            P(),
            P("tower", "batch", None, None),
            P(),
            P(),
            P(),
            P(),
            P(),
            P(),
            P(),
            P(),
            P(),
        ),
        out_specs=(
            P("tower", "batch", None, None),
            P("tower", "batch", None),
            P(),
            P("tower", "batch", None, None),
            P(),
            P(),
            P(),
            P(),
            P(),
            P(),
            P(),
            P(),
            P(),
        ),
        check_vma=False,
    )
```

profile of v0, /device:TPU:0, one launch (start us, length us, event | category | flops | bytes accessed | tf_op | source)
XLA Modules:
  0.0 1530.8 jit_solution(14113904634239864576)
XLA Ops:
  7.7 8.8 iota_compare_fusion
  16.5 45.3 %copy.70 = pred[512,512,32]{1,2,0:T(32,128)(4,1)S(1)} copy(pred[512,512,32]{0,2,1:T(32,128)(4,1)} %iota_compare_fusion) | data formatting | bytes 16777216 | tf_op jit(solution)/shard_map/eq | solution.py:24
  61.8 12.2 convolution_bitcast_fusion
  74.0 17.7 %copy.71 = f32[12,512,512]{1,2,0:T(8,128)} copy(f32[12,512,512]{2,0,1:T(8,128)} %convolution_bitcast_fusion) | data formatting | bytes 25165824 | tf_op jit(solution)/shard_map/qkb,bh->hqk/dot_general | solution.py:101
  94.9 2.5 convolution_convert_fusion.5
  97.5 2.6 copy.67
  100.1 4.2 reshape.328
  104.3 4.3 convolution_convert_fusion.6
  108.6 2.6 copy.66
  111.1 3.8 reshape.327
  115.0 14.8 fusion
  129.8 14.2 exponential_reduce_fusion
  144.1 4.7 copy-done.1
  148.8 12.9 fusion.3
  161.7 2.5 convolution_convert_fusion.7
  164.2 2.6 copy.65
  166.8 4.0 reshape.326
  170.8 7.0 fusion.22
  177.9 1.6 copy.74
  180.0 1.7 multiply_reduce_fusion.3
  181.7 36.2 %multiply_convert_fusion.1 = (bf16[1024,3072]{1,0:T(8,128)(2,1)S(1)}, f32[1024,3072]{1,0:T(8,128)}, f32[1024,3072]{1,0:T(8,128)}) fusion(bf16[768,3072]{1,0:T(8,128)(2,1)} %param.23, f32[1024,768]{1,0:T(8,128)S(1)} %get-tuple-element.73, f32[768]{0:T(1024)S(1)} %copy-done.41, f32[1024]{0:T(1024)S(1)} %fusion.58), kind=kOutput, calls=%fused_computation.14 | convolution fusion | flops 5038669824 | bytes 39328768 | tf_op jit(solution)/shard_map/dot_general | solution.py:54
  217.9 6.2 fusion.66
  224.9 71.1 %all_gather.30 = f32[1,64,768]{2,0,1:T(1,128)S(1)} all-gather(f32[1,2,768]{2,0,1:T(1,128)S(1)} %reshape_divide_fusion), channel_id=1, replica_groups=mesh['tower'=2,'batch'=16] {'tower','batch'}, dimensions={1}, use_global_device_ids=true | all-gather | bytes 202752 | tf_op jit(solution)/shard_map/all_gather | solution.py:145
  299.2 16.7 %add_convert_fusion = bf16[1024,3072]{1,0:T(8,128)(2,1)} fusion(f32[1024,3072]{1,0:T(8,128)} %get-tuple-element.67, f32[1024,3072]{1,0:T(8,128)} %get-tuple-element.74, bf16[1024,768]{1,0:T(8,128)(2,1)S(1)} %fusion.13, bf16[3072,768]{1,0:T(8,128)(2,1)} %param.24), kind=kOutput, calls=%fused_computation.13 | convolution fusion | flops 4875878400 | bytes 37748736 | tf_op jit(solution)/shard_map/dot_general | solution.py:64
  316.0 9.0 multiply_reduce_fusion.1
  325.0 1.5 fusion.10
  326.5 1.6 copy-done.6
  328.2 2.6 convolution_convert_fusion.4
  330.8 2.7 copy.75
  333.5 3.8 reshape.332
  337.3 23.1 %multiply_reduce_fusion = (f32[2,12,512]{2,1,0:T(8,128)S(1)}, f32[2,12,512,512]{2,3,1,0:T(8,128)}) fusion(f32[2,12,512,512]{2,3,1,0:T(8,128)} %get-tuple-element.71, f32[2,12,512]{2,1,0:T(8,128)S(1)} %copy-done.28, f32[12,512,512]{1,2,0:T(8,128)} %copy.71, pred[2,512]{1,0:T(4,128)(4,1)S(1)} %iota_compare_fusion.2, ...), kind=kOutput, calls=%fused_computation.3 | convolution fusion | flops 836751360 | bytes 66159616 | tf_op jit(solution)/shard_map/rqhd,rkhd->rhqk/dot_general | solution.py:173
  360.4 31.3 %convert_reduce_fusion = (f32[12,512,512]{1,2,0:T(8,128)}, bf16[2,12,512,512]{2,3,1,0:T(8,128)(2,1)}) fusion(f32[2,12,512,512]{2,3,1,0:T(8,128)} %get-tuple-element.81, f32[2,12,512]{2,1,0:T(8,128)S(1)} %get-tuple-element.80, f32[2,12,512]{2,1,0:T(8,128)S(1)} %copy-done.28, f32[2,12,512,512]{2,3,1,0:T(8,128)} %get-tuple-element.71, f32[12,512,512]{1,2,0:T(8,128)} %copy.71, ...), kind=kLoop, calls=%fused_computation.1 | loop fusion | flops 47185920 | bytes 88179712 | tf_op jit(solution)/shard_map/reduce_sum | solution.py:208
  391.7 6.5 fusion.23
  398.3 1.6 copy.80
  402.0 2.9 fusion.69
  405.1 9.1 fusion.24
  414.2 1.6 copy.83
  417.5 2.8 fusion.70
  420.4 9.1 fusion.25
  429.6 1.6 copy.86
  432.8 2.8 fusion.71
  435.9 5.2 fusion.49
  441.2 10.6 fusion.63
  451.8 9.9 fusion.72
  461.8 38.4 %reduce-scatter.7.cloned.1.call-done = f32[24,768]{1,0:T(8,128)} async-done(((f32[768,768]{1,0:T(8,128)}), f32[24,768]{1,0:T(8,128)}) %reduce-scatter.7.cloned.1.call-update) | async-done | bytes 73744 | tf_op jit(solution)/shard_map/reduce_scatter | solution.py:234
  500.3 104.8 %reduce-scatter.9.cloned.1.call-done = f32[24,768]{1,0:T(8,128)} async-done(((f32[768,768]{1,0:T(8,128)}), f32[24,768]{1,0:T(8,128)}) %reduce-scatter.9.cloned.1.call-update) | async-done | bytes 73744 | tf_op jit(solution)/shard_map/reduce_scatter | solution.py:235
  605.1 103.9 %reduce-scatter.11.cloned.1.call-done = f32[24,768]{1,0:T(8,128)} async-done(((f32[768,768]{1,0:T(8,128)}), f32[24,768]{1,0:T(8,128)}) %reduce-scatter.11.cloned.1.call-update) | async-done | bytes 73744 | tf_op jit(solution)/shard_map/reduce_scatter | solution.py:236
  709.1 104.6 %reduce-scatter.13.cloned.1.call-done = f32[24,768]{1,0:T(8,128)} async-done(((f32[768,768]{1,0:T(8,128)}), f32[24,768]{1,0:T(8,128)}) %reduce-scatter.13.cloned.1.call-update) | async-done | bytes 73744 | tf_op jit(solution)/shard_map/reduce_scatter | solution.py:237
  813.8 141.1 %reduce-scatter.15.cloned.1.call-done = f32[24,3072]{1,0:T(8,128)} async-done(((f32[768,3072]{1,0:T(8,128)}), f32[24,3072]{1,0:T(8,128)}) %reduce-scatter.15.cloned.1.call-update) | async-done | bytes 294928 | tf_op jit(solution)/shard_map/reduce_scatter | solution.py:238
  954.9 141.9 %reduce-scatter.17.cloned.1.call-done = f32[96,768]{1,0:T(8,128)} async-done(((f32[3072,768]{1,0:T(8,128)}), f32[96,768]{1,0:T(8,128)}) %reduce-scatter.17.cloned.1.call-update) | async-done | bytes 294928 | tf_op jit(solution)/shard_map/reduce_scatter | solution.py:239
  1097.4 3.3 fusion.67
  1102.3 3.8 fusion.17
  1106.1 40.5 %all-reduce.8 = (f32[768]{0:T(1024)S(1)}, f32[768]{0:T(1024)S(1)}) all-reduce(f32[768]{0:T(1024)S(1)} %get-tuple-element.54, f32[768]{0:T(1024)S(1)} %get-tuple-element.52), channel_id=8, replica_groups=mesh['tower'=2,'batch'=16] {'tower','batch'}, use_global_device_ids=true, to_apply=%region_24.25.clone | all-reduce | flops 1536 | bytes 12288
  1147.0 24.9 %fusion.36 = f32[32,12]{1,0:T(8,128)S(1)} fusion(f32[12,512,512]{1,2,0:T(8,128)} %get-tuple-element.64, s32[512,512]{0,1:T(8,128)} %copy-done.11), kind=kOutput, calls=%fused_computation.83 | convolution fusion | flops 1216348160 | bytes 13633024 | tf_op jit(solution)/shard_map/qkb,hqk->bh/dot_general | solution.py:209
  1171.9 40.1 %all-reduce.7 = (f32[768]{0:T(1024)}, f32[768]{0:T(1024)}, f32[32,12]{1,0:T(8,128)S(1)}) all-reduce(f32[768]{0:T(1024)S(1)} %dynamic-slice_dynamic-update-slice_fusion.1, f32[768]{0:T(1024)S(1)} %dynamic-slice_dynamic-update-slice_fusion, f32[32,12]{1,0:T(8,128)S(1)} %fusion.36), channel_id=1, replica_groups=mesh['tower'=2,'batch'=16] {'tower','batch'}, use_global_device_ids=true, to_apply=%add.2 | all-reduce | flops 1920 | bytes 15360
  1212.0 65.8 %all-gather = f32[32,1,12]{2,1,0:T(1,128)S(1)} all-gather(f32[1,1,12]{2,1,0:T(1,128)S(1)} %dynamic-slice_bitcast_fusion), channel_id=1, replica_groups=mesh['tower'=2,'batch'=16] {'tower','batch'}, dimensions={0}, use_global_device_ids=true | all-gather | bytes 1584 | tf_op jit(solution)/shard_map/all_gather | solution.py:253
  1279.8 4.8 fusion.12
  1284.6 49.1 %all-gather.14.cloned.1.call-done = f32[768,768]{1,0:T(8,128)} async-done(((f32[24,768]{1,0:T(8,128)}), f32[768,768]{1,0:T(8,128)}) %all-gather.14.cloned.1.call-update) | async-done | bytes 2359312 | tf_op jit(solution)/shard_map/all_gather | solution.py:248
  1333.7 83.9 %all-gather.16.cloned.1.call-done = f32[768,3072]{1,0:T(8,128)} async-done(((f32[24,3072]{1,0:T(8,128)}), f32[768,3072]{1,0:T(8,128)}) %all-gather.16.cloned.1.call-update) | async-done | bytes 9437200 | tf_op jit(solution)/shard_map/all_gather | solution.py:249
  1417.6 83.4 %all-gather.18.cloned.1.call-done = f32[3072,768]{1,0:T(8,128)} async-done(((f32[96,768]{1,0:T(8,128)}), f32[3072,768]{1,0:T(8,128)}) %all-gather.18.cloned.1.call-update) | async-done | bytes 9437200 | tf_op jit(solution)/shard_map/all_gather | solution.py:250
  1501.0 3.4 copy.138
  1508.6 2.0 copy-done.7
  1510.6 3.7 copy.142
  1514.4 8.0 copy.143
  (184 shorter events, 22.3 us)
Async XLA Ops:
  7.2 154.5 %copy-start = (bf16[768,768]{1,0:T(8,128)(2,1)S(1)}, bf16[768,768]{1,0:T(8,128)(2,1)}, u32[]{:S(2)}) copy-start(bf16[768,768]{1,0:T(8,128)(2,1)} %param.21) | copy-start | bytes 3538948
  7.2 493.0 %reduce-scatter.7.cloned.1.call-start = ((), (), s32[]{:S(2)}) async-start(), calls=%async_computation.6 | async-start | bytes 2433024 | tf_op jit(solution)/shard_map/reduce_scatter | solution.py:234
  7.7 8.8 copy-start.11
  16.5 45.3 %copy-start.39 = (f32[32,12]{0,1:T(8,128)S(1)}, f32[32,12]{0,1:T(8,128)}, u32[]{:S(2)}) copy-start(f32[32,12]{0,1:T(8,128)} %param.27) | copy-start | bytes 4612
  74.0 17.7 %copy-start.46 = (s32[1,2]{1,0:T(1,128)S(1)}, s32[1,2]{1,0:T(1,128)}, u32[]{:S(2)}) copy-start(s32[1,2]{1,0:T(1,128)} %param.15) | copy-start | bytes 28
  74.0 18.3 %copy-start.2 = (bf16[1,2,512,768]{3,2,1,0:T(8,128)(2,1)S(1)}, bf16[1,2,512,768]{3,2,1,0:T(8,128)(2,1)}, u32[]{:S(2)}) copy-start(bf16[1,2,512,768]{3,2,1,0:T(8,128)(2,1)} %param.14) | copy-start | bytes 4718596
  74.0 19.3 %copy-start.29 = (f32[768]{0:T(1024)S(1)}, f32[768]{0:T(1024)}, u32[]{:S(2)}) copy-start(f32[768]{0:T(1024)} %param.25) | copy-start | bytes 9220
  91.8 3.2 copy-start.49
  93.3 4.1 copy-start.33
  93.3 4.1 copy-start.31
  93.8 1.1 copy-start.25
  129.8 19.0 %copy-start.1 = (f32[2,12,512,512]{2,3,1,0:T(8,128)S(1)}, f32[2,12,512,512]{2,3,1,0:T(8,128)}, u32[]{:S(2)}) copy-start(f32[2,12,512,512]{2,3,1,0:T(8,128)} %get-tuple-element.71) | copy-start | bytes 75497472
  148.8 12.9 copy-start.27
  148.8 12.9 copy-start.26
  177.9 2.1 copy-start.47
  179.9 1.7 copy-start.18
  179.9 1.7 copy-start.41
  180.0 37.9 %slice-start = ((s8[4718592]{0:T(1024)(128)(4,1)}), s8[4194304]{0:T(1024)(128)(4,1)S(1)}, s32[]{:S(2)}) async-start(s8[4718592]{0:T(1024)(128)(4,1)} %bitcast.164), calls=%async_computation.18 | async-start | bytes 8388608
  181.7 36.2 %copy-start.12 = (f32[1024,768]{1,0:T(8,128)}, f32[1024,768]{1,0:T(8,128)S(1)}, u32[]{:S(2)}) copy-start(f32[1024,768]{1,0:T(8,128)S(1)} %get-tuple-element.73) | copy-start | bytes 9437188
  181.7 36.2 %slice-start.1 = ((s8[4718592]{0:T(1024)(128)(4,1)}), s8[524288]{0:T(1024)(128)(4,1)S(1)}, s32[]{:S(2)}) async-start(s8[4718592]{0:T(1024)(128)(4,1)} %bitcast.164), calls=%async_computation.19 | async-start | bytes 1048576
  217.9 6.3 copy-start.51
  224.1 72.5 %copy-start.38 = (s32[32]{0:T(128)S(1)}, s32[32]{0:T(128)}, u32[]{:S(2)}) copy-start(s32[32]{0:T(128)} %param.16) | copy-start | bytes 388
  224.1 72.5 %copy-start.40 = (s32[32]{0:T(128)S(1)}, s32[32]{0:T(128)}, u32[]{:S(2)}) copy-start(s32[32]{0:T(128)} %param.17) | copy-start | bytes 388
  224.1 74.6 %copy-start.8 = (bf16[1,2,512,768]{3,2,1,0:T(8,128)(2,1)S(1)}, bf16[1,2,512,768]{3,2,1,0:T(8,128)(2,1)}, u32[]{:S(2)}) copy-start(bf16[1,2,512,768]{3,2,1,0:T(8,128)(2,1)} %param.18) | copy-start | bytes 4718596
  297.1 1.5 copy-start.35
  299.2 16.7 %copy-start.21 = (bf16[1024,768]{1,0:T(8,128)(2,1)}, bf16[1024,768]{1,0:T(8,128)(2,1)S(1)}, u32[]{:S(2)}) copy-start(bf16[1024,768]{1,0:T(8,128)(2,1)S(1)} %fusion.13) | copy-start | bytes 4718596
  299.2 16.7 %copy-start.13 = (f32[1024,768]{1,0:T(8,128)S(1)}, f32[1024,768]{1,0:T(8,128)}, u32[]{:S(2)}) copy-start(f32[1024,768]{1,0:T(8,128)} %copy-done.12) | copy-start | bytes 9437188
  325.0 3.2 copy-start.48
  326.5 1.7 copy-start.6
  330.8 6.5 copy-start.5
  330.8 6.5 copy-start.28
  360.4 31.3 %copy-start.4 = (bf16[2,512,12,64]{1,0,3,2:T(2,128)(2,1)S(1)}, bf16[2,512,12,64]{1,0,3,2:T(2,128)(2,1)}, u32[]{:S(2)}) copy-start(bf16[2,512,12,64]{1,0,3,2:T(2,128)(2,1)} %reshape.328) | copy-start | bytes 4718596
  398.2 2.1 copy-start.3
  398.3 2.1 copy-start.30
  398.3 2.1 copy-start.37
  400.3 1.2 copy-start.17
  400.8 1.2 copy-start.22
  404.9 200.2 %reduce-scatter.9.cloned.1.call-start = ((), (), s32[]{:S(2)}) async-start(), calls=%async_computation.8 | async-start | bytes 2433024 | tf_op jit(solution)/shard_map/reduce_scatter | solution.py:235
  414.2 3.3 copy-start.23
  416.3 1.3 copy-start.19
  420.4 288.6 %reduce-scatter.11.cloned.1.call-start = ((), (), s32[]{:S(2)}) async-start(), calls=%async_computation.10 | async-start | bytes 2433024 | tf_op jit(solution)/shard_map/reduce_scatter | solution.py:236
  429.6 3.2 copy-start.24
  431.6 1.1 copy-start.9
  435.6 378.1 %reduce-scatter.13.cloned.1.call-start = ((), (), s32[]{:S(2)}) async-start(), calls=%async_computation.12 | async-start | bytes 2433024 | tf_op jit(solution)/shard_map/reduce_scatter | solution.py:237
  441.2 513.7 %reduce-scatter.15.cloned.1.call-start = ((), (), s32[]{:S(2)}) async-start(), calls=%async_computation.14 | async-start | bytes 9732096 | tf_op jit(solution)/shard_map/reduce_scatter | solution.py:238
  451.8 645.0 %reduce-scatter.17.cloned.1.call-start = ((), (), s32[]{:S(2)}) async-start(), calls=%async_computation.16 | async-start | bytes 9732096 | tf_op jit(solution)/shard_map/reduce_scatter | solution.py:239
  461.8 822.8 %all-gather.8.cloned.1.call-start = ((), (), s32[]{:S(2)}) async-start(), calls=%async_computation.7 | async-start | bytes 2433024 | tf_op jit(solution)/shard_map/all_gather | solution.py:245
  500.2 784.4 %all-gather.10.cloned.1.call-start = ((), (), s32[]{:S(2)}) async-start(), calls=%async_computation.9 | async-start | bytes 2433024 | tf_op jit(solution)/shard_map/all_gather | solution.py:246
  605.1 679.5 %all-gather.12.cloned.1.call-start = ((), (), s32[]{:S(2)}) async-start(), calls=%async_computation.11 | async-start | bytes 2433024 | tf_op jit(solution)/shard_map/all_gather | solution.py:247
  709.1 624.7 %all-gather.14.cloned.1.call-start = ((), (), s32[]{:S(2)}) async-start(), calls=%async_computation.13 | async-start | bytes 2433024 | tf_op jit(solution)/shard_map/all_gather | solution.py:248
  813.7 603.9 %all-gather.16.cloned.1.call-start = ((), (), s32[]{:S(2)}) async-start(), calls=%async_computation.15 | async-start | bytes 9732096 | tf_op jit(solution)/shard_map/all_gather | solution.py:249
  954.9 546.2 %all-gather.18.cloned.1.call-start = ((), (), s32[]{:S(2)}) async-start(), calls=%async_computation.17 | async-start | bytes 9732096 | tf_op jit(solution)/shard_map/all_gather | solution.py:250
  1097.4 3.4 copy-start.20
  1097.4 3.4 copy-start.50
  1100.8 1.5 copy-start.10
  1100.8 1.5 copy-start.32
  1147.0 131.5 %copy-start.36 = (f32[32]{0:T(128)S(1)}, f32[32]{0:T(128)}, u32[]{:S(2)}) copy-start(f32[32]{0:T(128)} %copy-done.35) | copy-start | bytes 388
  1147.0 131.5 %copy-start.43 = (f32[32]{0:T(128)S(1)}, f32[32]{0:T(128)}, u32[]{:S(2)}) copy-start(f32[32]{0:T(128)} %copy-done.42) | copy-start | bytes 388
  1147.0 131.5 %copy-start.44 = (f32[32]{0:T(128)S(1)}, f32[32]{0:T(128)}, u32[]{:S(2)}) copy-start(f32[32]{0:T(128)} %get-tuple-element.58) | copy-start | bytes 388
  1147.0 132.8 %copy-start.34 = (f32[1,4,2,128]{3,1,2,0:T(4,128)S(1)}, f32[1,4,2,128]{3,1,2,0:T(4,128)}, u32[]{:S(2)}) copy-start(f32[1,4,2,128]{3,1,2,0:T(4,128)} %copy-done.33) | copy-start | bytes 12292
  1284.6 219.8 %copy-start.14 = (f32[768,768]{1,0:T(8,128)S(1)}, f32[768,768]{1,0:T(8,128)}, u32[]{:S(2)}) copy-start(f32[768,768]{1,0:T(8,128)} %all-gather.10.cloned.1.call-done) | copy-start | bytes 7077892
  1501.0 4.8 copy-start.15
  1501.0 6.2 copy-start.16
  1504.4 6.2 copy-start.7
  (2 other events, 1.2 us)
Sparse Core Ops, SparseCore 0:
  405.0 95.1 reduce-scatter.6
  506.9 98.0 reduce-scatter.8
  610.9 98.0 reduce-scatter.10
  715.6 98.0 reduce-scatter.12
  820.0 134.7 reduce-scatter.14
  962.2 134.6 reduce-scatter.16
  1099.7 56.6 all-gather.7
  1159.3 56.3 all-gather.9
  1218.6 56.0 all-gather.11
  1277.5 56.1 all-gather.13
  1336.6 80.9 all-gather.15
  1420.3 80.6 all-gather.17
where the time goes:
time: 1540 us; the launch traced here: 1530 us
  waiting for transfers between devices  851 us (55%)
  matrix products  232 us (15%)
  blocking collectives  217 us (14%)
  local copies, waits for them, and re-layouts  132 us (9%)
  other arithmetic  79.5 us (5%)
  between operations  17.1 us (1%)
    reduce_scatter x1, waiting for transfers between devices, shards(): lax.psum_scatter(members[5], ('tower', 'batch'), scatter_dimension=0, til...  142 us
    reduce_scatter x1, waiting for transfers between devices, shards(): lax.psum_scatter(members[4], ('tower', 'batch'), scatter_dimension=0, til...  141 us
    reduce_scatter x1, waiting for transfers between devices, shards(): lax.psum_scatter(members[1], ('tower', 'batch'), scatter_dimension=0, til...  105 us
    reduce_scatter x1, waiting for transfers between devices, shards(): lax.psum_scatter(members[3], ('tower', 'batch'), scatter_dimension=0, til...  105 us
    reduce_scatter x1, waiting for transfers between devices, shards(): lax.psum_scatter(members[2], ('tower', 'batch'), scatter_dimension=0, til...  104 us
    all_gather x1, waiting for transfers between devices, shards(): lax.all_gather(shares[4], ('tower', 'batch'), axis=0, tiled=True)  83.9 us
    all_gather x1, waiting for transfers between devices, shards(): lax.all_gather(shares[5], ('tower', 'batch'), axis=0, tiled=True)  83.4 us
    unnamed x2, blocking collectives  80.6 us
  transfers between devices with their start and end apart: 12, of which 9 were waited for; matrix products, arithmetic and copies ran while one was open for 6% of the time, Pallas kernels for 0%

commit v1 on v0

--- a/solution.py
+++ b/solution.py
@@ -1,6 +1,10 @@
+import functools
+
 import jax
 import jax.numpy as jnp
 from jax import lax
+from jax.experimental import pallas as pl
+from jax.experimental.pallas import tpu as pltpu
 from jax.sharding import PartitionSpec as P
 
 EPSILON = 1e-06
@@ -66,9 +70,256 @@
     )
 
 
-def padded(matrix, slots):
-    extra = -matrix.shape[0] % slots
-    return jnp.pad(matrix, ((0, extra),) + ((0, 0),) * (matrix.ndim - 1))
+LINK = 45.0e3
+CORE = 480.0e3
+MESH = pl.DeviceIdType.MESH
+
+
+class Bit:
+    def __init__(self, axis, mask, place):
+        self.axis, self.mask = axis, mask
+        self.value = lax.rem(lax.div(place[axis], jnp.int32(mask)), jnp.int32(2))
+        other = dict(place)
+        other[axis] = place[axis] + mask * (1 - 2 * self.value)
+        self.partner = (other["tower"], other["batch"])
+
+
+def bit_names(sizes):
+    names = []
+    for axis in ("tower", "batch"):
+        mask = 1
+        while mask < sizes[axis]:
+            names.append((axis, mask))
+            mask *= 2
+    return names
+
+
+def bit_orders(sizes):
+    tower = [k for k, name in enumerate(bit_names(sizes)) if name[0] == "tower"]
+    rest = [k for k, name in enumerate(bit_names(sizes)) if name[0] == "batch"]
+    firsts = [(0, 1, 2), (1, 0, 2), (2, 0, 1), (2, 1, 0)]
+    return [tower + [rest[i] for i in first] + rest[3:] for first in firsts]
+
+
+class Unit:
+    def __init__(self, name, matrix, row, rows, col, cols, order):
+        self.name, self.matrix = name, matrix
+        self.row, self.rows, self.col, self.cols, self.order = row, rows, col, cols, order
+        self.steps = []
+        size = rows
+        back = []
+        recv = 0
+        for k in order:
+            halves = size % 16 == 0
+            sent = size // 2 if halves else size
+            self.steps.append(("halve" if halves else "whole", k, sent, recv))
+            recv += sent
+            if halves:
+                back.append(("double", k, sent, 0))
+                size = sent
+        self.recv_rows = recv
+        self.returns = len(self.steps)
+        self.steps += back[::-1]
+
+    def place_at(self, bits):
+        start = jnp.int32(self.row)
+        self.starts = []
+        stack = []
+        for kind, k, sent, _ in self.steps:
+            self.starts.append(start)
+            if kind == "halve":
+                stack.append(start)
+                start = start + bits[k].value * sent
+            elif kind == "double":
+                start = stack.pop()
+
+
+def service_order(units, names, ready, work=()):
+    free = {k: 0.0 for k in range(len(names))}
+    clock = 0.0
+    waiting = []
+    order = []
+
+    def issue(u, s, now):
+        kind, k, sent, _ = units[u].steps[s]
+        size = sent * units[u].cols * 4
+        rate = CORE if names[k][0] == "tower" else LINK / (2 if names[k][1] == 8 else 1)
+        start = max(now, free[k])
+        free[k] = start + size / rate
+        waiting.append((free[k] + 1.5, u, s))
+
+    for u in range(len(units)):
+        clock = max(clock, ready[u])
+        issue(u, 0, clock)
+    while waiting:
+        waiting.sort()
+        done, u, s = waiting.pop(0)
+        clock = max(clock, done) + 0.3
+        kind, k, sent, _ = units[u].steps[s]
+        if kind != "double":
+            clock += sent * units[u].cols * 4 / 2.0e6
+        order.append((u, s))
+        if s + 1 < len(units[u].steps):
+            issue(u, s + 1, clock)
+    return order, clock
+
+
+class Exchange:
+    def __init__(self, units, bits, grads, kept, land, outs, sems):
+        self.units, self.bits, self.grads, self.kept, self.land, self.outs = units, bits, grads, kept, land, outs
+        self.send_sem, self.recv_sem, self.load_sem, self.store_sem = sems
+        for unit in units:
+            unit.place_at(bits)
+
+    def part(self, refs, unit, start, rows):
+        return refs[unit.matrix].at[pl.ds(pl.multiple_of(start, 8), rows), pl.ds(unit.col, unit.cols)]
+
+    def own(self, u, start, rows):
+        unit = self.units[u]
+        return self.kept[u].at[pl.ds(pl.multiple_of(start - unit.starts[1], 8), rows), :]
+
+    def load(self, u):
+        unit = self.units[u]
+        half = unit.steps[0][2]
+        return pltpu.make_async_copy(
+            self.part(self.grads, unit, unit.starts[1], half), self.kept[u], self.load_sem.at[u]
+        )
+
+    def store(self, u):
+        unit = self.units[u]
+        s = unit.returns
+        start, rows = unit.starts[s], unit.steps[s][2]
+        return pltpu.make_async_copy(
+            self.own(u, start, rows), self.part(self.outs, unit, start, rows), self.store_sem.at[u]
+        )
+
+    def copy(self, u, s):
+        unit = self.units[u]
+        kind, k, sent, recv = unit.steps[s]
+        bit = self.bits[k]
+        start = unit.starts[s]
+        if kind == "halve":
+            start = start + (1 - bit.value) * sent
+        if s == 0:
+            source = self.part(self.grads, unit, start, sent)
+        elif s <= unit.returns:
+            source = self.own(u, start, sent)
+        else:
+            source = self.part(self.outs, unit, start, sent)
+        if kind == "double":
+            target = self.part(self.outs, unit, start, sent)
+        else:
+            target = self.land[u].at[pl.ds(recv, sent), :]
+        return pltpu.make_async_remote_copy(
+            src_ref=source,
+            dst_ref=target,
+            send_sem=self.send_sem.at[u, s],
+            recv_sem=self.recv_sem.at[u, s],
+            device_id=bit.partner,
+            device_id_type=MESH,
+        )
+
+    def begin(self, u):
+        self.load(u).start()
+        self.copy(u, 0).start()
+
+    def serve(self, u, s):
+        unit = self.units[u]
+        if s == 0:
+            self.load(u).wait()
+        self.copy(u, s).wait()
+        kind, k, sent, recv = unit.steps[s]
+        if kind != "double":
+            start = unit.starts[s]
+            if kind == "halve":
+                start = start + self.bits[k].value * sent
+            kept = self.own(u, start, sent)
+            kept[...] = kept[...] + self.land[u][pl.ds(recv, sent), :]
+        if s + 1 == unit.returns:
+            self.store(u).start()
+        if s == unit.returns:
+            self.store(u).wait()
+        if s + 1 < len(unit.steps):
+            self.copy(u, s + 1).start()
+
+
+def gradient_units(sizes):
+    orders = bit_orders(sizes)
+    pattern = (0, 1, 2, 0, 1, 3)
+    units = [Unit("outer%d" % i, 0, 512 * i, 512, 0, 768, orders[pattern[i]]) for i in range(6)]
+    units += [Unit("inner%d" % i, 1, 0, 768, 512 * i, 512, orders[pattern[i]]) for i in range(6)]
+    for i in range(8):
+        units.append(Unit("proj%d" % i, 2 + i // 2, 0, 768, 384 * (i % 2), 384, orders[pattern[i % 6]]))
+    return units
+
+
+def sum_kernel(sizes, units, names, *refs):
+    count = len(units)
+    grads, small_in = refs[:6], refs[6]
+    outs, small_out = refs[7:13], refs[13]
+    kept, land = refs[14 : 14 + count], refs[14 + count : 14 + 2 * count]
+    small_land, send_sem, recv_sem, small_send, small_recv, load_sem, store_sem = refs[14 + 2 * count :]
+    place = {axis: lax.axis_index(axis) for axis in ("tower", "batch")}
+    bits = [Bit(axis, mask, place) for axis, mask in names]
+    exchange = Exchange(units, bits, grads, kept, land, outs, (send_sem, recv_sem, load_sem, store_sem))
+    barrier = pltpu.get_barrier_semaphore()
+    for bit in bits:
+        pl.semaphore_signal(barrier, inc=1, device_id=bit.partner, device_id_type=MESH)
+    pl.semaphore_wait(barrier, len(bits))
+    for u in range(count):
+        exchange.begin(u)
+
+    def small_copy(k):
+        return pltpu.make_async_remote_copy(
+            src_ref=small_out,
+            dst_ref=small_land.at[k],
+            send_sem=small_send.at[k],
+            recv_sem=small_recv.at[k],
+            device_id=bits[k].partner,
+            device_id_type=MESH,
+        )
+
+    small_out[...] = small_in[...]
+    small_copy(0).start()
+    order, _ = service_order(units, names, [0.0] * count)
+    small_at = {len(order) * (k + 1) // (len(bits) + 1): k for k in range(len(bits))}
+    for place_in_order, (u, s) in enumerate(order):
+        if place_in_order in small_at:
+            k = small_at[place_in_order]
+            small_copy(k).wait()
+            small_out[...] = small_out[...] + small_land[k]
+            if k + 1 < len(bits):
+                small_copy(k + 1).start()
+        exchange.serve(u, s)
+
+
+def sum_gradients(sizes, grads, small):
+    units = gradient_units(sizes)
+    names = bit_names(sizes)
+    steps = max(len(unit.steps) for unit in units)
+    any_spec = pl.BlockSpec(memory_space=pl.ANY)
+    vmem_spec = pl.BlockSpec(memory_space=pltpu.VMEM)
+    return pl.pallas_call(
+        functools.partial(sum_kernel, sizes, units, names),
+        out_shape=[jax.ShapeDtypeStruct(g.shape, g.dtype) for g in grads]
+        + [jax.ShapeDtypeStruct(small.shape, small.dtype)],
+        in_specs=[any_spec] * 6 + [vmem_spec],
+        out_specs=[any_spec] * 6 + [vmem_spec],
+        scratch_shapes=[pltpu.VMEM((unit.steps[0][2], unit.cols), jnp.float32) for unit in units]
+        + [pltpu.VMEM((unit.recv_rows, unit.cols), jnp.float32) for unit in units]
+        + [
+            pltpu.VMEM((len(names),) + small.shape, jnp.float32),
+            pltpu.SemaphoreType.DMA((len(units), steps)),
+            pltpu.SemaphoreType.DMA((len(units), steps)),
+            pltpu.SemaphoreType.DMA((len(names),)),
+            pltpu.SemaphoreType.DMA((len(names),)),
+            pltpu.SemaphoreType.DMA((len(units),)),
+            pltpu.SemaphoreType.DMA((len(units),)),
+        ],
+        compiler_params=pltpu.CompilerParams(
+            collective_id=0, has_side_effects=True, vmem_limit_bytes=62 * 2**20
+        ),
+    )(*grads, small)
 
 
 def shards(
@@ -217,42 +468,31 @@
     )
     grad_in_norm, gain_attn_grad = norm_back1(grad_normed1)
     tokens_grad = (grad_hidden1 + grad_in_norm).astype(jnp.bfloat16).reshape(tokens.shape)
-    slots = lax.axis_size(("tower", "batch"))
-    locals_list = [
-        w_query_grad,
-        w_key_grad,
-        w_value_grad,
-        w_mixed_grad,
-        w_inner_grad,
-        w_outer_grad,
-        gain_attn_grad,
-        gain_ffn_grad,
-        table_grad,
+    sizes = {axis: lax.axis_size(axis) for axis in ("tower", "batch")}
+    small = jnp.concatenate(
+        [
+            gain_attn_grad[None],
+            gain_ffn_grad[None],
+            jnp.pad(table_grad.reshape(1, -1), ((0, 0), (0, width - table_grad.size))),
+            jnp.zeros((5, width), jnp.float32),
+        ]
+    )
+    total = sum_gradients(
+        sizes,
+        [w_outer_grad, w_inner_grad, w_query_grad, w_key_grad, w_value_grad, w_mixed_grad],
+        small,
+    )
+    results = [
+        total[2],
+        total[3],
+        total[4],
+        total[5],
+        total[1],
+        total[0],
+        total[6][0],
+        total[6][1],
+        total[6][2, : table_grad.size].reshape(table_grad.shape),
     ]
-    members = [padded(member, slots) for member in locals_list]
-    shares = (
-        lax.psum_scatter(members[0], ("tower", "batch"), scatter_dimension=0, tiled=True),
-        lax.psum_scatter(members[1], ("tower", "batch"), scatter_dimension=0, tiled=True),
-        lax.psum_scatter(members[2], ("tower", "batch"), scatter_dimension=0, tiled=True),
-        lax.psum_scatter(members[3], ("tower", "batch"), scatter_dimension=0, tiled=True),
-        lax.psum_scatter(members[4], ("tower", "batch"), scatter_dimension=0, tiled=True),
-        lax.psum_scatter(members[5], ("tower", "batch"), scatter_dimension=0, tiled=True),
-        lax.psum_scatter(members[6], ("tower", "batch"), scatter_dimension=0, tiled=True),
-        lax.psum_scatter(members[7], ("tower", "batch"), scatter_dimension=0, tiled=True),
-        lax.psum_scatter(members[8], ("tower", "batch"), scatter_dimension=0, tiled=True),
-    )
-    summed = (
-        lax.all_gather(shares[0], ("tower", "batch"), axis=0, tiled=True),
-        lax.all_gather(shares[1], ("tower", "batch"), axis=0, tiled=True),
-        lax.all_gather(shares[2], ("tower", "batch"), axis=0, tiled=True),
-        lax.all_gather(shares[3], ("tower", "batch"), axis=0, tiled=True),
-        lax.all_gather(shares[4], ("tower", "batch"), axis=0, tiled=True),
-        lax.all_gather(shares[5], ("tower", "batch"), axis=0, tiled=True),
-        lax.all_gather(shares[6], ("tower", "batch"), axis=0, tiled=True),
-        lax.all_gather(shares[7], ("tower", "batch"), axis=0, tiled=True),
-        lax.all_gather(shares[8], ("tower", "batch"), axis=0, tiled=True),
-    )
-    results = [whole[: member.shape[0]] for whole, member in zip(summed, locals_list)]
     return (
         activations,
         pooled[None],

time: 1540 us -> 742 us (0.48)
  waiting for transfers between devices: 851 us -> 0 us
  Pallas kernels: 0 us -> 235 us
  blocking collectives: 217 us -> 71.1 us
  matrix products: 232 us -> 216 us
    reduce_scatter x6 -> x0, waiting for transfers between devices: 635 us -> none  [the longest x1 142 us: shards(): lax.psum_scatter(members[5], ('tower', 'batch'), scatter_dimension=0, til...]
    pallas_call x0 -> x1, Pallas kernels: none -> 235 us  [sum_gradients(): pl.pallas_call(functools.partial(sum_kernel, sizes, units, names), out_sh...]
    all_gather x6 -> x0, waiting for transfers between devices: 216 us -> none  [the longest x1 83.9 us: shards(): lax.all_gather(shares[4], ('tower', 'batch'), axis=0, tiled=True)]
    unnamed x2 -> x0, blocking collectives: 80.6 us -> none
    all_gather x1 -> x0, blocking collectives: 65.8 us -> none  [shards(): lax.all_gather(shares[8], ('tower', 'batch'), axis=0, tiled=True)]
    unnamed x127 -> x132, local copies, waits for them, and re-layouts: 36.3 us -> 35.9 us
  transfers between devices with their start and end apart: 12 -> 0, of which waited for: 9 -> 0; matrix products, arithmetic and copies ran while one was open for 6% -> 0% of each run, Pallas kernels for 0% -> 0%
where the time goes in v1:
time: 742 us; the launch traced here: 736 us
  Pallas kernels  235 us (32%)
  matrix products  216 us (29%)
  local copies, waits for them, and re-layouts  134 us (18%)
  other arithmetic  76.5 us (10%)
  blocking collectives  71.1 us (10%)
    pallas_call x1, Pallas kernels, sum_gradients(): pl.pallas_call(functools.partial(sum_kernel, sizes, units, names), out_sh...  235 us
    all_gather x1, blocking collectives, shards(): lax.all_gather(pooled[None], ('tower', 'batch'), axis=1, tiled=True)[0]  71.1 us
    dot_general x6, matrix products, matmul(): return jnp.dot(left, right, preferred_element_type=jnp.float32)  53.9 us
    eq x1, local copies, waits for them, and re-layouts, bucket_onehot(): ids[:, :, None] == jnp.arange(count_buckets, dtype=jnp.int32)[None, None, :]  45.2 us
    unnamed x132, local copies, waits for them, and re-layouts  35.9 us
    dot_general x6, matrix products, right_product(): lax.dot_general(left, right, (((1,), (1,)), ((), ())), preferred_element_...  32.7 us
    reduce_sum x1, other arithmetic, shards(): bias_grad = jnp.sum(grad_scores.astype(jnp.float32), 0)  31.3 us
    dot_general x6, matrix products, left_product(): lax.dot_general(left, right, (((0,), (0,)), ((), ())), preferred_element_...  27.2 us

profile of v1, /device:TPU:0, one launch (start us, length us, event | category | flops | bytes accessed | tf_op | source)
XLA Modules:
  0.0 736.4 jit_solution(4165672916836382773)
XLA Ops:
  1.1 8.8 %iota_compare_fusion = pred[512,512,32]{0,2,1:T(32,128)(4,1)} fusion(s32[512,512]{0,1:T(8,128)S(1)} %fusion.39), kind=kLoop, calls=%fused_computation | loop fusion | flops 8388608 | bytes 9437184 | tf_op jit(solution)/shard_map/eq | solution.py:28
  9.9 45.2 %copy.72 = pred[512,512,32]{1,2,0:T(32,128)(4,1)S(1)} copy(pred[512,512,32]{0,2,1:T(32,128)(4,1)} %iota_compare_fusion) | data formatting | bytes 16777216 | tf_op jit(solution)/shard_map/eq | solution.py:28
  55.1 12.3 %convolution_bitcast_fusion = f32[12,512,512]{2,0,1:T(8,128)} fusion(pred[512,512,32]{1,2,0:T(32,128)(4,1)S(1)} %copy.72, f32[32,12]{0,1:T(8,128)S(1)} %copy-done.36), kind=kOutput, calls=%fused_computation.28 | convolution fusion | flops 1207959552 | bytes 20973056 | tf_op jit(solution)/shard_map/qkb,bh->hqk/dot_general | solution.py:352
  67.4 17.8 %copy.73 = f32[12,512,512]{1,2,0:T(8,128)} copy(f32[12,512,512]{2,0,1:T(8,128)} %convolution_bitcast_fusion) | data formatting | bytes 25165824 | tf_op jit(solution)/shard_map/qkb,bh->hqk/dot_general | solution.py:352
  86.8 1.1 copy-done.24
  87.9 2.5 convolution_convert_fusion.5
  90.5 2.6 copy.69
  93.1 4.0 reshape.335
  97.1 4.3 convolution_convert_fusion.6
  101.4 2.6 copy.68
  103.9 3.8 reshape.334
  107.8 14.8 %fusion = (f32[2,12,512]{2,1,0:T(8,128)S(1)}, f32[2,12,512,512]{2,3,1,0:T(8,128)}) fusion(f32[12,512,512]{1,2,0:T(8,128)} %copy.73, pred[2,512]{1,0:T(4,128)(4,1)S(1)} %iota_compare_fusion.4, bf16[2,512,12,64]{1,0,3,2:T(2,128)(2,1)} %reshape.335, bf16[2,512,12,64]{1,0,3,2:T(2,128)(2,1)} %reshape.334), kind=kOutput, calls=%fused_computation.7 | convolution fusion | flops 824168448 | bytes 40944640 | tf_op jit(solution)/shard_map/rqhd,rkhd->rhqk/dot_general | solution.py:365
  122.6 14.2 %exponential_reduce_fusion = f32[2,12,512]{2,1,0:T(8,128)S(1)} fusion(f32[2,12,512,512]{2,3,1,0:T(8,128)} %get-tuple-element.82, f32[2,12,512]{2,1,0:T(8,128)S(1)} %get-tuple-element.81, f32[12,512,512]{1,2,0:T(8,128)} %copy.73, pred[2,512]{1,0:T(4,128)(4,1)S(1)} %iota_compare_fusion.4), kind=kLoop, calls=%fused_computation.5 | loop fusion | flops 25153536 | bytes 37848064 | tf_op jit(solution)/shard_map/reduce_sum | solution.py:377
  136.9 4.7 copy-done.1
  141.6 12.9 %fusion.3 = bf16[2,12,512,512]{2,3,1,0:T(8,128)(2,1)} fusion(f32[2,12,512,512]{2,3,1,0:T(8,128)S(1)} %copy-done.1, f32[2,12,512]{2,1,0:T(8,128)S(1)} %log_add_fusion, f32[12,512,512]{1,2,0:T(8,128)} %copy.73, pred[2,512]{1,0:T(4,128)(4,1)S(1)} %iota_compare_fusion.4), kind=kLoop, calls=%fused_computation.11 | loop fusion | flops 25165824 | bytes 50381824 | tf_op jit(solution)/shard_map/convert_element_type | solution.py:381
  154.5 2.5 convolution_convert_fusion.7
  157.1 2.6 copy.67
  159.7 4.1 reshape.333
  163.7 7.0 fusion.22
  170.8 1.6 copy.76
  172.9 1.7 multiply_reduce_fusion.3
  174.6 36.6 %multiply_convert_fusion.1 = (bf16[1024,3072]{1,0:T(8,128)(2,1)S(1)}, f32[1024,3072]{1,0:T(8,128)}, f32[1024,3072]{1,0:T(8,128)}) fusion(bf16[768,3072]{1,0:T(8,128)(2,1)} %param.23, f32[1024,768]{1,0:T(8,128)S(1)} %get-tuple-element.84, f32[768]{0:T(1024)S(1)} %copy-done.38, f32[1024]{0:T(1024)S(1)} %fusion.60), kind=kOutput, calls=%fused_computation.14 | convolution fusion | flops 5038669824 | bytes 39328768 | tf_op jit(solution)/shard_map/dot_general | solution.py:58
  211.3 6.2 fusion.68
  219.0 71.1 %all_gather.3 = f32[1,64,768]{2,0,1:T(1,128)S(1)} all-gather(f32[1,2,768]{2,0,1:T(1,128)S(1)} %reshape_divide_fusion), channel_id=1, replica_groups=mesh['tower'=2,'batch'=16] {'tower','batch'}, dimensions={1}, use_global_device_ids=true | all-gather | bytes 202752 | tf_op jit(solution)/shard_map/all_gather | solution.py:396
  294.1 16.7 %add_convert_fusion = bf16[1024,3072]{1,0:T(8,128)(2,1)} fusion(f32[1024,3072]{1,0:T(8,128)} %get-tuple-element.78, f32[1024,3072]{1,0:T(8,128)} %get-tuple-element.85, bf16[1024,768]{1,0:T(8,128)(2,1)S(1)} %fusion.13, bf16[3072,768]{1,0:T(8,128)(2,1)} %param.24), kind=kOutput, calls=%fused_computation.13 | convolution fusion | flops 4875878400 | bytes 37748736 | tf_op jit(solution)/shard_map/dot_general | solution.py:68
  310.7 9.0 %multiply_reduce_fusion.1 = (f32[768]{0:T(1024)S(1)}, f32[1024]{0:T(1024)S(1)}, f32[1024,768]{1,0:T(8,128)S(1)}) fusion(f32[1024,768]{1,0:T(8,128)S(1)} %copy-done.13, f32[1024]{0:T(1024)S(1)} %fusion.60, f32[768]{0:T(1024)S(1)} %copy-done.38, bf16[1024,3072]{1,0:T(8,128)(2,1)} %add_convert_fusion, bf16[768,3072]{1,0:T(8,128)(2,1)} %param.23), kind=kOutput, calls=%fused_computation.51 | convolution fusion | flops 4836554752 | bytes 17315840 | tf_op jit(solution)/shard_map/dot_general | solution.py:68
  319.8 1.5 fusion.10
  321.3 1.7 copy-done.7
  323.0 1.4 convolution_convert_fusion.4
  324.4 1.6 copy.77
  326.0 3.1 reshape.339
  329.1 8.5 %fusion.25 = bf16[2,512,12,64]{1,3,2,0:T(8,128)(2,1)S(1)} fusion(bf16[2,12,512,512]{2,3,1,0:T(8,128)(2,1)} %fusion.3, bf16[2,512,12,64]{1,0,3,2:T(2,128)(2,1)S(1)} %reshape.339), kind=kOutput, calls=%fused_computation.70 | convolution fusion | flops 806092800 | bytes 15728640 | tf_op jit(solution)/shard_map/rhqk,rqhd->rkhd/dot_general | solution.py:450
  337.6 1.6 copy.88
  339.7 22.4 %multiply_reduce_fusion = (f32[2,12,512]{2,1,0:T(8,128)S(1)}, f32[2,12,512,512]{2,3,1,0:T(8,128)}) fusion(f32[2,12,512,512]{2,3,1,0:T(8,128)} %get-tuple-element.82, f32[2,12,512]{2,1,0:T(8,128)S(1)} %copy-done.27, f32[12,512,512]{1,2,0:T(8,128)} %copy.73, pred[2,512]{1,0:T(4,128)(4,1)S(1)} %iota_compare_fusion.4, ...), kind=kOutput, calls=%fused_computation.3 | convolution fusion | flops 836751360 | bytes 66159616 | tf_op jit(solution)/shard_map/rqhd,rkhd->rhqk/dot_general | solution.py:424
  362.1 31.3 %convert_reduce_fusion = (f32[12,512,512]{1,2,0:T(8,128)}, bf16[2,12,512,512]{2,3,1,0:T(8,128)(2,1)}) fusion(f32[2,12,512,512]{2,3,1,0:T(8,128)} %get-tuple-element.92, f32[2,12,512]{2,1,0:T(8,128)S(1)} %get-tuple-element.91, f32[2,12,512]{2,1,0:T(8,128)S(1)} %copy-done.27, f32[2,12,512,512]{2,3,1,0:T(8,128)} %get-tuple-element.82, f32[12,512,512]{1,2,0:T(8,128)} %copy.73, ...), kind=kLoop, calls=%fused_computation.1 | loop fusion | flops 47185920 | bytes 88179712 | tf_op jit(solution)/shard_map/reduce_sum | solution.py:459
  393.4 6.5 fusion.23
  400.0 1.6 copy.82
  402.1 1.1 copy-done.22
  403.2 1.5 fusion.69
  404.7 8.5 %fusion.24 = bf16[2,512,12,64]{1,3,2,0:T(8,128)(2,1)S(1)} fusion(bf16[2,12,512,512]{2,3,1,0:T(8,128)(2,1)} %get-tuple-element.76, bf16[2,512,12,64]{1,0,3,2:T(2,128)(2,1)S(1)} %copy-done.6), kind=kOutput, calls=%fused_computation.69 | convolution fusion | flops 806092800 | bytes 15728640 | tf_op jit(solution)/shard_map/rhqk,rqhd->rkhd/dot_general | solution.py:443
  413.2 1.6 copy.85
  415.3 1.5 fusion.70
  416.8 2.7 fusion.17
  419.6 2.0 fusion.12
  421.6 7.8 %fusion.71.refs_0_ = f32[3072,768]{1,0:T(8,128)} fusion(bf16[1024,3072]{1,0:T(8,128)(2,1)S(1)} %bitcast.170, bf16[1024,768]{1,0:T(8,128)(2,1)S(1)} %copy-done.21), kind=kOutput, calls=%fused_computation.150 | convolution fusion | flops 4831838208 | bytes 17301504 | tf_op jit(solution)/shard_map/dot_general | solution.py:62
  429.4 8.0 %fusion.65.refs_1_ = f32[768,3072]{1,0:T(8,128)} fusion(bf16[1024,3072]{1,0:T(8,128)(2,1)S(1)} %bitcast.168, f32[1024,768]{1,0:T(8,128)S(1)} %copy-done.14, f32[768]{0:T(1024)S(1)} %copy-done.38, f32[1024]{0:T(1024)S(1)} %fusion.60), kind=kOutput, calls=%fused_computation.145 | convolution fusion | flops 4834197504 | bytes 18881536 | tf_op jit(solution)/shard_map/dot_general | solution.py:62
  437.9 1.0 copy-done.23
  438.8 2.9 fusion.72.refs_2_
  441.7 2.8 fusion.73.refs_3_
  444.6 2.8 fusion.74.refs_4_
  447.4 2.8 fusion.49.refs_5_
  450.3 21.7 %fusion.36 = f32[32,12]{1,0:T(8,128)S(1)} fusion(f32[12,512,512]{1,2,0:T(8,128)S(1)} %bitcast.138, s32[512,512]{0,1:T(8,128)S(1)} %copy-done.11), kind=kOutput, calls=%fused_computation.83 | convolution fusion | flops 1216348160 | bytes 13633024 | tf_op jit(solution)/shard_map/qkb,hqk->bh/dot_general | solution.py:460
  472.8 235.1 %shard_map.237 = (f32[3072,768]{1,0:T(8,128)}, f32[768,3072]{1,0:T(8,128)}, f32[768,768]{1,0:T(8,128)}, f32[768,768]{1,0:T(8,128)}, f32[768,768]{1,0:T(8,128)}, /*index=5*/f32[768,768]{1,0:T(8,128)}, f32[8,768]{1,0:T(8,128)}) custom-call(f32[3072,768]{1,0:T(8,128)} %fusion.71.refs_0_, f32[768,3072]{1,0:T(8,128)} %fusion.65.refs_1_, ...), custom_call_target="tpu_custom_call" | custom-call | tf_op jit(solution)/shard_map/pallas_call | solution.py:302
  708.0 1.5 slice_reduce_fusion
  709.5 1.3 slice_reduce_fusion.2
  710.8 0.8 reshape_squeeze.7
  712.3 3.2 copy.141
  715.5 1.4 copy.142
  716.9 1.1 copy-done.16
  718.0 1.4 copy.143
  719.4 1.1 copy-done.15
  720.5 1.4 copy.144
  721.9 9.3 %copy.145 = f32[768,3072]{1,0:T(8,128)} copy(f32[768,3072]{1,0:T(8,128)} %get-tuple-element.117) | data formatting | bytes 18874368
  731.3 3.7 copy.146
  (163 shorter events, 10.5 us)
Async XLA Ops:
  0.6 153.9 %copy-start = (bf16[768,768]{1,0:T(8,128)(2,1)S(1)}, bf16[768,768]{1,0:T(8,128)(2,1)}, u32[]{:S(2)}) copy-start(bf16[768,768]{1,0:T(8,128)(2,1)} %param.21) | copy-start | bytes 3538948
  1.1 8.8 %copy-start.10 = (s32[512,512]{0,1:T(8,128)}, s32[512,512]{0,1:T(8,128)S(1)}, u32[]{:S(2)}) copy-start(s32[512,512]{0,1:T(8,128)S(1)} %fusion.39) | copy-start | bytes 3145732
  9.9 45.3 %copy-start.36 = (f32[32,12]{0,1:T(8,128)S(1)}, f32[32,12]{0,1:T(8,128)}, u32[]{:S(2)}) copy-start(f32[32,12]{0,1:T(8,128)} %param.27) | copy-start | bytes 4612
  67.4 17.9 %copy-start.39 = (s32[1,2]{1,0:T(1,128)S(1)}, s32[1,2]{1,0:T(1,128)}, u32[]{:S(2)}) copy-start(s32[1,2]{1,0:T(1,128)} %param.15) | copy-start | bytes 28
  67.4 17.9 %copy-start.2 = (bf16[1,2,512,768]{3,2,1,0:T(8,128)(2,1)S(1)}, bf16[1,2,512,768]{3,2,1,0:T(8,128)(2,1)}, u32[]{:S(2)}) copy-start(bf16[1,2,512,768]{3,2,1,0:T(8,128)(2,1)} %param.14) | copy-start | bytes 4718596
  67.4 18.9 %copy-start.28 = (f32[768]{0:T(1024)S(1)}, f32[768]{0:T(1024)}, u32[]{:S(2)}) copy-start(f32[768]{0:T(1024)} %param.25) | copy-start | bytes 9220
  85.3 2.7 copy-start.44
  86.3 4.1 copy-start.32
  86.3 4.1 copy-start.30
  86.8 1.1 copy-start.24
  122.6 19.0 %copy-start.1 = (f32[2,12,512,512]{2,3,1,0:T(8,128)S(1)}, f32[2,12,512,512]{2,3,1,0:T(8,128)}, u32[]{:S(2)}) copy-start(f32[2,12,512,512]{2,3,1,0:T(8,128)} %get-tuple-element.82) | copy-start | bytes 75497472
  141.6 12.9 %copy-start.26 = (f32[2,12,512]{2,1,0:T(8,128)}, f32[2,12,512]{2,1,0:T(8,128)S(1)}, u32[]{:S(2)}) copy-start(f32[2,12,512]{2,1,0:T(8,128)S(1)} %log_add_fusion) | copy-start | bytes 147460
  141.6 12.9 %copy-start.25 = (bf16[1024,768]{1,0:T(8,128)(2,1)S(1)}, bf16[1024,768]{1,0:T(8,128)(2,1)}, u32[]{:S(2)}) copy-start(bf16[1024,768]{1,0:T(8,128)(2,1)} %copy-done.24) | copy-start | bytes 4718596
  170.8 2.1 copy-start.41
  172.8 1.7 copy-start.18
  172.9 1.7 copy-start.38
  172.9 38.4 %slice-start.6 = ((s8[4718592]{0:T(1024)(128)(4,1)}), s8[4194304]{0:T(1024)(128)(4,1)S(1)}, s32[]{:S(2)}) async-start(s8[4718592]{0:T(1024)(128)(4,1)} %bitcast.164), calls=%async_computation.6 | async-start | bytes 8388608
  174.6 36.7 %copy-start.12 = (f32[1024,768]{1,0:T(8,128)}, f32[1024,768]{1,0:T(8,128)S(1)}, u32[]{:S(2)}) copy-start(f32[1024,768]{1,0:T(8,128)S(1)} %get-tuple-element.84) | copy-start | bytes 9437188
  174.6 36.7 %slice-start.7 = ((s8[4718592]{0:T(1024)(128)(4,1)}), s8[524288]{0:T(1024)(128)(4,1)S(1)}, s32[]{:S(2)}) async-start(s8[4718592]{0:T(1024)(128)(4,1)} %bitcast.164), calls=%async_computation.7 | async-start | bytes 1048576
  211.3 6.3 copy-start.46
  217.5 0.7 copy-start.40
  217.5 1.3 copy-start.35
  217.6 1.3 copy-start.37
  217.6 76.0 %copy-start.9 = (bf16[1,2,512,768]{3,2,1,0:T(8,128)(2,1)S(1)}, bf16[1,2,512,768]{3,2,1,0:T(8,128)(2,1)}, u32[]{:S(2)}) copy-start(bf16[1,2,512,768]{3,2,1,0:T(8,128)(2,1)} %param.18) | copy-start | bytes 4718596
  294.0 16.7 %copy-start.20 = (bf16[1024,768]{1,0:T(8,128)(2,1)}, bf16[1024,768]{1,0:T(8,128)(2,1)S(1)}, u32[]{:S(2)}) copy-start(bf16[1024,768]{1,0:T(8,128)(2,1)S(1)} %fusion.13) | copy-start | bytes 4718596
  294.0 16.7 %copy-start.13 = (f32[1024,768]{1,0:T(8,128)S(1)}, f32[1024,768]{1,0:T(8,128)}, u32[]{:S(2)}) copy-start(f32[1024,768]{1,0:T(8,128)} %copy-done.12) | copy-start | bytes 9437188
  319.7 3.2 copy-start.42
  321.3 1.7 copy-start.7
  337.6 2.1 copy-start.5
  337.6 2.1 copy-start.27
  362.1 31.3 %copy-start.4 = (bf16[2,512,12,64]{1,0,3,2:T(2,128)(2,1)S(1)}, bf16[2,512,12,64]{1,0,3,2:T(2,128)(2,1)}, u32[]{:S(2)}) copy-start(bf16[2,512,12,64]{1,0,3,2:T(2,128)(2,1)} %reshape.335) | copy-start | bytes 4718596
  400.0 3.2 copy-start.43
  402.1 1.1 copy-start.22
  403.2 1.5 copy-start.6
  413.2 2.1 copy-start.45
  415.2 1.5 copy-start.3
  415.2 1.5 copy-start.29
  415.2 1.5 copy-start.31
  415.3 6.3 slice-start.10
  416.8 2.7 copy-start.33
  416.8 2.7 copy-start.8
  416.8 4.8 slice-start.11
  419.5 2.0 copy-start.21
  419.5 9.8 %slice-start.8 = ((s8[6291456]{0:T(1024)(128)(4,1)}), s8[4194304]{0:T(1024)(128)(4,1)S(1)}, s32[]{:S(2)}) async-start(s8[6291456]{0:T(1024)(128)(4,1)} %bitcast.167), calls=%async_computation.8 | async-start | bytes 8388608
  421.6 7.8 %copy-start.14 = (f32[1024,768]{1,0:T(8,128)S(1)}, f32[1024,768]{1,0:T(8,128)}, u32[]{:S(2)}) copy-start(f32[1024,768]{1,0:T(8,128)} %copy-done.12) | copy-start | bytes 9437188
  421.6 7.8 %slice-start.9 = ((s8[6291456]{0:T(1024)(128)(4,1)}), s8[2097152]{0:T(1024)(128)(4,1)S(1)}, s32[]{:S(2)}) async-start(s8[6291456]{0:T(1024)(128)(4,1)} %bitcast.167), calls=%async_computation.9 | async-start | bytes 4194304
  429.4 8.1 %copy-start.34 = (f32[2,512]{1,0:T(2,128)S(1)}, f32[2,512]{1,0:T(2,128)}, u32[]{:S(2)}) copy-start(f32[2,512]{1,0:T(2,128)} %get-tuple-element.79) | copy-start | bytes 12292
  437.4 1.4 copy-start.23
  441.7 8.5 %slice-start = ((s8[12582912]{0:T(1024)(128)(4,1)}), s8[4194304]{0:T(1024)(128)(4,1)S(1)}, s32[]{:S(2)}) async-start(s8[12582912]{0:T(1024)(128)(4,1)} %bitcast.137), calls=%async_computation | async-start | bytes 8388608
  444.5 2.9 copy-start.19
  444.5 5.7 slice-start.1
  447.4 2.8 slice-start.2
  447.4 2.8 copy-start.11
  708.0 7.5 %copy-start.17 = (f32[768,768]{1,0:T(8,128)S(1)}, f32[768,768]{1,0:T(8,128)}, u32[]{:S(2)}) copy-start(f32[768,768]{1,0:T(8,128)} %get-tuple-element.114) | copy-start | bytes 7077892
  715.5 2.5 copy-start.16
  718.0 2.5 copy-start.15
  720.5 10.7 %slice-start.3 = ((s8[9437184]{0:T(1024)(128)(4,1)}), s8[4194304]{0:T(1024)(128)(4,1)S(1)}, s32[]{:S(2)}) async-start(s8[9437184]{0:T(1024)(128)(4,1)} %bitcast.139), calls=%async_computation.3 | async-start | bytes 8388608
  721.9 9.3 %slice-start.4 = ((s8[9437184]{0:T(1024)(128)(4,1)}), s8[4194304]{0:T(1024)(128)(4,1)S(1)}, s32[]{:S(2)}) async-start(s8[9437184]{0:T(1024)(128)(4,1)} %bitcast.139), calls=%async_computation.4 | async-start | bytes 8388608
  721.9 9.3 %slice-start.5 = ((s8[9437184]{0:T(1024)(128)(4,1)}), s8[1048576]{0:T(1024)(128)(4,1)S(1)}, s32[]{:S(2)}) async-start(s8[9437184]{0:T(1024)(128)(4,1)} %bitcast.139), calls=%async_computation.5 | async-start | bytes 2097152

commit v2 on v1

--- a/solution.py
+++ b/solution.py
@@ -12,62 +12,6 @@
 NEGATIVE = -1000000000.0
 THRESHOLDS = (12, 16, 23, 32, 46, 64, 91)
 HIGHEST = lax.Precision.HIGHEST
-
-
-def bucket_ids(length):
-    places = jnp.arange(length, dtype=jnp.int32)
-    offsets = places[None, :] - places[:, None]
-    distance = jnp.abs(offsets)
-    distant = 8 + sum(((distance >= limit).astype(jnp.int32) for limit in THRESHOLDS))
-    buckets = jnp.where(distance < 8, distance, distant)
-    return buckets + 16 * (offsets > 0).astype(jnp.int32)
-
-
-def bucket_onehot(length, count_buckets):
-    ids = bucket_ids(length)
-    return (ids[:, :, None] == jnp.arange(count_buckets, dtype=jnp.int32)[None, None, :]).astype(
-        jnp.float32
-    )
-
-
-def normalize(values, gain_vec):
-    return values * lax.rsqrt(jnp.mean(values * values, -1, keepdims=True) + EPSILON) * gain_vec
-
-
-def contrast(stacked, doc_groups, positives):
-    unit_vecs = stacked * lax.rsqrt(jnp.sum(stacked * stacked, -1, keepdims=True) + EPSILON)
-    scores = SCALE * jnp.dot(
-        unit_vecs[0], unit_vecs[1].T, precision=HIGHEST, preferred_element_type=jnp.float32
-    )
-    indices = jnp.arange(doc_groups.shape[0], dtype=jnp.int32)
-    chosen = positives[:, None] == indices[None, :]
-    query_groups = jnp.sum(jnp.where(chosen, doc_groups[None, :], 0), 1)
-    same_group = query_groups[:, None] == doc_groups[None, :]
-    masked = jnp.where(same_group, scores, NEGATIVE)
-    highest = jnp.max(masked, 1, keepdims=True)
-    log_total = highest[:, 0] + jnp.log(jnp.sum(jnp.exp(masked - highest), 1))
-    matched = jnp.sum(jnp.where(chosen, scores, 0.0), 1)
-    return jnp.sum(log_total - matched)
-
-
-def smooth(values):
-    return jax.nn.gelu(values, approximate=False)
-
-
-def matmul(left, right):
-    return jnp.dot(left, right, preferred_element_type=jnp.float32)
-
-
-def left_product(left, right):
-    return lax.dot_general(
-        left, right, (((0,), (0,)), ((), ())), preferred_element_type=jnp.float32
-    )
-
-
-def right_product(left, right):
-    return lax.dot_general(
-        left, right, (((1,), (1,)), ((), ())), preferred_element_type=jnp.float32
-    )
 
 
 LINK = 45.0e3
@@ -241,6 +185,692 @@
             self.store(u).wait()
         if s + 1 < len(unit.steps):
             self.copy(u, s + 1).start()
+
+
+LOW = jnp.bfloat16
+FULL = jnp.float32
+
+
+def dot_nn(left, right):
+    return lax.dot_general(left, right, (((1,), (0,)), ((), ())), preferred_element_type=FULL)
+
+
+def dot_nt(left, right):
+    return lax.dot_general(left, right, (((1,), (1,)), ((), ())), preferred_element_type=FULL)
+
+
+def dot_tn(left, right):
+    return lax.dot_general(left, right, (((0,), (0,)), ((), ())), preferred_element_type=FULL)
+
+
+def loop(count, body):
+    def step(i, carry):
+        body(i)
+        return carry
+
+    lax.fori_loop(0, count, step, 0)
+
+
+def rows_of(i, size):
+    return pl.ds(pl.multiple_of(i * size, size), size)
+
+
+def offset_buckets(shift):
+    keys = lax.broadcasted_iota(jnp.int32, (128, 128), 0)
+    queries = lax.broadcasted_iota(jnp.int32, (128, 128), 1)
+    offsets = keys - queries + 128 * shift
+    distance = jnp.abs(offsets)
+    distant = jnp.full((128, 128), 8, jnp.int32)
+    for limit in THRESHOLDS:
+        distant = distant + jnp.where(distance >= limit, 1, 0)
+    buckets = jnp.where(distance < 8, distance, distant)
+    return buckets + jnp.where(offsets > 0, 16, 0)
+
+
+NEAR = ((-1, range(1, 16)), (0, range(32)), (1, range(17, 32)))
+
+
+def bias_strip(bias, table, head, jb, blocks):
+    parts = []
+    for ib in range(blocks):
+        shift = jb - ib
+        if abs(shift) <= 1:
+            parts.append(bias[head, shift + 1])
+        else:
+            parts.append(jnp.full((128, 128), table[31 if shift > 0 else 15, head], FULL))
+    return jnp.concatenate(parts, axis=1)
+
+
+def forward_kernel(
+    tokens, lengths, wq, wk, wv, wm, wi, wo, gain1, gain2, table,
+    q_out, k_out, v_out, ho_out, n1_out, n2_out, h1_out, act_out, slope_out, result_out, lse_out, bias_out, pooled_out,
+    x_s, wq_s, wk_s, wv_s, wm_s, wi_s, wo_s, q_s, k_s, v_s, ho_s, n1_s, n2_s, h1_s, act_s, slope_s, result_s, total_s,
+    score_s, prob_s, in_sem, out_sem,
+):
+    count, width = tokens.shape
+    rows, seq = lengths.shape[0], tokens.shape[0] // lengths.shape[0]
+    heads = table.shape[1]
+    size = width // heads
+    hidden = wi.shape[1]
+    parts = hidden // width
+    loads = [
+        pltpu.make_async_copy(source, target, in_sem.at[i])
+        for i, (source, target) in enumerate(
+            [(tokens, x_s), (wq, wq_s), (wk, wk_s), (wv, wv_s), (wm, wm_s), (wi, wi_s), (wo, wo_s)]
+        )
+    ]
+    for load in loads:
+        load.start()
+    stores = []
+
+    def store(source, target):
+        copy = pltpu.make_async_copy(source, target, out_sem.at[len(stores)])
+        copy.start()
+        stores.append(copy)
+
+    ids = [offset_buckets(shift) for shift, _ in NEAR]
+
+    def bias_of(head):
+        for place, (shift, members) in enumerate(NEAR):
+            block = jnp.zeros((128, 128), FULL)
+            for b in members:
+                block = jnp.where(ids[place] == b, table[b, head], block)
+            bias_out[head, place] = block
+
+    loop(heads, bias_of)
+    block = 256
+    loads[0].wait()
+
+    def norm1(i):
+        at = rows_of(i, block)
+        x = x_s[at, :].astype(FULL)
+        scale = lax.rsqrt(jnp.mean(x * x, -1, keepdims=True) + EPSILON)
+        n1_s[at, :] = (x * scale * gain1[...]).astype(LOW)
+
+    loop(count // block, norm1)
+    store(n1_s, n1_out)
+    for i, (w_s, p_s, p_out) in enumerate(((wq_s, q_s, q_out), (wk_s, k_s, k_out), (wv_s, v_s, v_out))):
+        loads[1 + i].wait()
+
+        def project(m, w_s=w_s, p_s=p_s):
+            at = rows_of(m, 512)
+            p_s[at, :] = dot_nn(n1_s[at, :], w_s[...]).astype(LOW)
+
+        loop(count // 512, project)
+        store(p_s, p_out)
+    blocks = seq // 128
+    lanes = lax.broadcasted_iota(jnp.int32, (seq, 2 * size), 1)
+    keys = lax.broadcasted_iota(jnp.int32, (128, seq), 0)
+
+    def attend(step):
+        row = lax.div(step, jnp.int32(heads // 2))
+        pair = lax.rem(step, jnp.int32(heads // 2))
+        at = rows_of(row, seq)
+        here = rows_of(pair, 2 * size)
+        limit = lengths[row]
+        q, k = q_s[at, here], k_s[at, here]
+        vt = v_s[at, here].T
+        found = []
+        for side in range(2):
+            head = pair * 2 + side
+            chosen = jnp.where((lanes >= size) == (side == 1), q, jnp.zeros_like(q))
+            score_s[side] = dot_nt(k, chosen)
+        for side in range(2):
+            head = pair * 2 + side
+            top = jnp.full((1, seq), NEGATIVE, FULL)
+            for jb in range(blocks):
+                strip = score_s[side, jb * 128 : (jb + 1) * 128, :] + bias_strip(bias_out, table, head, jb, blocks)
+                strip = jnp.where(keys + jb * 128 < limit, strip, NEGATIVE)
+                score_s[side, jb * 128 : (jb + 1) * 128, :] = strip
+                top = jnp.maximum(top, jnp.max(strip, 0, keepdims=True))
+            mass = jnp.zeros((1, seq), FULL)
+            for jb in range(blocks):
+                strip = jnp.exp(score_s[side, jb * 128 : (jb + 1) * 128, :] - top)
+                mass = mass + jnp.sum(strip, 0, keepdims=True)
+                prob_s[side, jb * 128 : (jb + 1) * 128, :] = strip.astype(LOW)
+            lse_out[row * heads + head] = top + jnp.log(mass)
+            found.append(dot_nn(vt[side * size : (side + 1) * size, :], prob_s[side]) / mass)
+        ho_s[at, here] = jnp.concatenate(found, 0).T.astype(LOW)
+
+    loop(rows * (heads // 2), attend)
+    store(ho_s, ho_out)
+    loads[4].wait()
+
+    def mix(i):
+        at = rows_of(i, block)
+        h1 = x_s[at, :].astype(FULL) + dot_nn(ho_s[at, :], wm_s[...])
+        h1_s[at, :] = h1
+        scale = lax.rsqrt(jnp.mean(h1 * h1, -1, keepdims=True) + EPSILON)
+        n2_s[at, :] = (h1 * scale * gain2[...]).astype(LOW)
+
+    loop(count // block, mix)
+    store(h1_s, h1_out)
+    store(n2_s, n2_out)
+    loads[5].wait()
+    loads[6].wait()
+
+    for part in range(parts):
+        columns = pl.ds(part * width, width)
+
+        def feed(i, part=part, columns=columns):
+            at = rows_of(i, block)
+            inner = dot_nn(n2_s[at, :], wi_s[:, columns])
+            share = 0.5 + 0.5 * lax.erf(inner * 0.7071067811865476)
+            act = (inner * share).astype(LOW)
+            act_s[at, columns] = act
+            slope = share + inner * (jnp.exp(inner * inner * -0.5) * 0.3989422804014327)
+            slope_s[at, columns] = slope.astype(LOW)
+            more = dot_nn(act, wo_s[columns, :])
+            if part == 0:
+                total_s[at, :] = h1_s[at, :] + more
+            elif part < parts - 1:
+                total_s[at, :] = total_s[at, :] + more
+            else:
+                output = total_s[at, :] + more
+                total_s[at, :] = output
+                result_s[at, :] = output.astype(LOW)
+
+        loop(count // block, feed)
+        store(act_s.at[:, columns], act_out.at[:, columns])
+        store(slope_s.at[:, columns], slope_out.at[:, columns])
+    store(result_s, result_out)
+    slots = lax.broadcasted_iota(jnp.int32, (seq, 1), 0)
+    for row in range(rows):
+        kept = jnp.where(slots < lengths[row], total_s[row * seq : (row + 1) * seq, :], 0.0)
+        pooled_out[row : row + 1, :] = jnp.sum(kept, 0, keepdims=True) / lengths[row].astype(FULL)
+    for copy in stores:
+        copy.wait()
+
+
+def forward(tokens, lengths, wq, wk, wv, wm, wi, wo, gain1, gain2, table):
+    count, width = tokens.shape
+    hidden = wi.shape[1]
+    rows = lengths.shape[0]
+    heads = table.shape[1]
+    seq = count // rows
+    shape = jax.ShapeDtypeStruct
+    any_spec = pl.BlockSpec(memory_space=pl.ANY)
+    vmem_spec = pl.BlockSpec(memory_space=pltpu.VMEM)
+    smem_spec = pl.BlockSpec(memory_space=pltpu.SMEM)
+    low = shape((count, width), LOW)
+    wide = shape((count, hidden), LOW)
+    weights = [pltpu.VMEM(w.shape, LOW) for w in (wq, wk, wv, wm, wi, wo)]
+    narrow_s = pltpu.VMEM((count, width), LOW)
+    full_s = pltpu.VMEM((count, width), FULL)
+    wide_s = pltpu.VMEM((count, hidden), LOW)
+    return pl.pallas_call(
+        forward_kernel,
+        out_shape=[low, low, low, low, low, low, shape((count, width), FULL), wide, wide, low]
+        + [shape((rows * heads, 1, seq), FULL), shape((heads, 3, 128, 128), FULL), shape((rows, width), FULL)],
+        in_specs=[any_spec, smem_spec] + [any_spec] * 6 + [vmem_spec] * 2 + [smem_spec],
+        out_specs=[any_spec] * 10 + [vmem_spec] * 3,
+        scratch_shapes=[narrow_s]
+        + weights
+        + [narrow_s] * 6
+        + [full_s, wide_s, wide_s, narrow_s, full_s]
+        + [
+            pltpu.VMEM((2, seq, seq), FULL),
+            pltpu.VMEM((2, seq, seq), LOW),
+            pltpu.SemaphoreType.DMA((7,)),
+            pltpu.SemaphoreType.DMA((24,)),
+        ],
+        compiler_params=pltpu.CompilerParams(vmem_limit_bytes=62 * 2**20),
+    )(tokens, lengths, wq, wk, wv, wm, wi, wo, gain1.reshape(1, width), gain2.reshape(1, width), table)
+
+
+def contrast_kernel(units, doc_groups_row, positives_col):
+    count = doc_groups_row.shape[1]
+    queries, documents = units
+    precise = functools.partial(
+        lax.dot_general, precision=HIGHEST, preferred_element_type=FULL
+    )
+    rates = [lax.rsqrt(jnp.sum(p * p, -1, keepdims=True) + EPSILON) for p in units]
+    unit = [p * rate for p, rate in zip(units, rates)]
+    scores = SCALE * precise(unit[0], unit[1], (((1,), (1,)), ((), ())))
+    indices = lax.broadcasted_iota(jnp.int32, (count, count), 1)
+    chosen = positives_col == indices
+    query_groups = jnp.sum(jnp.where(chosen, doc_groups_row, 0), 1, keepdims=True)
+    masked = jnp.where(query_groups == doc_groups_row, scores, NEGATIVE)
+    highest = jnp.max(masked, 1, keepdims=True)
+    weights = jnp.exp(masked - highest)
+    mass = jnp.sum(weights, 1, keepdims=True)
+    matched = jnp.sum(jnp.where(chosen, scores, 0.0), 1, keepdims=True)
+    loss = jnp.sum(highest + jnp.log(mass) - matched, 0, keepdims=True) / count
+    dscore = weights / mass - jnp.where(chosen, 1.0, 0.0)
+    dunit = (
+        SCALE * precise(dscore, unit[1], (((1,), (0,)), ((), ()))),
+        SCALE * precise(dscore, unit[0], (((0,), (0,)), ((), ()))),
+    )
+    dpooled = [
+        rate * (d - u * jnp.sum(u * d, -1, keepdims=True)) for rate, d, u in zip(rates, dunit, unit)
+    ]
+    return loss, dpooled
+
+
+def middle_kernel(
+    sizes, names,
+    cot, pooled, lengths, doc_groups, positives, act, slope, wo, n2,
+    wo_grad, wi_grad, dinner, spread_out, loss_out,
+    cot_s, act_s, slope_s, wo_s, n2_s, dact_s, wo_grad_s, wi_grad_s, mass_s, every_s, pool_s,
+    in_sem, out_sem, send_sem, recv_sem,
+):
+    count, width = cot_s.shape
+    rows = pooled.shape[0]
+    seq = count // rows
+    parts = act_s.shape[1] // width
+    places = sizes["batch"]
+    place = {axis: lax.axis_index(axis) for axis in ("tower", "batch")}
+    tower, batch = place["tower"], place["batch"]
+    bits = [Bit(axis, mask, place) for axis, mask in names]
+    hops = [k for k, name in enumerate(names) if name[0] == "batch"]
+    hops += [k for k, name in enumerate(names) if name[0] == "tower"]
+    loads = []
+
+    def load(source, target):
+        copy = pltpu.make_async_copy(source, target, in_sem.at[len(loads)])
+        copy.start()
+        loads.append(copy)
+
+    def cut(part):
+        return pl.ds(part * width, width)
+
+    load(cot, cot_s)
+    for part in range(parts):
+        load(wo.at[cut(part), :], wo_s.at[cut(part), :])
+    for part in range(parts):
+        load(act.at[:, cut(part)], act_s.at[:, cut(part)])
+    load(n2, n2_s)
+    for part in range(parts):
+        load(slope.at[:, cut(part)], slope_s.at[:, cut(part)])
+    every_s[tower, batch] = pooled[...]
+    barrier = pltpu.get_barrier_semaphore()
+    for bit in bits:
+        pl.semaphore_signal(barrier, inc=1, device_id=bit.partner, device_id_type=MESH)
+    pl.semaphore_wait(barrier, len(bits))
+
+    def hop(h):
+        axis, mask = names[hops[h]]
+        bit = bits[hops[h]]
+        if axis == "batch":
+            first = lax.div(batch, jnp.int32(mask)) * mask
+            block = every_s.at[tower, pl.ds(first, mask)]
+        else:
+            block = every_s.at[tower]
+        return pltpu.make_async_remote_copy(
+            src_ref=block,
+            dst_ref=block,
+            send_sem=send_sem.at[h],
+            recv_sem=recv_sem.at[h],
+            device_id=bit.partner,
+            device_id_type=MESH,
+        )
+
+    hop(0).start()
+    slots = lax.broadcasted_iota(jnp.int32, (seq, 1), 0)
+    columns = lax.broadcasted_iota(jnp.int32, (seq, 128), 1)
+    marks = jnp.concatenate(
+        [
+            jnp.where((slots < lengths[row]) & (columns == row), 1.0, 0.0).astype(LOW)
+            for row in range(rows)
+        ],
+        0,
+    )
+
+    def first_dact(part):
+        loads[1 + part].wait()
+
+        def body(i):
+            at = rows_of(i, 512)
+            dact_s[at, cut(part)] = dot_nt(cot_s[at, :], wo_s[cut(part), :])
+
+        loop(count // 512, body)
+
+    def first_grad(part):
+        loads[1 + parts + part].wait()
+        wo_grad_s[cut(part), :] = dot_tn(act_s[:, cut(part)], cot_s[...])
+        mass_s[cut(part), :] = dot_tn(act_s[:, cut(part)], marks)
+
+    loads[0].wait()
+    work = [functools.partial(first_dact, part) for part in range(parts)]
+    work += [functools.partial(first_grad, part) for part in range(parts)]
+    served = 0
+    for done, item in enumerate(work):
+        item()
+        while served < len(hops) and (served + 1) * len(work) <= (done + 1) * len(hops):
+            hop(served).wait()
+            served += 1
+            if served < len(hops):
+                hop(served).start()
+    for t in range(2):
+        for b in range(places):
+            pool_s[t, b * rows : (b + 1) * rows, :] = every_s[t, b]
+    loss, dpooled = contrast_kernel((pool_s[0], pool_s[1]), doc_groups[...], positives[...])
+    loss_out[...] = loss
+    chosen = jnp.where(tower == 0, dpooled[0], dpooled[1])
+    ids = lax.broadcasted_iota(jnp.int32, (chosen.shape[0], 1), 0)
+    spread = [
+        jnp.sum(jnp.where(ids == batch * rows + row, chosen, 0.0), 0, keepdims=True) / lengths[row].astype(FULL)
+        for row in range(rows)
+    ]
+    for row in range(rows):
+        spread_out[row : row + 1, :] = spread[row]
+    stacked = jnp.concatenate(spread, 0)
+    upper = stacked.astype(LOW)
+    lower = (stacked - upper.astype(FULL)).astype(LOW)
+    stacked = jnp.concatenate([upper, lower, jnp.zeros((16 - 2 * rows, width), LOW)], 0)
+    stores = []
+
+    def store(source, target):
+        copy = pltpu.make_async_copy(source, target, out_sem.at[len(stores)])
+        copy.start()
+        stores.append(copy)
+
+    loads[1 + 2 * parts].wait()
+    for part in range(parts):
+        shift = dot_nt(stacked, wo_s[cut(part), :])
+        loads[2 + 2 * parts + part].wait()
+        for row in range(rows):
+            extra = shift[row : row + 1] + shift[rows + row : rows + row + 1]
+
+            def body(i, row=row, extra=extra, part=part):
+                at = rows_of(i + row * (seq // 128), 128)
+                inside = rows_of(i, 128)
+                present = lax.broadcasted_iota(jnp.int32, (128, 1), 0) + i * 128 < lengths[row]
+                dact = dact_s[at, cut(part)] + jnp.where(present, extra, 0.0)
+                slope_s[at, cut(part)] = (slope_s[at, cut(part)].astype(FULL) * dact).astype(LOW)
+
+            loop(seq // 128, body)
+        wi_grad_s[:, cut(part)] = dot_tn(n2_s[...], slope_s[:, cut(part)])
+        store(wi_grad_s.at[:, cut(part)], wi_grad.at[:, cut(part)])
+        store(slope_s.at[:, cut(part)], dinner.at[:, cut(part)])
+
+        def correct(i, part=part):
+            at = pl.ds(pl.multiple_of(part * width + i * 128, 128), 128)
+            more = wo_grad_s[at, :]
+            sums = mass_s[at, :]
+            for row in range(rows):
+                more = more + sums[:, row : row + 1] * spread[row]
+            wo_grad_s[at, :] = more
+
+        loop(width // 128, correct)
+        store(wo_grad_s.at[cut(part), :], wo_grad.at[cut(part), :])
+    for copy in stores:
+        copy.wait()
+
+
+def middle(sizes, cot, pooled, lengths, doc_groups, positives, act, slope, wo, n2):
+    count, width = cot.shape
+    hidden = wo.shape[0]
+    rows = lengths.shape[0]
+    names = bit_names(sizes)
+    parts = hidden // width
+    total = doc_groups.shape[0]
+    shape = jax.ShapeDtypeStruct
+    any_spec = pl.BlockSpec(memory_space=pl.ANY)
+    vmem_spec = pl.BlockSpec(memory_space=pltpu.VMEM)
+    smem_spec = pl.BlockSpec(memory_space=pltpu.SMEM)
+    narrow_s = pltpu.VMEM((count, width), LOW)
+    wide_s = pltpu.VMEM((count, hidden), LOW)
+    return pl.pallas_call(
+        functools.partial(middle_kernel, sizes, names),
+        out_shape=[
+            shape((hidden, width), FULL),
+            shape((width, hidden), FULL),
+            shape((count, hidden), LOW),
+            shape((rows, width), FULL),
+            shape((1, 1), FULL),
+        ],
+        in_specs=[any_spec, vmem_spec, smem_spec, vmem_spec, vmem_spec] + [any_spec] * 4,
+        out_specs=[any_spec] * 3 + [vmem_spec] * 2,
+        scratch_shapes=[
+            narrow_s,
+            wide_s,
+            wide_s,
+            pltpu.VMEM((hidden, width), LOW),
+            narrow_s,
+            pltpu.VMEM((count, hidden), FULL),
+            pltpu.VMEM((hidden, width), FULL),
+            pltpu.VMEM((width, hidden), FULL),
+            pltpu.VMEM((hidden, 128), FULL),
+            pltpu.VMEM((2, sizes["batch"], rows, width), FULL),
+            pltpu.VMEM((2, total, width), FULL),
+            pltpu.SemaphoreType.DMA((2 + 3 * parts,)),
+            pltpu.SemaphoreType.DMA((3 * parts,)),
+            pltpu.SemaphoreType.DMA((len(names),)),
+            pltpu.SemaphoreType.DMA((len(names),)),
+        ],
+        compiler_params=pltpu.CompilerParams(
+            collective_id=1, has_side_effects=True, vmem_limit_bytes=63 * 2**20
+        ),
+    )(cot, pooled, lengths, doc_groups.reshape(1, total), positives.reshape(total, 1), act, slope, wo, n2)
+
+
+def norm_back(values, gain, dy):
+    scale = lax.rsqrt(jnp.mean(values * values, -1, keepdims=True) + EPSILON)
+    along = values * scale
+    dscaled = gain * dy
+    mean = jnp.mean(along * dscaled, -1, keepdims=True)
+    return scale * (dscaled - along * mean), jnp.sum(along * dy, 0, keepdims=True)
+
+
+def backward_kernel(
+    cot, spread, lengths, dinner, wi, h1, ho, q, k, v, n1, tokens, lse, bias, wq, wk, wv, wm, gain1, gain2, table,
+    wq_grad, wk_grad, wv_grad, wm_grad, tokens_grad, small_out,
+    cot_s, h1_s, sum_s, ho_s, q_s, k_s, v_s, n1_s, x_s, dh_s, dq_s, dk_s, dv_s, wq_s, wk_s, wv_s, wm_s,
+    score_s, dprob_s, prob_s, dscore_s, near_s, stage_s, in_sem, out_sem, chunk_sem,
+):
+    count, width = cot_s.shape
+    rows = lengths.shape[0]
+    seq = count // rows
+    heads = table.shape[1]
+    size = width // heads
+    parts = wi.shape[1] // width
+    block = 256
+    loads = {}
+
+    def load(name, source, target):
+        copy = pltpu.make_async_copy(source, target, in_sem.at[len(loads)])
+        copy.start()
+        loads[name] = copy
+
+    def chunk(part):
+        turn = part % 2
+        return (
+            pltpu.make_async_copy(
+                dinner.at[:, pl.ds(part * width, width)], (dq_s, dk_s)[turn], chunk_sem.at[0, part]
+            ),
+            pltpu.make_async_copy(
+                wi.at[:, pl.ds(part * width, width)], (dv_s, dh_s)[turn].at[pl.ds(0, width), :], chunk_sem.at[1, part]
+            ),
+        )
+
+    for part in range(2):
+        for copy in chunk(part):
+            copy.start()
+    load("h1", h1, h1_s)
+    load("cot", cot, cot_s)
+    load("wm", wm, wm_s)
+    load("ho", ho, ho_s)
+    for name, source, target in (
+        ("q", q, q_s), ("k", k, k_s), ("v", v, v_s), ("n1", n1, n1_s),
+        ("wq", wq, wq_s), ("wk", wk, wk_s), ("wv", wv, wv_s), ("x", tokens, x_s),
+    ):
+        load(name, source, target)
+    stores = []
+
+    def store(source, target):
+        copy = pltpu.make_async_copy(source, target, out_sem.at[len(stores)])
+        copy.start()
+        stores.append(copy)
+
+    small_out[...] = jnp.zeros_like(small_out)
+    near_s[...] = jnp.zeros_like(near_s)
+
+    for part in range(parts):
+        for copy in chunk(part):
+            copy.wait()
+        left, right = (dq_s, dk_s)[part % 2], (dv_s, dh_s)[part % 2]
+
+        def add_dn2(i, part=part, left=left, right=right):
+            at = rows_of(i, block)
+            more = dot_nt(left[at, :], right[0:width, :])
+            sum_s[at, :] = more if part == 0 else sum_s[at, :] + more
+
+        loop(count // block, add_dn2)
+        if part + 2 < parts:
+            for copy in chunk(part + 2):
+                copy.start()
+    loads["h1"].wait()
+    loads["cot"].wait()
+    loads["wm"].wait()
+
+    def mix_back(i):
+        at = rows_of(i, block)
+        row = lax.div(i, jnp.int32(seq // block))
+        slot = lax.broadcasted_iota(jnp.int32, (block, 1), 0) + lax.rem(i, jnp.int32(seq // block)) * block
+        extra = spread[0:1, :]
+        for other in range(1, rows):
+            extra = jnp.where(row == other, spread[other : other + 1, :], extra)
+        dout = cot_s[at, :].astype(FULL) + jnp.where(slot < lengths[row], extra, 0.0)
+        dv, dgain = norm_back(h1_s[at, :], gain2[...], sum_s[at, :])
+        dh1 = dout + dv
+        h1_s[at, :] = dh1
+        small_out[1:2, :] = small_out[1:2, :] + dgain
+        da = dh1.astype(LOW)
+        cot_s[at, :] = da
+        dh_s[at, :] = dot_nt(da, wm_s[...]).astype(LOW)
+
+    loop(count // block, mix_back)
+    loads["ho"].wait()
+    stage_s[0] = dot_tn(ho_s[...], cot_s[...])
+    store(stage_s.at[0], wm_grad)
+
+    for name in ("q", "k", "v"):
+        loads[name].wait()
+    blocks = seq // 128
+    lanes = lax.broadcasted_iota(jnp.int32, (seq, 2 * size), 1)
+    keys = lax.broadcasted_iota(jnp.int32, (128, seq), 0)
+
+    def attend_back(step):
+        row = lax.div(step, jnp.int32(heads // 2))
+        pair = lax.rem(step, jnp.int32(heads // 2))
+        at = rows_of(row, seq)
+        here = rows_of(pair, 2 * size)
+        limit = lengths[row]
+        qp, kp, vp, dp = q_s[at, here], k_s[at, here], v_s[at, here], dh_s[at, here]
+        nothing = jnp.zeros_like(qp)
+        kt = kp.T
+        dq, dk, dv = [], [], []
+        for side in range(2):
+            chosen = (lanes >= size) == (side == 1)
+            score_s[side] = dot_nt(kp, jnp.where(chosen, qp, nothing))
+            dprob_s[side] = dot_nt(vp, jnp.where(chosen, dp, nothing))
+        for side in range(2):
+            head = pair * 2 + side
+            level = lse[row * heads + head]
+            delta = jnp.zeros((1, seq), FULL)
+            for jb in range(blocks):
+                here_rows = slice(jb * 128, (jb + 1) * 128)
+                strip = score_s[side, here_rows, :] + bias_strip(bias, table, head, jb, blocks)
+                strip = jnp.where(keys + jb * 128 < limit, strip, NEGATIVE)
+                prob = jnp.exp(strip - level)
+                prob_s[side, here_rows, :] = prob.astype(LOW)
+                score_s[side, here_rows, :] = prob
+                delta = delta + jnp.sum(prob * dprob_s[side, here_rows, :], 0, keepdims=True)
+            for jb in range(blocks):
+                here_rows = slice(jb * 128, (jb + 1) * 128)
+                prob = score_s[side, here_rows, :]
+                dscore = prob * (dprob_s[side, here_rows, :] - delta)
+                dscore_s[side, here_rows, :] = dscore.astype(LOW)
+                for ib in range(blocks):
+                    place = min(max(jb - ib, -2), 2) + 2
+                    near_s[head, place] = near_s[head, place] + dscore[:, ib * 128 : (ib + 1) * 128]
+            dk.append(dot_nn(dscore_s[side], qp))
+            dv.append(dot_nn(prob_s[side], dp))
+            dq.append(dot_nn(kt[side * size : (side + 1) * size, :], dscore_s[side]))
+        first = lanes < size
+        dk_s[at, here] = jnp.where(first, dk[0], dk[1]).astype(LOW)
+        dv_s[at, here] = jnp.where(first, dv[0], dv[1]).astype(LOW)
+        dq_s[at, here] = jnp.concatenate(dq, 0).T.astype(LOW)
+
+    loop(rows * (heads // 2), attend_back)
+
+    ids = [offset_buckets(shift) for shift, _ in NEAR]
+
+    def bucket_sums(head):
+        row_id = lax.broadcasted_iota(jnp.int32, (1, 128), 1)
+        found = jnp.zeros((1, 128), FULL)
+        for place, (shift, members) in enumerate(NEAR):
+            block_sum = near_s[head, place + 1]
+            for b in members:
+                part = jnp.sum(jnp.where(ids[place] == b, block_sum, 0.0), 0, keepdims=True)
+                found = found + jnp.where(row_id == b, jnp.sum(part, 1, keepdims=True), 0.0)
+        for place, b in ((0, 15), (4, 31)):
+            part = jnp.sum(near_s[head, place], 0, keepdims=True)
+            found = found + jnp.where(row_id == b, jnp.sum(part, 1, keepdims=True), 0.0)
+        near_s[head, 0, 0:1, :] = found
+
+    loop(heads, bucket_sums)
+    for head in range(heads):
+        small_out[8 + head : 9 + head, 0:128] = near_s[head, 0, 0:1, :]
+
+    loads["n1"].wait()
+    for turn, (d_s, target) in enumerate(((dq_s, wq_grad), (dk_s, wk_grad), (dv_s, wv_grad))):
+        spot = (turn + 1) % 2
+        if turn >= 1:
+            stores[turn - 1].wait()
+        stage_s[spot] = dot_tn(n1_s[...], d_s[...])
+        store(stage_s.at[spot], target)
+    for name in ("wq", "wk", "wv", "x"):
+        loads[name].wait()
+
+    def input_back(i):
+        at = rows_of(i, block)
+        dn1 = dot_nt(dq_s[at, :], wq_s[...]) + dot_nt(dk_s[at, :], wk_s[...]) + dot_nt(dv_s[at, :], wv_s[...])
+        dv, dgain = norm_back(x_s[at, :].astype(FULL), gain1[...], dn1)
+        small_out[0:1, :] = small_out[0:1, :] + dgain
+        cot_s[at, :] = (h1_s[at, :] + dv).astype(LOW)
+
+    loop(count // block, input_back)
+    store(cot_s, tokens_grad)
+    for copy in stores[2:]:
+        copy.wait()
+
+
+def backward(cot, spread, lengths, dinner, wi, h1, ho, q, k, v, n1, tokens, lse, bias, wq, wk, wv, wm, gain1, gain2, table):
+    count, width = cot.shape
+    rows = lengths.shape[0]
+    heads = table.shape[1]
+    seq = count // rows
+    shape = jax.ShapeDtypeStruct
+    any_spec = pl.BlockSpec(memory_space=pl.ANY)
+    vmem_spec = pl.BlockSpec(memory_space=pltpu.VMEM)
+    smem_spec = pl.BlockSpec(memory_space=pltpu.SMEM)
+    narrow_s = pltpu.VMEM((count, width), LOW)
+    full_s = pltpu.VMEM((count, width), FULL)
+    square = shape((width, width), FULL)
+    return pl.pallas_call(
+        backward_kernel,
+        out_shape=[square] * 4 + [shape((count, width), LOW), shape((24, width), FULL)],
+        in_specs=[any_spec, vmem_spec, smem_spec] + [any_spec] * 9 + [vmem_spec] * 2 + [any_spec] * 4 + [vmem_spec] * 2 + [smem_spec],
+        out_specs=[any_spec] * 5 + [vmem_spec],
+        scratch_shapes=[narrow_s, full_s, full_s]
+        + [narrow_s] * 10
+        + [pltpu.VMEM((width, width), LOW)] * 4
+        + [
+            pltpu.VMEM((2, seq, seq), FULL),
+            pltpu.VMEM((2, seq, seq), FULL),
+            pltpu.VMEM((2, seq, seq), LOW),
+            pltpu.VMEM((2, seq, seq), LOW),
+            pltpu.VMEM((heads, 5, 128, 128), FULL),
+            pltpu.VMEM((2, width, width), FULL),
+            pltpu.SemaphoreType.DMA((16,)),
+            pltpu.SemaphoreType.DMA((8,)),
+            pltpu.SemaphoreType.DMA((2, 8)),
+        ],
+        compiler_params=pltpu.CompilerParams(vmem_limit_bytes=62 * 2**20),
+    )(cot, spread, lengths, dinner, wi, h1, ho, q, k, v, n1, tokens, lse, bias, wq, wk, wv, wm,
+      gain1.reshape(1, width), gain2.reshape(1, width), table)
 
 
 def gradient_units(sizes):
@@ -338,151 +968,29 @@
     gain_ffn,
     rel_table,
 ):
-    rows_dev = tokens.shape[1]
-    seq_len = tokens.shape[2]
-    width = tokens.shape[3]
-    heads = rel_table.shape[1]
-    head_size = width // heads
-    count = rows_dev * seq_len
-    inputs = tokens.reshape(count, width).astype(jnp.float32)
-    row_lengths = lengths.reshape(rows_dev)
-    length_f = row_lengths.astype(jnp.float32)
-    present = jnp.arange(seq_len, dtype=jnp.int32)[None, :] < row_lengths[:, None]
-    onehot = bucket_onehot(seq_len, rel_table.shape[0])
-    bias = jnp.einsum("qkb,bh->hqk", onehot, rel_table, precision=HIGHEST)
-
-    def split_heads(matrix):
-        return matrix.reshape(rows_dev, seq_len, heads, head_size)
-
-    normed1, norm_back1 = jax.vjp(normalize, inputs, gain_attn)
-    normed1 = normed1.astype(jnp.bfloat16)
-    queries = matmul(normed1, w_query).astype(jnp.bfloat16)
-    keys_all = matmul(normed1, w_key).astype(jnp.bfloat16)
-    values_all = matmul(normed1, w_value).astype(jnp.bfloat16)
-
-    def score_of():
-        raw = (
-            jnp.einsum(
-                "rqhd,rkhd->rhqk",
-                split_heads(queries),
-                split_heads(keys_all),
-                preferred_element_type=jnp.float32,
-            )
-            + bias[None]
-        )
-        return jnp.where(present[:, None, None, :], raw, NEGATIVE)
-
-    scores = score_of()
-    highest = jnp.max(scores, -1, keepdims=True)
-    log_sums = highest + jnp.log(jnp.sum(jnp.exp(scores - highest), -1, keepdims=True))
-    weights_soft = jnp.exp(scores - log_sums)
-    heads_out = jnp.einsum(
-        "rhqk,rkhd->rqhd",
-        weights_soft.astype(jnp.bfloat16),
-        split_heads(values_all),
-        preferred_element_type=jnp.float32,
+    rows = tokens.shape[1]
+    count, width = rows * tokens.shape[2], tokens.shape[3]
+    buckets, heads = rel_table.shape
+    sizes = {axis: lax.axis_size(axis) for axis in ("tower", "batch")}
+    flat = tokens.reshape(count, width)
+    cot = cotangent.reshape(count, width)
+    own_lengths = lengths.reshape(rows)
+    q, k, v, ho, n1, n2, h1, act, slope, result, lse, bias, pooled = forward(
+        flat, own_lengths, w_query, w_key, w_value, w_mixed, w_inner, w_outer, gain_attn, gain_ffn, rel_table
     )
-    heads_out = heads_out.reshape(count, width).astype(jnp.bfloat16)
-    hidden1 = inputs + matmul(heads_out, w_mixed)
-    normed2, norm_back2 = jax.vjp(normalize, hidden1, gain_ffn)
-    normed2 = normed2.astype(jnp.bfloat16)
-    inner_pre = matmul(normed2, w_inner)
-    activated, smooth_back = jax.vjp(smooth, inner_pre)
-    activated = activated.astype(jnp.bfloat16)
-    output = hidden1 + matmul(activated, w_outer)
-    activations = output.astype(jnp.bfloat16).reshape(tokens.shape)
-    row_outputs = output.reshape(rows_dev, seq_len, width)
-    pooled = jnp.sum(jnp.where(present[:, :, None], row_outputs, 0.0), 1) / length_f[:, None]
-    gathered = lax.all_gather(pooled[None], ("tower", "batch"), axis=1, tiled=True)[0]
-    position = lax.axis_index(("tower", "batch"))
-
-    def summed_loss(every):
-        return contrast(every.reshape(2, -1, width), doc_groups, positives)
-
-    summed_ce, loss_back = jax.vjp(summed_loss, gathered)
-    grad_every = loss_back(jnp.ones((), jnp.float32))[0]
-    loss = summed_ce / doc_groups.shape[0]
-    grad_pooled = lax.dynamic_slice_in_dim(grad_every, position * rows_dev, rows_dev, 0)
-    spread_grad = jnp.where(
-        present[:, :, None], grad_pooled[:, None, :] / length_f[:, None, None], 0.0
+    wo_grad, wi_grad, dinner, spread, loss = middle(
+        sizes, cot, pooled, own_lengths, doc_groups, positives, act, slope, w_outer, n2
     )
-    grad_output = cotangent.reshape(count, width).astype(jnp.float32) + spread_grad.reshape(
-        count, width
+    wq_grad, wk_grad, wv_grad, wm_grad, tokens_grad, small = backward(
+        cot, spread, own_lengths, dinner, w_inner, h1, ho, q, k, v, n1, flat, lse, bias,
+        w_query, w_key, w_value, w_mixed, gain_attn, gain_ffn, rel_table,
     )
-    grad_out_b = grad_output.astype(jnp.bfloat16)
-    w_outer_grad = left_product(activated, grad_out_b)
-    grad_act = right_product(grad_out_b, w_outer)
-    grad_inner = smooth_back(grad_act)[0].astype(jnp.bfloat16)
-    w_inner_grad = left_product(normed2, grad_inner)
-    grad_normed2 = right_product(grad_inner, w_inner)
-    grad_hid_norm, gain_ffn_grad = norm_back2(grad_normed2)
-    grad_hidden1 = grad_output + grad_hid_norm
-    grad_attn_b = grad_hidden1.astype(jnp.bfloat16)
-    w_mixed_grad = left_product(heads_out, grad_attn_b)
-    grad_heads = right_product(grad_attn_b, w_mixed).astype(jnp.bfloat16)
-    again = jnp.exp(score_of() - log_sums)
-    grad_soft = jnp.einsum(
-        "rqhd,rkhd->rhqk",
-        split_heads(grad_heads),
-        split_heads(values_all),
-        preferred_element_type=jnp.float32,
-    )
-    row_delta = jnp.sum(again * grad_soft, -1, keepdims=True)
-    grad_scores = (again * (grad_soft - row_delta)).astype(jnp.bfloat16)
-    grad_query = (
-        jnp.einsum(
-            "rhqk,rkhd->rqhd",
-            grad_scores,
-            split_heads(keys_all),
-            preferred_element_type=jnp.float32,
-        )
-        .reshape(count, width)
-        .astype(jnp.bfloat16)
-    )
-    grad_key = (
-        jnp.einsum(
-            "rhqk,rqhd->rkhd", grad_scores, split_heads(queries), preferred_element_type=jnp.float32
-        )
-        .reshape(count, width)
-        .astype(jnp.bfloat16)
-    )
-    grad_value = (
-        jnp.einsum(
-            "rhqk,rqhd->rkhd",
-            again.astype(jnp.bfloat16),
-            split_heads(grad_heads),
-            preferred_element_type=jnp.float32,
-        )
-        .reshape(count, width)
-        .astype(jnp.bfloat16)
-    )
-    bias_grad = jnp.sum(grad_scores.astype(jnp.float32), 0)
-    table_grad = jnp.einsum("qkb,hqk->bh", onehot, bias_grad, precision=HIGHEST)
-    w_query_grad = left_product(normed1, grad_query)
-    w_key_grad = left_product(normed1, grad_key)
-    w_value_grad = left_product(normed1, grad_value)
-    grad_normed1 = (
-        right_product(grad_query, w_query)
-        + right_product(grad_key, w_key)
-        + right_product(grad_value, w_value)
-    )
-    grad_in_norm, gain_attn_grad = norm_back1(grad_normed1)
-    tokens_grad = (grad_hidden1 + grad_in_norm).astype(jnp.bfloat16).reshape(tokens.shape)
-    sizes = {axis: lax.axis_size(axis) for axis in ("tower", "batch")}
-    small = jnp.concatenate(
-        [
-            gain_attn_grad[None],
-            gain_ffn_grad[None],
-            jnp.pad(table_grad.reshape(1, -1), ((0, 0), (0, width - table_grad.size))),
-            jnp.zeros((5, width), jnp.float32),
-        ]
-    )
-    total = sum_gradients(
-        sizes,
-        [w_outer_grad, w_inner_grad, w_query_grad, w_key_grad, w_value_grad, w_mixed_grad],
-        small,
-    )
-    results = [
+    total = sum_gradients(sizes, [wo_grad, wi_grad, wq_grad, wk_grad, wv_grad, wm_grad], small)
+    return (
+        result.reshape(tokens.shape),
+        pooled[None],
+        loss[0, 0],
+        tokens_grad.reshape(tokens.shape),
         total[2],
         total[3],
         total[4],
@@ -491,22 +999,7 @@
         total[0],
         total[6][0],
         total[6][1],
-        total[6][2, : table_grad.size].reshape(table_grad.shape),
-    ]
-    return (
-        activations,
-        pooled[None],
-        loss,
-        tokens_grad,
-        results[0],
-        results[1],
-        results[2],
-        results[3],
-        results[4],
-        results[5],
-        results[6],
-        results[7],
-        results[8],
+        total[6][8 : 8 + heads, :buckets].T,
     )
 
 

time: 742 us -> 428 us (0.58)
  the two profiles are of different devices: /device:TPU:0 before, /device:TPU:13 now
where the time goes in v2:
time: 428 us; the launch traced here: 420 us
  Pallas kernels  389 us (91%)
  local copies, waits for them, and re-layouts  27.7 us (6%)
    pallas_call x1, Pallas kernels, sum_gradients(): pl.pallas_call(functools.partial(sum_kernel, sizes, units, names), out_sh...  242 us
    pallas_call x1, Pallas kernels, backward(): pl.pallas_call(backward_kernel, out_shape=[square] * 4 + [shape((count, w...  63 us
    pallas_call x1, Pallas kernels, forward(): pl.pallas_call(forward_kernel, out_shape=[low, low, low, low, low, low, s...  47.2 us
    pallas_call x1, Pallas kernels, middle(): pl.pallas_call(functools.partial(middle_kernel, sizes, names), out_shape=...  37 us
    unnamed x21, local copies, waits for them, and re-layouts  20.9 us

profile of v2, /device:TPU:13, one launch (start us, length us, event | category | flops | bytes accessed | tf_op | source)
XLA Modules:
  0.0 419.8 jit_solution(546712912752016367)
XLA Ops:
  0.6 1.3 reshape.57.gain1
  1.9 1.3 reshape.58.gain2
  3.2 1.4 copy.27.table
  4.5 1.3 copy.28.positives
  5.9 47.2 %shard_map.237 = (bf16[1024,768]{1,0:T(8,128)(2,1)}, bf16[1024,768]{1,0:T(8,128)(2,1)}, bf16[1024,768]{1,0:T(8,128)(2,1)}, bf16[1024,768]{1,0:T(8,128)(2,1)}, bf...) custom-call(bf16[1024,768]{1,0:T(8,128)(2,1)} %bitcast.13, ...), custom_call_target="tpu_custom_call" | custom-call | tf_op jit(solution)/shard_map/pallas_call | solution.py:401
  53.1 37.0 %shard_map.238 = (f32[3072,768]{1,0:T(8,128)}, f32[768,3072]{1,0:T(8,128)}, bf16[1024,3072]{1,0:T(8,128)(2,1)}, f32[2,768]{1,0:T(2,128)}, f32[1,1]{1,0:T(1,128)}) custom-call(bf16[1024,768]{1,0:T(8,128)(2,1)} %bitcast.15, f32[2,768]{1,0:T(2,128)} %get-tuple-element.45.pooled, s32[2]{0:T(128)} %bitcast.19, s32[1,32]{1,0:T(1,128)} %bitcast.21, ...), custom_call_target="tpu_custom_call" | custom-call | tf_op jit(solution)/shard_map/pallas_call | solution.py:614
  90.1 63.0 %shard_map.239 = (f32[768,768]{1,0:T(8,128)}, f32[768,768]{1,0:T(8,128)}, f32[768,768]{1,0:T(8,128)}, f32[768,768]{1,0:T(8,128)}, bf16[1024,768]{1,0:T(8,128)(2,1)}, /*index=5*/f32[24,768]{1,0:T(8,128)}) custom-call(bf16[1024,768]{1,0:T(8,128)(2,1)} %bitcast.16, f32[2,768]{1,0:T(2,128)} %get-tuple-element.50.spread, s32[2]{0:T(128)} %bitcast.20, ...), custom_call_target="tpu_custom_call" | custom-call | tf_op jit(solution)/shard_map/pallas_call | solution.py:852
  153.2 241.9 %shard_map.240 = (f32[3072,768]{1,0:T(8,128)}, f32[768,3072]{1,0:T(8,128)}, f32[768,768]{1,0:T(8,128)}, f32[768,768]{1,0:T(8,128)}, f32[768,768]{1,0:T(8,128)}, /*index=5*/f32[768,768]{1,0:T(8,128)}, f32[24,768]{1,0:T(8,128)}) custom-call(f32[3072,768]{1,0:T(8,128)} %get-tuple-element.61.refs_0_, f32[768,3072]{1,0:T(8,128)} %get-tuple-element.62.refs_1_, ...), custom_call_target="tpu_custom_call" | custom-call | tf_op jit(solution)/shard_map/pallas_call | solution.py:932
  395.0 0.0 copy-start.3
  395.1 1.4 slice_bitcast_fusion
  396.5 1.4 slice_reduce_fusion
  398.6 0.0 copy-start.2
  398.6 0.0 copy-start.1
  398.6 3.4 copy.38
  402.0 0.0 copy-done.3
  402.0 0.0 copy-start
  402.0 1.4 copy.39
  403.4 0.0 copy-done.2
  403.4 1.4 copy.40
  404.8 0.0 copy-done.1
  404.8 0.0 slice-start
  404.8 1.4 copy.41
  406.2 2.0 copy-done
  408.3 0.0 slice-start.1
  408.3 0.0 slice-start.2
  408.3 4.8 %copy.42 = f32[768,3072]{1,0:T(8,128)} copy(f32[768,3072]{1,0:T(8,128)S(1)} %copy-done) | data formatting | bytes 18874368
  413.0 0.0 slice-done
  413.0 1.2 slice-done.1
  414.2 0.2 slice-done.2
  414.4 3.7 copy.43
  (1 shorter events, 0.0 us)
Async XLA Ops:
  395.0 7.0 %copy-start.3 = (f32[768,768]{1,0:T(8,128)S(1)}, f32[768,768]{1,0:T(8,128)}, u32[]{:S(2)}) copy-start(f32[768,768]{1,0:T(8,128)} %get-tuple-element.95) | copy-start | bytes 7077892
  398.6 4.8 %copy-start.2 = (f32[768,768]{1,0:T(8,128)S(1)}, f32[768,768]{1,0:T(8,128)}, u32[]{:S(2)}) copy-start(f32[768,768]{1,0:T(8,128)} %get-tuple-element.96) | copy-start | bytes 7077892
  398.6 6.2 %copy-start.1 = (f32[768,768]{1,0:T(8,128)S(1)}, f32[768,768]{1,0:T(8,128)}, u32[]{:S(2)}) copy-start(f32[768,768]{1,0:T(8,128)} %get-tuple-element.97) | copy-start | bytes 7077892
  402.0 6.2 %copy-start = (f32[768,3072]{1,0:T(8,128)S(1)}, f32[768,3072]{1,0:T(8,128)}, u32[]{:S(2)}) copy-start(f32[768,3072]{1,0:T(8,128)} %get-tuple-element.98) | copy-start | bytes 28311556
  404.8 8.2 %slice-start = ((s8[9437184]{0:T(1024)(128)(4,1)}), s8[4194304]{0:T(1024)(128)(4,1)S(1)}, s32[]{:S(2)}) async-start(s8[9437184]{0:T(1024)(128)(4,1)} %bitcast.11), calls=%async_computation | async-start | bytes 8388608
  408.3 6.0 %slice-start.1 = ((s8[9437184]{0:T(1024)(128)(4,1)}), s8[4194304]{0:T(1024)(128)(4,1)S(1)}, s32[]{:S(2)}) async-start(s8[9437184]{0:T(1024)(128)(4,1)} %bitcast.11), calls=%async_computation.1 | async-start | bytes 8388608
  408.3 6.2 %slice-start.2 = ((s8[9437184]{0:T(1024)(128)(4,1)}), s8[1048576]{0:T(1024)(128)(4,1)S(1)}, s32[]{:S(2)}) async-start(s8[9437184]{0:T(1024)(128)(4,1)} %bitcast.11), calls=%async_computation.2 | async-start | bytes 2097152

commit v3 on v0

v3 whole, which is shorter than its diff:
```python
import functools

import jax
import jax.numpy as jnp
from jax import lax
from jax.experimental import pallas as pl
from jax.experimental.pallas import tpu as pltpu
from jax.sharding import PartitionSpec as P

EPSILON = 1e-06
SCALE = 50.0
NEGATIVE = -1000000000.0
THRESHOLDS = (12, 16, 23, 32, 46, 64, 91)
HIGHEST = lax.Precision.HIGHEST


MESH = pl.DeviceIdType.MESH
LINK = 45.7e3
CORE = 500e3
FLIGHT = 1.8
CLASSES = "ABCD"
PATTERN = "ABCABD"
UNIT_ROWS = 256


def bit_names(sizes):
    names = []
    for axis in ("tower", "batch"):
        mask = 1
        while mask < sizes[axis]:
            names.append((axis, mask))
            mask *= 2
    return names


def set_counts(sizes):
    return {"A": 5, "B": 5, "C": 3, "D": 3} if sizes["batch"] <= 16 else {"A": 3, "B": 3, "C": 2, "D": 2}


def bit_groups(sizes):
    names = bit_names(sizes)
    core = [(k,) for k, name in enumerate(names) if name[0] == "tower"]
    rest = [k for k, name in enumerate(names) if name[0] == "batch"]
    x, y, low, high = rest[:4]
    more = [(k,) for k in rest[4:]]
    firsts = {
        "A": [(x,), (y,), (low, high)],
        "B": [(y,), (x,), (low, high)],
        "C": [(low,), (x,), (y,), (high,)],
        "D": [(low,), (y,), (x,), (high,)],
    }
    return {name: core + groups + more for name, groups in firsts.items()}


def flips_of(group):
    return [tuple(k for i, k in enumerate(group) if choice >> i & 1) for choice in range(1, 2 ** len(group))]


def gather_groups(sizes):
    rest = [k for k, name in enumerate(bit_names(sizes)) if name[0] == "batch"]
    groups = [tuple(rest[i : i + 2]) for i in range(0, len(rest), 2)]
    return groups + [(k,) for k, name in enumerate(bit_names(sizes)) if name[0] == "tower"]


class Place:
    def __init__(self, sizes):
        self.names = bit_names(sizes)
        self.at = {axis: lax.axis_index(axis) for axis in ("tower", "batch")}
        self.bits = [
            lax.rem(lax.div(self.at[axis], jnp.int32(mask)), jnp.int32(2)) for axis, mask in self.names
        ]

    def partner(self, flips):
        other = dict(self.at)
        for k in flips:
            axis, mask = self.names[k]
            other[axis] = other[axis] + mask * (1 - 2 * self.bits[k])
        return (other["tower"], other["batch"])

    def code(self, group, flips=()):
        total = jnp.int32(0)
        for k in group:
            total = total * 2 + (1 - self.bits[k] if k in flips else self.bits[k])
        return total


class Unit:
    def __init__(self, matrix, row, col, cols, kind, groups, item):
        self.matrix, self.row, self.col, self.cols, self.kind, self.item = matrix, row, col, cols, kind, item
        self.steps = []
        size, back, land = UNIT_ROWS, [], 0
        for group in groups:
            ways = 2 ** len(group)
            if size % (8 * ways) == 0:
                size //= ways
                self.steps.append(("cut", group, size, land))
                back.append(("join", group, size, 0))
                land += size * (ways - 1)
            else:
                for k in group:
                    self.steps.append(("whole", (k,), size, land))
                    land += size
        self.land = land
        self.returns = len(self.steps)
        self.steps += back[::-1]

    def place_at(self, place):
        start, stack = jnp.int32(self.row), []
        self.starts = []
        for kind, group, size, _ in self.steps:
            self.starts.append(start)
            if kind == "cut":
                stack.append(start)
                start = start + place.code(group) * size
            elif kind == "join":
                start = stack.pop()


def link_use(names, group, size):
    link = size / LINK
    masks = [names[k] for k in group]
    if masks[0][0] == "tower":
        return {"core": size / CORE}
    if masks == [("batch", 4)]:
        return {"end": link}
    if masks == [("batch", 8)]:
        return {"end": link, "middle": 2 * link}
    if masks == [("batch", 4), ("batch", 8)]:
        return {"end": 3 * link, "middle": 4 * link}
    return {mask: link * (2 ** len(group) - 1) for mask in masks}


def plan(units, names, counts, items, depth=4.0):
    free, clock, flight, pending = {}, 0.0, [], []
    idle = {kind: [(kind, i) for i in range(counts[kind])] for kind in CLASSES}
    done, order = 0, [[] for _ in items]
    left = list(range(len(units)))

    def use(u, s):
        _, group, size, _ = units[u].steps[s]
        return link_use(names, group, size * units[u].cols * 4)

    def pump():
        nonlocal clock
        for u in left:
            if units[u].item < done and (u, 0) not in pending:
                pending.append((u, 0))
        pending.sort()
        for u, s in list(pending):
            unit = units[u]
            if s == 0 and not idle[unit.kind]:
                continue
            if any(free.get(link, 0.0) - clock > depth for link in use(u, 1 if s == 0 else s)):
                continue
            pending.remove((u, s))
            if s == 0:
                left.remove(u)
                unit.set = idle[unit.kind].pop(0)
            clock += 0.08
            end = clock
            for link, time in use(u, s).items():
                free[link] = max(clock, free.get(link, 0.0)) + time
                end = max(end, free[link])
            flight.append((end + FLIGHT, u, s))
            order[done - 1].append(("go", u, s))

    while left or flight or pending or done < len(items):
        flight.sort()
        if flight and (flight[0][0] <= clock or done == len(items)):
            if flight[0][0] > clock and pending:
                clock = min(flight[0][0], clock + 0.5)
                pump()
                continue
            arrived, u, s = flight.pop(0)
            clock = max(clock, arrived) + 0.15
            kind, group, size, _ = units[u].steps[s]
            if kind != "join":
                clock += size * units[u].cols * 4 * (2 ** len(group) - 1) / 4e6
            order[done - 1].append(("serve", u, s))
            if s + 1 < len(units[u].steps):
                pending.append((u, s + 1))
            else:
                idle[units[u].kind].append(units[u].set)
            pump()
        elif done < len(items):
            clock += items[done]
            done += 1
            pump()
        else:
            clock += 0.5
            pump()
    return order, clock


class Exchange:
    def __init__(self, units, place, counts, grads, kept, land, outs, sems):
        self.units, self.place, self.grads, self.kept, self.land, self.outs = units, place, grads, kept, land, outs
        self.send_sem, self.recv_sem, self.load_sem, self.store_sem = sems
        self.sets = {name: i for i, name in enumerate((kind, i) for kind in CLASSES for i in range(counts[kind]))}
        for unit in units:
            unit.place_at(place)

    def part(self, refs, unit, start, rows):
        return refs[unit.matrix].at[pl.ds(pl.multiple_of(start, 8), rows), pl.ds(unit.col, unit.cols)]

    def own(self, unit, start, rows):
        ref = self.kept.at[self.sets[unit.set]]
        return ref.at[pl.ds(pl.multiple_of(start - unit.starts[1], 8), rows), :]

    def load(self, unit):
        spot = self.sets[unit.set]
        return pltpu.make_async_copy(
            self.part(self.grads, unit, unit.starts[1], unit.steps[0][2]), self.kept.at[spot], self.load_sem.at[spot]
        )

    def store(self, unit):
        spot, s = self.sets[unit.set], unit.returns
        start, rows = unit.starts[s], unit.steps[s][2]
        return pltpu.make_async_copy(
            self.own(unit, start, rows), self.part(self.outs, unit, start, rows), self.store_sem.at[spot]
        )

    def copies(self, unit, s):
        kind, group, size, land = unit.steps[s]
        spot, found = self.sets[unit.set], []
        for turn, flips in enumerate(flips_of(group)):
            start = unit.starts[s]
            if kind == "cut":
                start = start + self.place.code(group, flips) * size
            if s == 0:
                source = self.part(self.grads, unit, start, size)
            elif s <= unit.returns:
                source = self.own(unit, start, size)
            else:
                source = self.part(self.outs, unit, start, size)
            if kind == "join":
                target = self.part(self.outs, unit, start, size)
            else:
                target = self.land.at[spot, pl.ds(land + turn * size, size), :]
            found.append(
                pltpu.make_async_remote_copy(
                    src_ref=source,
                    dst_ref=target,
                    send_sem=self.send_sem.at[spot, s, turn],
                    recv_sem=self.recv_sem.at[spot, s, turn],
                    device_id=self.place.partner(flips),
                    device_id_type=MESH,
                )
            )
        return found

    def go(self, u, s):
        unit = self.units[u]
        if s == 0:
            self.load(unit).start()
        for copy in self.copies(unit, s):
            copy.start()

    def serve(self, u, s):
        unit = self.units[u]
        if s == 0:
            self.load(unit).wait()
        for copy in self.copies(unit, s):
            copy.wait()
        kind, group, size, land = unit.steps[s]
        if kind != "join":
            spot = self.sets[unit.set]
            start = unit.starts[s]
            if kind == "cut":
                start = start + self.place.code(group) * size
            kept = self.own(unit, start, size)
            total = kept[...]
            for turn in range(2 ** len(group) - 1):
                total = total + self.land[spot, land + turn * size : land + (turn + 1) * size, :]
            kept[...] = total
        if s + 1 == unit.returns:
            self.store(unit).start()
        if s == unit.returns:
            self.store(unit).wait()


LOW = jnp.bfloat16
FULL = jnp.float32


def dot_nn(left, right):
    return lax.dot_general(left, right, (((1,), (0,)), ((), ())), preferred_element_type=FULL)


def dot_nt(left, right):
    return lax.dot_general(left, right, (((1,), (1,)), ((), ())), preferred_element_type=FULL)


def dot_tn(left, right):
    return lax.dot_general(left, right, (((0,), (0,)), ((), ())), preferred_element_type=FULL)


def loop(count, body):
    def step(i, carry):
        body(i)
        return carry

    lax.fori_loop(0, count, step, 0)


def rows_of(i, size):
    return pl.ds(pl.multiple_of(i * size, size), size)


def offset_buckets(shift):
    keys = lax.broadcasted_iota(jnp.int32, (128, 128), 0)
    queries = lax.broadcasted_iota(jnp.int32, (128, 128), 1)
    offsets = keys - queries + 128 * shift
    distance = jnp.abs(offsets)
    distant = jnp.full((128, 128), 8, jnp.int32)
    for limit in THRESHOLDS:
        distant = distant + jnp.where(distance >= limit, 1, 0)
    buckets = jnp.where(distance < 8, distance, distant)
    return buckets + jnp.where(offsets > 0, 16, 0)


NEAR = ((-1, range(1, 16)), (0, range(32)), (1, range(17, 32)))


def fill_bias(bias, table, head, count):
    ids = [offset_buckets(shift) for shift, _ in NEAR]
    for side in range(count):
        for spot, (shift, members) in enumerate(NEAR):
            block = jnp.zeros((128, 128), FULL)
            for b in members:
                block = jnp.where(ids[spot] == b, table[head + side, b], block)
            bias[side, spot] = block


def bias_strip(bias, side, table, head, jb, blocks):
    parts = []
    for ib in range(blocks):
        shift = jb - ib
        if abs(shift) <= 1:
            parts.append(bias[side, shift + 1])
        else:
            parts.append(jnp.full((128, 128), table[head, 31 if shift > 0 else 15], FULL))
    return jnp.concatenate(parts, axis=1)


def forward_kernel(
    tokens, lengths, wq, wk, wv, wm, wi, wo, gain1, gain2, table,
    q_out, k_out, v_out, ho_out, n1_out, n2_out, h1_out, act_out, slope_out, result_out, lse_out, pooled_out,
    x_s, wq_s, wk_s, wv_s, wm_s, wi_s, wo_s, q_s, k_s, v_s, ho_s, n1_s, n2_s, h1_s, act_s, slope_s, result_s, total_s,
    score_s, prob_s, bias_s, in_sem, out_sem,
):
    count, width = tokens.shape
    rows, seq = lengths.shape[0], tokens.shape[0] // lengths.shape[0]
    heads = table.shape[0]
    size = width // heads
    hidden = wi.shape[1]
    parts = hidden // width
    loads = [
        pltpu.make_async_copy(source, target, in_sem.at[i])
        for i, (source, target) in enumerate(
            [(tokens, x_s), (wq, wq_s), (wk, wk_s), (wv, wv_s), (wm, wm_s), (wi, wi_s), (wo, wo_s)]
        )
    ]
    for load in loads:
        load.start()
    stores = []

    def store(source, target):
        copy = pltpu.make_async_copy(source, target, out_sem.at[len(stores)])
        copy.start()
        stores.append(copy)

    block = 256
    loads[0].wait()

    def norm1(i):
        at = rows_of(i, block)
        x = x_s[at, :].astype(FULL)
        scale = lax.rsqrt(jnp.mean(x * x, -1, keepdims=True) + EPSILON)
        n1_s[at, :] = (x * scale * gain1[...]).astype(LOW)

    loop(count // block, norm1)
    store(n1_s, n1_out)
    for i, (w_s, p_s, p_out) in enumerate(((wq_s, q_s, q_out), (wk_s, k_s, k_out), (wv_s, v_s, v_out))):
        loads[1 + i].wait()

        def project(m, w_s=w_s, p_s=p_s):
            at = rows_of(m, 512)
            p_s[at, :] = dot_nn(n1_s[at, :], w_s[...]).astype(LOW)

        loop(count // 512, project)
        store(p_s, p_out)
    blocks = seq // 128
    lanes = lax.broadcasted_iota(jnp.int32, (seq, 2 * size), 1)
    keys = lax.broadcasted_iota(jnp.int32, (128, seq), 0)

    def attend(step):
        pair = lax.div(step, jnp.int32(rows))
        row = lax.rem(step, jnp.int32(rows))
        at = rows_of(row, seq)
        here = rows_of(pair, 2 * size)
        limit = lengths[row]

        @pl.when(row == 0)
        def _():
            fill_bias(bias_s, table, pair * 2, 2)

        q, k = q_s[at, here], k_s[at, here]
        vt = v_s[at, here].T
        found = []
        for side in range(2):
            head = pair * 2 + side
            chosen = jnp.where((lanes >= size) == (side == 1), q, jnp.zeros_like(q))
            score_s[side] = dot_nt(k, chosen)
        for side in range(2):
            head = pair * 2 + side
            top = jnp.full((1, seq), NEGATIVE, FULL)
            for jb in range(blocks):
                strip = score_s[side, jb * 128 : (jb + 1) * 128, :] + bias_strip(bias_s, side, table, head, jb, blocks)
                strip = jnp.where(keys + jb * 128 < limit, strip, NEGATIVE)
                score_s[side, jb * 128 : (jb + 1) * 128, :] = strip
                top = jnp.maximum(top, jnp.max(strip, 0, keepdims=True))
            mass = jnp.zeros((1, seq), FULL)
            for jb in range(blocks):
                strip = jnp.exp(score_s[side, jb * 128 : (jb + 1) * 128, :] - top)
                mass = mass + jnp.sum(strip, 0, keepdims=True)
                prob_s[side, jb * 128 : (jb + 1) * 128, :] = strip.astype(LOW)
            lse_out[row * heads + head] = top + jnp.log(mass)
            found.append(dot_nn(vt[side * size : (side + 1) * size, :], prob_s[side]) / mass)
        ho_s[at, here] = jnp.concatenate(found, 0).T.astype(LOW)

    loop(rows * (heads // 2), attend)
    store(ho_s, ho_out)
    loads[4].wait()

    def mix(i):
        at = rows_of(i, block)
        h1 = x_s[at, :].astype(FULL) + dot_nn(ho_s[at, :], wm_s[...])
        h1_s[at, :] = h1
        scale = lax.rsqrt(jnp.mean(h1 * h1, -1, keepdims=True) + EPSILON)
        n2_s[at, :] = (h1 * scale * gain2[...]).astype(LOW)

    loop(count // block, mix)
    store(h1_s, h1_out)
    store(n2_s, n2_out)
    loads[5].wait()
    loads[6].wait()

    for part in range(parts):
        columns = pl.ds(part * width, width)

        def feed(i, part=part, columns=columns):
            at = rows_of(i, block)
            inner = dot_nn(n2_s[at, :], wi_s[:, columns])
            share = 0.5 + 0.5 * lax.erf(inner * 0.7071067811865476)
            act = (inner * share).astype(LOW)
            act_s[at, columns] = act
            slope = share + inner * (jnp.exp(inner * inner * -0.5) * 0.3989422804014327)
            slope_s[at, columns] = slope.astype(LOW)
            more = dot_nn(act, wo_s[columns, :])
            if part == 0:
                total_s[at, :] = h1_s[at, :] + more
            elif part < parts - 1:
                total_s[at, :] = total_s[at, :] + more
            else:
                output = total_s[at, :] + more
                total_s[at, :] = output
                result_s[at, :] = output.astype(LOW)

        loop(count // block, feed)
        store(act_s.at[:, columns], act_out.at[:, columns])
        store(slope_s.at[:, columns], slope_out.at[:, columns])
    store(result_s, result_out)
    slots = lax.broadcasted_iota(jnp.int32, (seq, 1), 0)
    for row in range(rows):
        kept = jnp.where(slots < lengths[row], total_s[row * seq : (row + 1) * seq, :], 0.0)
        pooled_out[row : row + 1, :] = jnp.sum(kept, 0, keepdims=True) / lengths[row].astype(FULL)
    for copy in stores:
        copy.wait()


def forward(tokens, lengths, wq, wk, wv, wm, wi, wo, gain1, gain2, table):
    count, width = tokens.shape
    hidden = wi.shape[1]
    rows = lengths.shape[0]
    heads = table.shape[0]
    seq = count // rows
    shape = jax.ShapeDtypeStruct
    any_spec = pl.BlockSpec(memory_space=pl.ANY)
    vmem_spec = pl.BlockSpec(memory_space=pltpu.VMEM)
    smem_spec = pl.BlockSpec(memory_space=pltpu.SMEM)
    low = shape((count, width), LOW)
    wide = shape((count, hidden), LOW)
    weights = [pltpu.VMEM(w.shape, LOW) for w in (wq, wk, wv, wm, wi, wo)]
    narrow_s = pltpu.VMEM((count, width), LOW)
    full_s = pltpu.VMEM((count, width), FULL)
    wide_s = pltpu.VMEM((count, hidden), LOW)
    return pl.pallas_call(
        forward_kernel,
        out_shape=[low, low, low, low, low, low, shape((count, width), FULL), wide, wide, low]
        + [shape((rows * heads, 1, seq), FULL), shape((rows, width), FULL)],
        in_specs=[any_spec, smem_spec] + [any_spec] * 6 + [vmem_spec] * 2 + [smem_spec],
        out_specs=[any_spec] * 10 + [vmem_spec] * 2,
        scratch_shapes=[narrow_s]
        + weights
        + [narrow_s] * 6
        + [full_s, wide_s, wide_s, narrow_s, full_s]
        + [
            pltpu.VMEM((2, seq, seq), FULL),
            pltpu.VMEM((2, seq, seq), LOW),
            pltpu.VMEM((2, 3, 128, 128), FULL),
            pltpu.SemaphoreType.DMA((7,)),
            pltpu.SemaphoreType.DMA((24,)),
        ],
        compiler_params=pltpu.CompilerParams(vmem_limit_bytes=62 * 2**20),
    )(tokens, lengths, wq, wk, wv, wm, wi, wo, gain1.reshape(1, width), gain2.reshape(1, width), table)


def norm_back(values, gain, dy):
    scale = lax.rsqrt(jnp.mean(values * values, -1, keepdims=True) + EPSILON)
    along = values * scale
    dscaled = gain * dy
    mean = jnp.mean(along * dscaled, -1, keepdims=True)
    return scale * (dscaled - along * mean), jnp.sum(along * dy, 0, keepdims=True)


def contrast(queries, documents, doc_groups, positives):
    count = doc_groups.shape[1]
    precise = functools.partial(lax.dot_general, precision=HIGHEST, preferred_element_type=FULL)
    rates = [lax.rsqrt(jnp.sum(p * p, -1, keepdims=True) + EPSILON) for p in (queries, documents)]
    unit = [p * rate for p, rate in zip((queries, documents), rates)]
    scores = SCALE * precise(unit[0], unit[1], (((1,), (1,)), ((), ())))
    indices = lax.broadcasted_iota(jnp.int32, (count, count), 0)
    chosen = jnp.where(positives == indices, 1.0, 0.0).T
    query_groups = jnp.sum(chosen * doc_groups.astype(FULL), 1, keepdims=True)
    masked = jnp.where(query_groups == doc_groups.astype(FULL), scores, NEGATIVE)
    highest = jnp.max(masked, 1, keepdims=True)
    weights = jnp.exp(masked - highest)
    mass = jnp.sum(weights, 1, keepdims=True)
    matched = jnp.sum(jnp.where(chosen > 0.5, scores, 0.0), 1, keepdims=True)
    loss = jnp.sum(highest + jnp.log(mass) - matched, 0, keepdims=True) / count
    dscore = weights / mass - chosen
    dunit = (
        SCALE * precise(dscore, unit[1], (((1,), (0,)), ((), ()))),
        SCALE * precise(dscore, unit[0], (((0,), (0,)), ((), ()))),
    )
    dpooled = [rate * (d - u * jnp.sum(u * d, -1, keepdims=True)) for rate, d, u in zip(rates, dunit, unit)]
    return loss, dpooled


def make_units(sizes, hidden, width):
    groups = bit_groups(sizes)
    parts, thirds = hidden // width, width // UNIT_ROWS
    items = [("gather", 12.0), ("loss", 3.0)]
    blocks = []
    for part in range(parts):
        items.append(("outer", 1.9))
        blocks += [(0, part * width + i * UNIT_ROWS, 0, len(items)) for i in range(thirds)]
    for part in range(parts):
        items.append(("inner", 6.2))
        blocks += [(1, i * UNIT_ROWS, part * width, len(items)) for i in range(thirds)]
    items += [("mix", 3.5), ("mixed", 1.8)]
    blocks += [(5, i * UNIT_ROWS, 0, len(items)) for i in range(thirds)]
    items += [("attend", 2.4)] * 24
    for matrix in range(2, 5):
        items.append(("projection", 1.8))
        blocks += [(matrix, i * UNIT_ROWS, 0, len(items)) for i in range(thirds)]
    items.append(("input", 6.0))
    units = []
    for i, (matrix, row, col, item) in enumerate(blocks):
        kind = PATTERN[i % len(PATTERN)]
        units.append(Unit(matrix, row, col, width, kind, groups[kind], item))
    return units, items


def backward_kernel(
    sizes, units, order, counts,
    cot, pooled, lengths, doc_groups, positives, act, slope, wo, wi, n2, h1, ho, q, k, v, n1, tokens, lse,
    wq, wk, wv, wm, gain1, gain2, table,
    *refs,
):
    grads, outs = refs[:6], refs[6:12]
    tokens_grad, small_out, loss_out = refs[12:15]
    (
        narrow, square, staged, full, bias_s, near_s, sums_s, every_s, small_land, kept, land,
        in_sem, chunk_sem, stage_sem, last_sem, hop_send, hop_recv, small_send, small_recv,
        send_sem, recv_sem, load_sem, store_sem,
    ) = refs[15:]
    count, width = narrow.shape[1:]
    rows = lengths.shape[0]
    seq = count // rows
    heads = table.shape[0]
    size = width // heads
    parts = wo.shape[0] // width
    block = 256
    place = Place(sizes)
    names = place.names
    tower, batch = place.at["tower"], place.at["batch"]
    exchange = Exchange(units, place, counts, grads, kept, land, outs, (send_sem, recv_sem, load_sem, store_sem))
    cot_s, n2_s, dout_s = narrow.at[8], narrow.at[9], narrow.at[10]
    act_s = [narrow.at[part] for part in range(parts)]
    slope_s = [narrow.at[parts + part] for part in range(parts)]
    h1_s, sum_s = full.at[0], full.at[1]
    loads = {}

    def load(name, source, target):
        copy = pltpu.make_async_copy(source, target, in_sem.at[len(loads)])
        copy.start()
        loads[name] = copy

    def cut(part):
        return pl.ds(part * width, width)

    load("cot", cot, cot_s)
    for part in range(parts):
        load("act%d" % part, act.at[:, cut(part)], act_s[part])
    for part in range(parts):
        load("wo%d" % part, wo.at[cut(part), :], square.at[part])
    load("n2", n2, n2_s)
    for part in range(parts):
        load("slope%d" % part, slope.at[:, cut(part)], slope_s[part])

    def wi_chunk(part):
        return pltpu.make_async_copy(wi.at[:, cut(part)], square.at[parts + part % 2], chunk_sem.at[part])

    for part in range(2):
        wi_chunk(part).start()
    load("h1", h1, h1_s)

    item = 0
    stage_of = {}

    def act_on(actions):
        for action, u, s in actions:
            if action == "go":
                if s == 0:
                    exchange_ready(u)
                exchange.go(u, s)
            else:
                exchange.serve(u, s)

    def exchange_ready(u):
        unit = units[u]
        key = (unit.matrix, unit.row // width if unit.matrix == 0 else unit.col // width)
        if key in stage_of:
            stage_of.pop(key).wait()

    def between():
        nonlocal item
        act_on(order[item])
        item += 1

    staged_count = 0
    staged_last = {}

    def stage(value, matrix, part, target):
        nonlocal staged_count
        spot = staged_count % 3
        if spot in staged_last and staged_last[spot] in stage_of:
            stage_of.pop(staged_last[spot]).wait()
        staged[spot] = value
        copy = pltpu.make_async_copy(staged.at[spot], target, stage_sem.at[staged_count])
        copy.start()
        stage_of[(matrix, part)] = copy
        staged_last[spot] = (matrix, part)
        staged_count += 1

    hops = gather_groups(sizes)
    every_s[tower, batch] = pooled[...]
    deltas = set()
    for group in list(bit_groups(sizes).values()) + [hops]:
        for bits in group:
            deltas.update(flips_of(bits))
    barrier = pltpu.get_barrier_semaphore()
    for flips in sorted(deltas):
        pl.semaphore_signal(barrier, inc=1, device_id=place.partner(flips), device_id_type=MESH)
    pl.semaphore_wait(barrier, len(deltas))
    for h, group in enumerate(hops):
        masks = [names[bit] for bit in group]
        if masks[0][0] == "tower":
            held = every_s.at[tower]
        else:
            mask = masks[0][1]
            held = every_s.at[tower, pl.ds(lax.div(batch, jnp.int32(mask)) * mask, mask)]
        copies = [
            pltpu.make_async_remote_copy(
                src_ref=held,
                dst_ref=held,
                send_sem=hop_send.at[h, turn],
                recv_sem=hop_recv.at[h, turn],
                device_id=place.partner(flips),
                device_id_type=MESH,
            )
            for turn, flips in enumerate(flips_of(group))
        ]
        for copy in copies:
            copy.start()
        for copy in copies:
            copy.wait()
    between()

    for t in range(2):
        for b in range(sizes["batch"]):
            staged[t, b * rows : (b + 1) * rows, :] = every_s[t, b]
    total = rows * sizes["batch"]
    loss, dpooled = contrast(staged[0, 0:total, :], staged[1, 0:total, :], doc_groups[...], positives[...])
    loss_out[...] = loss
    mine = jnp.where(tower == 0, dpooled[0], dpooled[1])
    ids = lax.broadcasted_iota(jnp.int32, (mine.shape[0], 1), 0)
    spread = [
        jnp.sum(jnp.where(ids == batch * rows + row, mine, 0.0), 0, keepdims=True) / lengths[row].astype(FULL)
        for row in range(rows)
    ]
    loads["cot"].wait()

    def full_dout(row, i):
        at = pl.ds(pl.multiple_of(row * seq + i * block, block), block)
        slot = lax.broadcasted_iota(jnp.int32, (block, 1), 0) + i * block
        return at, cot_s[at, :].astype(FULL) + jnp.where(slot < lengths[row], spread[row], 0.0)

    for row in range(rows):

        def round_dout(i, row=row):
            at, dout = full_dout(row, i)
            dout_s[at, :] = dout.astype(LOW)

        loop(seq // block, round_dout)
    between()

    for part in range(parts):
        loads["act%d" % part].wait()
        stage(dot_tn(act_s[part][...], dout_s[...]), 0, part, grads[0].at[cut(part), :])
        between()
    for name, source, target in (("q", q, 0), ("k", k, 1), ("v", v, 2), ("n1", n1, 3)):
        load(name, source, narrow.at[target])
    loads["n2"].wait()
    for part in range(parts):
        loads["slope%d" % part].wait()
        loads["wo%d" % part].wait()
        wi_chunk(part).wait()

        def inner_back(i, part=part):
            at = rows_of(i, block)
            dact = dot_nt(dout_s[at, :], square[part])
            dinner = (slope_s[part][at, :].astype(FULL) * dact).astype(LOW)
            slope_s[part][at, :] = dinner
            more = dot_nt(dinner, square[parts + part % 2])
            sum_s[at, :] = more if part == 0 else sum_s[at, :] + more

        loop(count // block, inner_back)
        if part + 2 < parts:
            wi_chunk(part + 2).start()
        stage(dot_tn(n2_s[...], slope_s[part][...]), 1, part, grads[1].at[:, cut(part)])
        between()
    load("ho", ho, narrow.at[9])
    for name, source, target in (("wm", wm, 0), ("wq", wq, 1), ("wk", wk, 2), ("wv", wv, 3)):
        load(name, source, square.at[target])
    small_out[...] = jnp.zeros_like(small_out)
    loads["h1"].wait()
    loads["wm"].wait()
    q_s, k_s, v_s, n1_s = (narrow.at[i] for i in range(4))
    dh_s, dq_s, dk_s, dv_s = (narrow.at[i] for i in range(4, 8))

    for row in range(rows):

        def mix_back(i, row=row):
            at, dout = full_dout(row, i)
            dv, dgain = norm_back(h1_s[at, :], gain2[...], sum_s[at, :])
            dh1 = dout + dv
            h1_s[at, :] = dh1
            small_out[1:2, :] = small_out[1:2, :] + dgain
            da = dh1.astype(LOW)
            cot_s[at, :] = da
            dh_s[at, :] = dot_nt(da, square[0]).astype(LOW)

        loop(seq // block, mix_back)
    between()
    loads["ho"].wait()
    stage(dot_tn(narrow[9], cot_s[...]), 5, 0, grads[5])
    between()
    for copy in list(stage_of.values()):
        copy.wait()
    stage_of.clear()
    load("x", tokens, narrow.at[9])
    for name in ("q", "k", "v"):
        loads[name].wait()

    blocks = seq // 128
    lanes = lax.broadcasted_iota(jnp.int32, (seq, 2 * size), 1)
    keys = lax.broadcasted_iota(jnp.int32, (128, seq), 0)
    first_item = item
    steps = rows * (heads // 2)

    def between_at(step, side):
        for index in range(steps):
            actions = order[first_item + 2 * index + side] if 2 * index + side < 24 else []
            if actions:
                pl.when(step == index)(functools.partial(act_on, actions))

    def attend_back(step):
        pair = lax.div(step, jnp.int32(rows))
        row = lax.rem(step, jnp.int32(rows))
        at = rows_of(row, seq)
        here = rows_of(pair, 2 * size)
        limit = lengths[row]

        @pl.when(row == 0)
        def _():
            near_s[...] = jnp.zeros_like(near_s)
            fill_bias(bias_s, table, pair * 2, 2)

        qp, kp, vp, dp = q_s[at, here], k_s[at, here], v_s[at, here], dh_s[at, here]
        nothing = jnp.zeros_like(qp)
        kt = kp.T
        dq, dk, dv = [], [], []
        score_s = [staged.at[side, 0:seq, 0:seq] for side in range(2)]
        dprob_s = [staged.at[2 + side, 0:seq, 0:seq] for side in range(2)]
        prob_s = [narrow.at[8, side * seq : (side + 1) * seq, 0:seq] for side in range(2)]
        dscore_s = [narrow.at[10, side * seq : (side + 1) * seq, 0:seq] for side in range(2)]
        for side in range(2):
            chosen = (lanes >= size) == (side == 1)
            score_s[side][...] = dot_nt(kp, jnp.where(chosen, qp, nothing))
            dprob_s[side][...] = dot_nt(vp, jnp.where(chosen, dp, nothing))
        for side in range(2):
            head = pair * 2 + side
            level = lse[row * heads + head]
            delta = jnp.zeros((1, seq), FULL)
            for jb in range(blocks):
                some = slice(jb * 128, (jb + 1) * 128)
                strip = score_s[side][some, :] + bias_strip(bias_s, side, table, head, jb, blocks)
                strip = jnp.where(keys + jb * 128 < limit, strip, NEGATIVE)
                prob = jnp.exp(strip - level)
                prob_s[side][some, :] = prob.astype(LOW)
                score_s[side][some, :] = prob
                delta = delta + jnp.sum(prob * dprob_s[side][some, :], 0, keepdims=True)
            for jb in range(blocks):
                some = slice(jb * 128, (jb + 1) * 128)
                dscore = score_s[side][some, :] * (dprob_s[side][some, :] - delta)
                dscore_s[side][some, :] = dscore.astype(LOW)
                for ib in range(blocks):
                    spot = min(max(jb - ib, -2), 2) + 2
                    near_s[side, spot] = near_s[side, spot] + dscore[:, ib * 128 : (ib + 1) * 128]
            dk.append(dot_nn(dscore_s[side][...], qp))
            dv.append(dot_nn(prob_s[side][...], dp))
            dq.append(dot_nn(kt[side * size : (side + 1) * size, :], dscore_s[side][...]))
            if side == 0:
                between_at(step, 0)
        first = lanes < size
        dk_s[at, here] = jnp.where(first, dk[0], dk[1]).astype(LOW)
        dv_s[at, here] = jnp.where(first, dv[0], dv[1]).astype(LOW)
        dq_s[at, here] = jnp.concatenate(dq, 0).T.astype(LOW)

        @pl.when(row == rows - 1)
        def _():
            ids = [offset_buckets(shift) for shift, _ in NEAR]
            for side in range(2):
                bucket = lax.broadcasted_iota(jnp.int32, (1, 128), 1)
                found = jnp.zeros((1, 128), FULL)
                for spot, (shift, members) in enumerate(NEAR):
                    total = near_s[side, spot + 1]
                    for b in members:
                        share = jnp.sum(jnp.where(ids[spot] == b, total, 0.0), 0, keepdims=True)
                        found = found + jnp.where(bucket == b, jnp.sum(share, 1, keepdims=True), 0.0)
                for spot, b in ((0, 15), (4, 31)):
                    share = jnp.sum(near_s[side, spot], 0, keepdims=True)
                    found = found + jnp.where(bucket == b, jnp.sum(share, 1, keepdims=True), 0.0)
                sums_s[pair * 2 + side] = found

        between_at(step, 1)

    loop(steps, attend_back)
    item = first_item + 24
    for head in range(heads):
        small_out[8 + head : 9 + head, 0:128] = sums_s[head]

    loads["n1"].wait()
    for matrix, d_s in ((2, dq_s), (3, dk_s), (4, dv_s)):
        stage(dot_tn(n1_s[...], d_s[...]), matrix, 0, grads[matrix])
        between()
    for name in ("wq", "wk", "wv", "x"):
        loads[name].wait()

    def input_back(i):
        at = rows_of(i, block)
        dn1 = dot_nt(dq_s[at, :], square[1]) + dot_nt(dk_s[at, :], square[2]) + dot_nt(dv_s[at, :], square[3])
        dv, dgain = norm_back(narrow[9, at, :].astype(FULL), gain1[...], dn1)
        small_out[0:1, :] = small_out[0:1, :] + dgain
        cot_s[at, :] = (h1_s[at, :] + dv).astype(LOW)

    loop(count // block, input_back)
    last = pltpu.make_async_copy(cot_s, tokens_grad, last_sem)
    last.start()

    def small_copy(bit):
        return pltpu.make_async_remote_copy(
            src_ref=small_out,
            dst_ref=small_land.at[bit],
            send_sem=small_send.at[bit],
            recv_sem=small_recv.at[bit],
            device_id=place.partner((bit,)),
            device_id_type=MESH,
        )

    small_copy(0).start()
    actions = order[item]
    for bit in range(len(names)):
        act_on(actions[len(actions) * bit // (len(names) + 1) : len(actions) * (bit + 1) // (len(names) + 1)])
        small_copy(bit).wait()
        small_out[...] = small_out[...] + small_land[bit]
        if bit + 1 < len(names):
            small_copy(bit + 1).start()
    act_on(actions[len(actions) * len(names) // (len(names) + 1) :])
    last.wait()
    for copy in stage_of.values():
        copy.wait()


def backward(
    sizes, cot, pooled, lengths, doc_groups, positives, act, slope, wo, wi, n2, h1, ho, q, k, v, n1, tokens, lse,
    wq, wk, wv, wm, gain1, gain2, table,
):
    count, width = cot.shape
    hidden = wo.shape[0]
    rows = lengths.shape[0]
    heads = table.shape[0]
    total = doc_groups.shape[0]
    names = bit_names(sizes)
    units, items = make_units(sizes, hidden, width)
    counts = set_counts(sizes)
    order, _ = plan(units, names, counts, [time for _, time in items])
    steps = max(len(unit.steps) for unit in units)
    sets = sum(counts.values())
    shape = jax.ShapeDtypeStruct
    any_spec = pl.BlockSpec(memory_space=pl.ANY)
    vmem_spec = pl.BlockSpec(memory_space=pltpu.VMEM)
    smem_spec = pl.BlockSpec(memory_space=pltpu.SMEM)
    squares = [shape((hidden, width), FULL), shape((width, hidden), FULL)] + [shape((width, width), FULL)] * 4
    hops = len(gather_groups(sizes))
    dma = pltpu.SemaphoreType.DMA
    return pl.pallas_call(
        functools.partial(backward_kernel, sizes, units, order, counts),
        out_shape=squares + squares + [shape((count, width), LOW), shape((24, width), FULL), shape((1, 1), FULL)],
        in_specs=[any_spec, vmem_spec, smem_spec, vmem_spec, vmem_spec]
        + [any_spec] * 12
        + [vmem_spec]
        + [any_spec] * 4
        + [vmem_spec] * 2
        + [smem_spec],
        out_specs=[any_spec] * 13 + [vmem_spec] * 2,
        scratch_shapes=[
            pltpu.VMEM((11, count, width), LOW),
            pltpu.VMEM((6, width, width), LOW),
            pltpu.VMEM((4, width, width), FULL),
            pltpu.VMEM((2, count, width), FULL),
            pltpu.VMEM((2, 3, 128, 128), FULL),
            pltpu.VMEM((2, 5, 128, 128), FULL),
            pltpu.VMEM((heads, 1, 128), FULL),
            pltpu.VMEM((2, sizes["batch"], rows, width), FULL),
            pltpu.VMEM((len(names), 24, width), FULL),
            pltpu.VMEM((sets, units[0].steps[0][2], width), FULL),
            pltpu.VMEM((sets, max(unit.land for unit in units), width), FULL),
            dma((32,)),
            dma((8,)),
            dma((16,)),
            dma,
            dma((hops, 3)),
            dma((hops, 3)),
            dma((len(names),)),
            dma((len(names),)),
            dma((sets, steps, 3)),
            dma((sets, steps, 3)),
            dma((sets,)),
            dma((sets,)),
        ],
        compiler_params=pltpu.CompilerParams(
            collective_id=0, has_side_effects=True, vmem_limit_bytes=int(63.5 * 2**20)
        ),
    )(
        cot, pooled, lengths, doc_groups.reshape(1, total), positives.reshape(1, total), act, slope, wo, wi, n2, h1,
        ho, q, k, v, n1, tokens, lse, wq, wk, wv, wm, gain1.reshape(1, width), gain2.reshape(1, width), table,
    )


def hand_out_kernel(count, *refs):
    sources, targets, sem = refs[:count], refs[count : 2 * count], refs[-1]
    copies = [pltpu.make_async_copy(source, target, sem.at[i]) for i, (source, target) in enumerate(zip(sources, targets))]
    for copy in copies:
        copy.start()
    for copy in copies:
        copy.wait()


def hand_out(arrays):
    any_spec = pl.BlockSpec(memory_space=pl.ANY)
    return pl.pallas_call(
        functools.partial(hand_out_kernel, len(arrays)),
        out_shape=[jax.ShapeDtypeStruct(a.shape, a.dtype) for a in arrays],
        in_specs=[any_spec] * len(arrays),
        out_specs=[any_spec] * len(arrays),
        scratch_shapes=[pltpu.SemaphoreType.DMA((len(arrays),))],
    )(*arrays)


def shards(
    tokens,
    lengths,
    doc_groups,
    positives,
    cotangent,
    w_query,
    w_key,
    w_value,
    w_mixed,
    w_inner,
    w_outer,
    gain_attn,
    gain_ffn,
    rel_table,
):
    rows = tokens.shape[1]
    count, width = rows * tokens.shape[2], tokens.shape[3]
    buckets, heads = rel_table.shape
    sizes = {axis: lax.axis_size(axis) for axis in ("tower", "batch")}
    flat = tokens.reshape(count, width)
    cot = cotangent.reshape(count, width)
    own_lengths = lengths.reshape(rows)
    table = rel_table.T
    q, k, v, ho, n1, n2, h1, act, slope, result, lse, pooled = forward(
        flat, own_lengths, w_query, w_key, w_value, w_mixed, w_inner, w_outer, gain_attn, gain_ffn, table
    )
    found = backward(
        sizes, cot, pooled, own_lengths, doc_groups, positives, act, slope, w_outer, w_inner, n2, h1, ho, q, k, v, n1,
        flat, lse, w_query, w_key, w_value, w_mixed, gain_attn, gain_ffn, table,
    )
    small, loss = found[13:]
    wo_grad, wi_grad, wq_grad, wk_grad, wv_grad, wm_grad, tokens_grad = hand_out(found[6:13])
    return (
        result.reshape(tokens.shape),
        pooled[None],
        loss[0, 0],
        tokens_grad.reshape(tokens.shape),
        wq_grad,
        wk_grad,
        wv_grad,
        wm_grad,
        wi_grad,
        wo_grad,
        small[0],
        small[1],
        small[8 : 8 + heads, :buckets].T,
    )


def solution(mesh):
    return jax.shard_map(
        shards,
        mesh=mesh,
        in_specs=(
            P("tower", "batch", None, None),
            P("tower", "batch"),
            P(),
            P(),
            P("tower", "batch", None, None),
            P(),
            P(),
            P(),
            P(),
            P(),
            P(),
            P(),
            P(),
            P(),
        ),
        out_specs=(
            P("tower", "batch", None, None),
            P("tower", "batch", None),
            P(),
            P("tower", "batch", None, None),
            P(),
            P(),
            P(),
            P(),
            P(),
            P(),
            P(),
            P(),
            P(),
        ),
        check_vma=False,
    )
```

time: 1540 us -> 1240 us (0.81)
  Pallas kernels: 0 us -> 1220 us
  waiting for transfers between devices: 851 us -> 0 us
  matrix products: 232 us -> 0 us
  blocking collectives: 217 us -> 0 us
  local copies, waits for them, and re-layouts: 132 us -> 5.26 us
  other arithmetic: 79.5 us -> 0 us
    pallas_call x0 -> x3, Pallas kernels: none -> 1220 us  [the longest x1 906 us: hand_out(): pl.pallas_call(functools.partial(hand_out_kernel, len(arrays)), out_shape...]
    reduce_scatter x6 -> x0, waiting for transfers between devices: 635 us -> none  [the longest x1 142 us: shards(): lax.psum_scatter(members[5], ('tower', 'batch'), scatter_dimension=0, til...]
    dot_general x29 -> x0, matrix products: 232 us -> none  [the longest x6 53.4 us: matmul(): return jnp.dot(left, right, preferred_element_type=jnp.float32)]
    all_gather x6 -> x0, waiting for transfers between devices: 216 us -> none  [the longest x1 83.9 us: shards(): lax.all_gather(shares[4], ('tower', 'batch'), axis=0, tiled=True)]
    all_gather x2 -> x0, blocking collectives: 137 us -> none  [the longest x1 71.1 us: shards(): lax.all_gather(pooled[None], ('tower', 'batch'), axis=1, tiled=True)[0]]
    unnamed x2 -> x0, blocking collectives: 80.6 us -> none
    reduce_sum x10 -> x0, other arithmetic: 48.2 us -> none  [the longest x1 31.3 us: shards(): bias_grad = jnp.sum(grad_scores.astype(jnp.float32), 0)]
    eq x1 -> x0, local copies, waits for them, and re-layouts: 45.3 us -> none  [bucket_onehot(): ids[:, :, None] == jnp.arange(count_buckets, dtype=jnp.int32)[None, None, :]]
  transfers between devices with their start and end apart: 12 -> 0, of which waited for: 9 -> 0; matrix products, arithmetic and copies ran while one was open for 6% -> 0% of each run, Pallas kernels for 0% -> 0%
where the time goes in v3:
time: 1240 us; the launch traced here: 1230 us
  Pallas kernels  1220 us (98%)
    pallas_call x1, Pallas kernels, hand_out(): pl.pallas_call(functools.partial(hand_out_kernel, len(arrays)), out_shape...  906 us
    pallas_call x1, Pallas kernels, backward(): pl.pallas_call(functools.partial(backward_kernel, sizes, units, order, co...  267 us
    pallas_call x1, Pallas kernels, forward(): pl.pallas_call(forward_kernel, out_shape=[low, low, low, low, low, low, s...  48 us

profile of v3, /device:TPU:0, one launch (start us, length us, event | category | flops | bytes accessed | tf_op | source)
XLA Modules:
  0.0 1229.5 jit_solution(898103441462556353)
XLA Ops:
  0.6 1.3 reshape.57.gain1
  1.9 1.3 reshape.58.gain2
  3.2 48.0 %shard_map.237 = (bf16[1024,768]{1,0:T(8,128)(2,1)}, bf16[1024,768]{1,0:T(8,128)(2,1)}, bf16[1024,768]{1,0:T(8,128)(2,1)}, bf16[1024,768]{1,0:T(8,128)(2,1)}, bf...) custom-call(bf16[1024,768]{1,0:T(8,128)(2,1)} %bitcast.12, ...), custom_call_target="tpu_custom_call" | custom-call | tf_op jit(solution)/shard_map/pallas_call | solution.py:498
  51.2 266.9 %shard_map.238 = (f32[3072,768]{1,0:T(8,128)}, f32[768,3072]{1,0:T(8,128)}, f32[768,768]{1,0:T(8,128)}, f32[768,768]{1,0:T(8,128)}, f32[768,768]{1,0:T(8,128)}, ...) custom-call(bf16[1024,768]{1,0:T(8,128)(2,1)} %bitcast.14, ...), custom_call_target="tpu_custom_call" | custom-call | tf_op jit(solution)/shard_map/pallas_call | solution.py:940
  318.1 906.4 %shard_map.239 = (f32[3072,768]{1,0:T(8,128)}, f32[768,3072]{1,0:T(8,128)}, f32[768,768]{1,0:T(8,128)}, f32[768,768]{1,0:T(8,128)}, f32[768,768]{1,0:T(8,128)}, ...) custom-call(f32[3072,768]{1,0:T(8,128)} %get-tuple-element.54.refs_0_, f32[768,3072]{1,0:T(8,128)} %get-tuple-element.55.refs_1_, ...), custom_call_target="tpu_custom_call" | custom-call | tf_op jit(solution)/shard_map/pallas_call | solution.py:995
  1224.6 1.3 slice_bitcast_fusion
  1225.9 1.4 slice_reduce_fusion

commit v4 on v3

--- a/solution.py
+++ b/solution.py
@@ -377,7 +377,7 @@
         at = rows_of(i, block)
         x = x_s[at, :].astype(FULL)
         scale = lax.rsqrt(jnp.mean(x * x, -1, keepdims=True) + EPSILON)
-        n1_s[at, :] = (x * scale * gain1[...]).astype(LOW)
+        n1_s[at, :] = (x * scale * gain1[...].reshape(1, width)).astype(LOW)
 
     loop(count // block, norm1)
     store(n1_s, n1_out)
@@ -438,7 +438,7 @@
         h1 = x_s[at, :].astype(FULL) + dot_nn(ho_s[at, :], wm_s[...])
         h1_s[at, :] = h1
         scale = lax.rsqrt(jnp.mean(h1 * h1, -1, keepdims=True) + EPSILON)
-        n2_s[at, :] = (h1 * scale * gain2[...]).astype(LOW)
+        n2_s[at, :] = (h1 * scale * gain2[...].reshape(1, width)).astype(LOW)
 
     loop(count // block, mix)
     store(h1_s, h1_out)
@@ -513,7 +513,7 @@
             pltpu.SemaphoreType.DMA((24,)),
         ],
         compiler_params=pltpu.CompilerParams(vmem_limit_bytes=62 * 2**20),
-    )(tokens, lengths, wq, wk, wv, wm, wi, wo, gain1.reshape(1, width), gain2.reshape(1, width), table)
+    )(tokens, lengths, wq, wk, wv, wm, wi, wo, gain1, gain2, table)
 
 
 def norm_back(values, gain, dy):
@@ -765,7 +765,7 @@
 
         def mix_back(i, row=row):
             at, dout = full_dout(row, i)
-            dv, dgain = norm_back(h1_s[at, :], gain2[...], sum_s[at, :])
+            dv, dgain = norm_back(h1_s[at, :], gain2[...].reshape(1, width), sum_s[at, :])
             dh1 = dout + dv
             h1_s[at, :] = dh1
             small_out[1:2, :] = small_out[1:2, :] + dgain
@@ -883,7 +883,7 @@
     def input_back(i):
         at = rows_of(i, block)
         dn1 = dot_nt(dq_s[at, :], square[1]) + dot_nt(dk_s[at, :], square[2]) + dot_nt(dv_s[at, :], square[3])
-        dv, dgain = norm_back(narrow[9, at, :].astype(FULL), gain1[...], dn1)
+        dv, dgain = norm_back(narrow[9, at, :].astype(FULL), gain1[...].reshape(1, width), dn1)
         small_out[0:1, :] = small_out[0:1, :] + dgain
         cot_s[at, :] = (h1_s[at, :] + dv).astype(LOW)
 
@@ -977,28 +977,59 @@
         ),
     )(
         cot, pooled, lengths, doc_groups.reshape(1, total), positives.reshape(1, total), act, slope, wo, wi, n2, h1,
-        ho, q, k, v, n1, tokens, lse, wq, wk, wv, wm, gain1.reshape(1, width), gain2.reshape(1, width), table,
+        ho, q, k, v, n1, tokens, lse, wq, wk, wv, wm, gain1, gain2, table,
     )
 
 
-def hand_out_kernel(count, *refs):
-    sources, targets, sem = refs[:count], refs[count : 2 * count], refs[-1]
-    copies = [pltpu.make_async_copy(source, target, sem.at[i]) for i, (source, target) in enumerate(zip(sources, targets))]
-    for copy in copies:
-        copy.start()
-    for copy in copies:
-        copy.wait()
-
-
-def hand_out(arrays):
+def hand_out_kernel(blocks, count, heads, *refs):
+    sources, (small, loss_in) = refs[:count], refs[count : count + 2]
+    targets = refs[count + 2 : 2 * count + 2]
+    gain1, gain2, table, loss = refs[2 * count + 2 : 2 * count + 6]
+    full, low, in_sem, out_sem = refs[2 * count + 6 :]
+    loads, stores = [], []
+    for i, (array, spot, at) in enumerate(blocks):
+        held = (low if sources[array].dtype == LOW else full).at[spot]
+        loads.append(pltpu.make_async_copy(sources[array].at[at], held, in_sem.at[i]))
+        stores.append(pltpu.make_async_copy(held, targets[array].at[at], out_sem.at[i]))
+    for load in loads:
+        load.start()
+    gain1[...] = small[0]
+    gain2[...] = small[1]
+    loss[...] = loss_in[...]
+    table[...] = small[8 : 8 + heads, 0 : table.shape[1]]
+    for load, store in zip(loads, stores):
+        load.wait()
+        store.start()
+    for store in stores:
+        store.wait()
+
+
+def hand_out(arrays, small, loss, heads, buckets):
+    width = small.shape[1]
+    blocks, held = [], {FULL: 0, LOW: 0}
+    for i, array in enumerate(arrays):
+        for col in range(0, array.shape[1], width):
+            for row in range(0, array.shape[0], UNIT_ROWS):
+                kind = LOW if array.dtype == LOW else FULL
+                blocks.append((i, held[kind], (pl.ds(row, UNIT_ROWS), pl.ds(col, width))))
+                held[kind] += 1
     any_spec = pl.BlockSpec(memory_space=pl.ANY)
+    vmem_spec = pl.BlockSpec(memory_space=pltpu.VMEM)
+    shape = jax.ShapeDtypeStruct
     return pl.pallas_call(
-        functools.partial(hand_out_kernel, len(arrays)),
-        out_shape=[jax.ShapeDtypeStruct(a.shape, a.dtype) for a in arrays],
-        in_specs=[any_spec] * len(arrays),
-        out_specs=[any_spec] * len(arrays),
-        scratch_shapes=[pltpu.SemaphoreType.DMA((len(arrays),))],
-    )(*arrays)
+        functools.partial(hand_out_kernel, blocks, len(arrays), heads),
+        out_shape=[shape(a.shape, a.dtype) for a in arrays]
+        + [shape((width,), FULL), shape((width,), FULL), shape((heads, buckets), FULL), shape((1, 1), FULL)],
+        in_specs=[any_spec] * len(arrays) + [vmem_spec] * 2,
+        out_specs=[any_spec] * len(arrays) + [vmem_spec] * 4,
+        scratch_shapes=[
+            pltpu.VMEM((held[FULL], UNIT_ROWS, width), FULL),
+            pltpu.VMEM((held[LOW], UNIT_ROWS, width), LOW),
+            pltpu.SemaphoreType.DMA((len(blocks),)),
+            pltpu.SemaphoreType.DMA((len(blocks),)),
+        ],
+        compiler_params=pltpu.CompilerParams(vmem_limit_bytes=63 * 2**20),
+    )(*arrays, small, loss)
 
 
 def shards(
@@ -1033,7 +1064,8 @@
         flat, lse, w_query, w_key, w_value, w_mixed, gain_attn, gain_ffn, table,
     )
     small, loss = found[13:]
-    wo_grad, wi_grad, wq_grad, wk_grad, wv_grad, wm_grad, tokens_grad = hand_out(found[6:13])
+    given = hand_out(found[6:13], small, loss, heads, buckets)
+    wo_grad, wi_grad, wq_grad, wk_grad, wv_grad, wm_grad, tokens_grad, gain1_grad, gain2_grad, table_grad, loss = given
     return (
         result.reshape(tokens.shape),
         pooled[None],
@@ -1045,9 +1077,9 @@
         wm_grad,
         wi_grad,
         wo_grad,
-        small[0],
-        small[1],
-        small[8 : 8 + heads, :buckets].T,
+        gain1_grad,
+        gain2_grad,
+        table_grad.T,
     )
 
 

time: 1240 us -> 345 us (0.28)
  Pallas kernels: 1220 us -> 337 us
    pallas_call x1, Pallas kernels: 906 us -> 22.7 us  [hand_out(): pl.pallas_call(functools.partial(hand_out_kernel, blocks, len(arrays), he...]
where the time goes in v4:
time: 345 us; the launch traced here: 338 us
  Pallas kernels  337 us (98%)
    pallas_call x1, Pallas kernels, backward(): pl.pallas_call(functools.partial(backward_kernel, sizes, units, order, co...  267 us
    pallas_call x1, Pallas kernels, forward(): pl.pallas_call(forward_kernel, out_shape=[low, low, low, low, low, low, s...  48 us
    pallas_call x1, Pallas kernels, hand_out(): pl.pallas_call(functools.partial(hand_out_kernel, blocks, len(arrays), he...  22.7 us

profile of v4, /device:TPU:0, one launch (start us, length us, event | category | flops | bytes accessed | tf_op | source)
XLA Modules:
  0.0 338.4 jit_solution(10288553027943362923)
XLA Ops:
  0.6 48.0 %shard_map.237 = (bf16[1024,768]{1,0:T(8,128)(2,1)}, bf16[1024,768]{1,0:T(8,128)(2,1)}, bf16[1024,768]{1,0:T(8,128)(2,1)}, bf16[1024,768]{1,0:T(8,128)(2,1)}, bf...) custom-call(bf16[1024,768]{1,0:T(8,128)(2,1)} %bitcast.11, ...), custom_call_target="tpu_custom_call" | custom-call | tf_op jit(solution)/shard_map/pallas_call | solution.py:498
  48.7 266.5 %shard_map.238 = (f32[3072,768]{1,0:T(8,128)}, f32[768,3072]{1,0:T(8,128)}, f32[768,768]{1,0:T(8,128)}, f32[768,768]{1,0:T(8,128)}, f32[768,768]{1,0:T(8,128)}, ...) custom-call(bf16[1024,768]{1,0:T(8,128)(2,1)} %bitcast.13, ...), custom_call_target="tpu_custom_call" | custom-call | tf_op jit(solution)/shard_map/pallas_call | solution.py:940
  315.2 22.7 %shard_map.239 = (f32[3072,768]{1,0:T(8,128)}, f32[768,3072]{1,0:T(8,128)}, f32[768,768]{1,0:T(8,128)}, f32[768,768]{1,0:T(8,128)}, f32[768,768]{1,0:T(8,128)}, ...) custom-call(f32[3072,768]{1,0:T(8,128)} %get-tuple-element.57.refs_0, ...), custom_call_target="tpu_custom_call" | custom-call | tf_op jit(solution)/shard_map/pallas_call | solution.py:1019

commit v5 on v4

--- a/solution.py
+++ b/solution.py
@@ -17,10 +17,10 @@
 MESH = pl.DeviceIdType.MESH
 LINK = 45.7e3
 CORE = 500e3
-FLIGHT = 1.8
+FLIGHT = 4.0
 CLASSES = "ABCD"
 PATTERN = "ABCABD"
-UNIT_ROWS = 256
+UNIT_COLS = 256
 
 
 def bit_names(sizes):
@@ -34,12 +34,11 @@
 
 
 def set_counts(sizes):
-    return {"A": 5, "B": 5, "C": 3, "D": 3} if sizes["batch"] <= 16 else {"A": 3, "B": 3, "C": 2, "D": 2}
+    return {"A": 7, "B": 7, "C": 4, "D": 4} if sizes["batch"] <= 16 else {"A": 2, "B": 2, "C": 1, "D": 1}
 
 
 def bit_groups(sizes):
     names = bit_names(sizes)
-    core = [(k,) for k, name in enumerate(names) if name[0] == "tower"]
     rest = [k for k, name in enumerate(names) if name[0] == "batch"]
     x, y, low, high = rest[:4]
     more = [(k,) for k in rest[4:]]
@@ -49,7 +48,7 @@
         "C": [(low,), (x,), (y,), (high,)],
         "D": [(low,), (y,), (x,), (high,)],
     }
-    return {name: core + groups + more for name, groups in firsts.items()}
+    return {name: groups + more for name, groups in firsts.items()}
 
 
 def flips_of(group):
@@ -85,10 +84,10 @@
 
 
 class Unit:
-    def __init__(self, matrix, row, col, cols, kind, groups, item):
-        self.matrix, self.row, self.col, self.cols, self.kind, self.item = matrix, row, col, cols, kind, item
+    def __init__(self, matrix, row, rows, col, cols, kind, groups, item):
+        self.matrix, self.row, self.rows, self.col, self.cols, self.kind, self.item = matrix, row, rows, col, cols, kind, item
         self.steps = []
-        size, back, land = UNIT_ROWS, [], 0
+        size, back, land = rows, [], 0
         for group in groups:
             ways = 2 ** len(group)
             if size % (8 * ways) == 0:
@@ -103,16 +102,17 @@
         self.land = land
         self.returns = len(self.steps)
         self.steps += back[::-1]
+        self.steps.append(("join", (0,), rows, 0))
 
     def place_at(self, place):
-        start, stack = jnp.int32(self.row), []
+        start, stack = self.row + place.at["tower"] * self.rows, []
         self.starts = []
         for kind, group, size, _ in self.steps:
             self.starts.append(start)
             if kind == "cut":
                 stack.append(start)
                 start = start + place.code(group) * size
-            elif kind == "join":
+            elif kind == "join" and stack:
                 start = stack.pop()
 
 
@@ -130,7 +130,7 @@
     return {mask: link * (2 ** len(group) - 1) for mask in masks}
 
 
-def plan(units, names, counts, items, depth=4.0):
+def plan(units, names, counts, items, depth=8.0):
     free, clock, flight, pending = {}, 0.0, [], []
     idle = {kind: [(kind, i) for i in range(counts[kind])] for kind in CLASSES}
     done, order = 0, [[] for _ in items]
@@ -195,7 +195,7 @@
 class Exchange:
     def __init__(self, units, place, counts, grads, kept, land, outs, sems):
         self.units, self.place, self.grads, self.kept, self.land, self.outs = units, place, grads, kept, land, outs
-        self.send_sem, self.recv_sem, self.load_sem, self.store_sem = sems
+        self.send_sem, self.recv_sem, self.load_sem, self.store_sem, self.last_send, self.last_recv = sems
         self.sets = {name: i for i, name in enumerate((kind, i) for kind in CLASSES for i in range(counts[kind]))}
         for unit in units:
             unit.place_at(place)
@@ -220,7 +220,9 @@
             self.own(unit, start, rows), self.part(self.outs, unit, start, rows), self.store_sem.at[spot]
         )
 
-    def copies(self, unit, s):
+    def copies(self, u, s):
+        unit = self.units[u]
+        last = s == len(unit.steps) - 1
         kind, group, size, land = unit.steps[s]
         spot, found = self.sets[unit.set], []
         for turn, flips in enumerate(flips_of(group)):
@@ -241,8 +243,8 @@
                 pltpu.make_async_remote_copy(
                     src_ref=source,
                     dst_ref=target,
-                    send_sem=self.send_sem.at[spot, s, turn],
-                    recv_sem=self.recv_sem.at[spot, s, turn],
+                    send_sem=self.last_send.at[u] if last else self.send_sem.at[spot, s, turn],
+                    recv_sem=self.last_recv.at[u] if last else self.recv_sem.at[spot, s, turn],
                     device_id=self.place.partner(flips),
                     device_id_type=MESH,
                 )
@@ -253,14 +255,14 @@
         unit = self.units[u]
         if s == 0:
             self.load(unit).start()
-        for copy in self.copies(unit, s):
+        for copy in self.copies(u, s):
             copy.start()
 
     def serve(self, u, s):
         unit = self.units[u]
         if s == 0:
             self.load(unit).wait()
-        for copy in self.copies(unit, s):
+        for copy in self.copies(u, s):
             copy.wait()
         kind, group, size, land = unit.steps[s]
         if kind != "join":
@@ -345,7 +347,7 @@
 
 def forward_kernel(
     tokens, lengths, wq, wk, wv, wm, wi, wo, gain1, gain2, table,
-    q_out, k_out, v_out, ho_out, n1_out, n2_out, h1_out, act_out, slope_out, result_out, lse_out, pooled_out,
+    q_out, k_out, v_out, ho_out, n1_out, n2_out, h1_out, act_out, slope_out, result_out, lse_out, pooled_out, sums_out,
     x_s, wq_s, wk_s, wv_s, wm_s, wi_s, wo_s, q_s, k_s, v_s, ho_s, n1_s, n2_s, h1_s, act_s, slope_s, result_s, total_s,
     score_s, prob_s, bias_s, in_sem, out_sem,
 ):
@@ -445,6 +447,13 @@
     store(n2_s, n2_out)
     loads[5].wait()
     loads[6].wait()
+    lane = lax.broadcasted_iota(jnp.int32, (16, count), 1)
+    which = lax.broadcasted_iota(jnp.int32, (16, count), 0)
+    marks = jnp.zeros((16, count), FULL)
+    for row in range(rows):
+        inside = (which == row) & (lane >= row * seq) & (lane < row * seq + lengths[row])
+        marks = jnp.where(inside, 1.0, marks)
+    marks = marks.astype(LOW)
 
     for part in range(parts):
         columns = pl.ds(part * width, width)
@@ -469,6 +478,9 @@
 
         loop(count // block, feed)
         store(act_s.at[:, columns], act_out.at[:, columns])
+        sums = dot_nn(marks, act_s[:, columns])
+        for row in range(rows):
+            sums_out[part * rows + row : part * rows + row + 1, :] = sums[row : row + 1] / lengths[row].astype(FULL)
         store(slope_s.at[:, columns], slope_out.at[:, columns])
     store(result_s, result_out)
     slots = lax.broadcasted_iota(jnp.int32, (seq, 1), 0)
@@ -498,9 +510,10 @@
     return pl.pallas_call(
         forward_kernel,
         out_shape=[low, low, low, low, low, low, shape((count, width), FULL), wide, wide, low]
-        + [shape((rows * heads, 1, seq), FULL), shape((rows, width), FULL)],
+        + [shape((rows * heads, 1, seq), FULL), shape((rows, width), FULL)]
+        + [shape((hidden // width * rows, width), FULL)],
         in_specs=[any_spec, smem_spec] + [any_spec] * 6 + [vmem_spec] * 2 + [smem_spec],
-        out_specs=[any_spec] * 10 + [vmem_spec] * 2,
+        out_specs=[any_spec] * 10 + [vmem_spec] * 3,
         scratch_shapes=[narrow_s]
         + weights
         + [narrow_s] * 6
@@ -548,44 +561,65 @@
     return loss, dpooled
 
 
-def make_units(sizes, hidden, width):
+def is_early(sizes, rows):
+    return sizes["tower"] * sizes["batch"] * rows <= 128
+
+
+def make_units(sizes, rows, hidden, width):
     groups = bit_groups(sizes)
-    parts, thirds = hidden // width, width // UNIT_ROWS
-    items = [("gather", 12.0), ("loss", 3.0)]
-    blocks = []
+    early = is_early(sizes, rows)
+    parts = hidden // width
+    items, blocks = [], []
+
+    def add(matrix, row, first, item):
+        blocks.extend((matrix, row, col, item) for col in range(first, first + width, UNIT_COLS))
+
+    def outer():
+        for part in range(parts):
+            items.append(("outer", 2.6))
+            add(0, part * width, 0, len(items))
+
+    if early:
+        outer()
+        items.append(("hop", 2.0))
+    else:
+        items.append(("hop", 12.0))
+    items.append(("loss", 4.0))
+    if not early:
+        outer()
     for part in range(parts):
-        items.append(("outer", 1.9))
-        blocks += [(0, part * width + i * UNIT_ROWS, 0, len(items)) for i in range(thirds)]
-    for part in range(parts):
-        items.append(("inner", 6.2))
-        blocks += [(1, i * UNIT_ROWS, part * width, len(items)) for i in range(thirds)]
-    items += [("mix", 3.5), ("mixed", 1.8)]
-    blocks += [(5, i * UNIT_ROWS, 0, len(items)) for i in range(thirds)]
-    items += [("attend", 2.4)] * 24
-    for matrix in range(2, 5):
-        items.append(("projection", 1.8))
-        blocks += [(matrix, i * UNIT_ROWS, 0, len(items)) for i in range(thirds)]
-    items.append(("input", 6.0))
+        items.append(("inner", 6.4))
+        add(1, 0, part * width, len(items))
+    items.append(("mix", 4.0))
+    items.append(("mixed", 1.8))
+    first = len(items)
+    items += [("attend", 2.5)] * 24
+    add(5, 0, 0, first + 4)
+    for turn in range(3):
+        item = first + 8 * turn + 10 if turn < 2 else first + 25
+        blocks.extend((matrix, 0, turn * UNIT_COLS, item) for matrix in range(2, 5))
+    items.append(("flush", 3.0))
+    items += [("input", 1.6)] * 4
     units = []
     for i, (matrix, row, col, item) in enumerate(blocks):
         kind = PATTERN[i % len(PATTERN)]
-        units.append(Unit(matrix, row, col, width, kind, groups[kind], item))
+        units.append(Unit(matrix, row, width // 2, col, UNIT_COLS, kind, groups[kind], item))
     return units, items
 
 
 def backward_kernel(
     sizes, units, order, counts,
-    cot, pooled, lengths, doc_groups, positives, act, slope, wo, wi, n2, h1, ho, q, k, v, n1, tokens, lse,
+    cot, pooled, sums, lengths, doc_groups, positives, act, slope, wo, wi, n2, h1, ho, q, k, v, n1, tokens, lse,
     wq, wk, wv, wm, gain1, gain2, table,
     *refs,
 ):
     grads, outs = refs[:6], refs[6:12]
-    tokens_grad, small_out, loss_out = refs[12:15]
+    tokens_grad, u_out, small_out, loss_out, dpooled_out = refs[12:17]
     (
-        narrow, square, staged, full, bias_s, near_s, sums_s, every_s, small_land, kept, land,
-        in_sem, chunk_sem, stage_sem, last_sem, hop_send, hop_recv, small_send, small_recv,
-        send_sem, recv_sem, load_sem, store_sem,
-    ) = refs[15:]
+        narrow, square, staged, full, bias_s, near_s, sums_s, every_s, every_u, thirds_s, core_land, small_land, kept, land,
+        in_sem, chunk_sem, stage_sem, core_send, core_recv, last_sem, hop_send, hop_recv, small_send, small_recv,
+        send_sem, recv_sem, load_sem, store_sem, final_send, final_recv,
+    ) = refs[17:]
     count, width = narrow.shape[1:]
     rows = lengths.shape[0]
     seq = count // rows
@@ -596,7 +630,9 @@
     place = Place(sizes)
     names = place.names
     tower, batch = place.at["tower"], place.at["batch"]
-    exchange = Exchange(units, place, counts, grads, kept, land, outs, (send_sem, recv_sem, load_sem, store_sem))
+    exchange = Exchange(
+        units, place, counts, grads, kept, land, outs, (send_sem, recv_sem, load_sem, store_sem, final_send, final_recv)
+    )
     cot_s, n2_s, dout_s = narrow.at[8], narrow.at[9], narrow.at[10]
     act_s = [narrow.at[part] for part in range(parts)]
     slope_s = [narrow.at[parts + part] for part in range(parts)]
@@ -627,6 +663,8 @@
         wi_chunk(part).start()
     load("h1", h1, h1_s)
 
+    early = is_early(sizes, rows)
+
     item = 0
     stage_of = {}
 
@@ -643,30 +681,84 @@
         unit = units[u]
         key = (unit.matrix, unit.row // width if unit.matrix == 0 else unit.col // width)
         if key in stage_of:
-            stage_of.pop(key).wait()
+            stage_of.pop(key)()
 
     def between():
         nonlocal item
         act_on(order[item])
         item += 1
 
-    staged_count = 0
+    half = width // 2
+    own_half = pl.ds(pl.multiple_of(tower * half, 8), half)
+    other_half = pl.ds(pl.multiple_of((1 - tower) * half, 8), half)
+    core_bit = next(bit for bit, name in enumerate(names) if name[0] == "tower")
+
+    def thirds_of(square_ref):
+        return [square_ref.at[:, pl.ds(i * UNIT_COLS, UNIT_COLS)] for i in range(3)]
+
+    def core_copies(turn, pieces):
+        return [
+            pltpu.make_async_remote_copy(
+                src_ref=piece.at[other_half, :],
+                dst_ref=core_land.at[turn % 2, i],
+                send_sem=core_send.at[turn % 2, i],
+                recv_sem=core_recv.at[turn % 2, i],
+                device_id=place.partner((core_bit,)),
+                device_id_type=MESH,
+            )
+            for i, piece in enumerate(pieces)
+        ]
+
+    def out_copies(turn, pieces, targets):
+        return [
+            pltpu.make_async_copy(piece.at[own_half, :], target.at[own_half, :], stage_sem.at[turn, i])
+            for i, (piece, target) in enumerate(zip(pieces, targets))
+        ]
+
+    def core_send_off(turn, pieces):
+        for copy in core_copies(turn, pieces):
+            copy.start()
+
+    def core_add(turn, pieces, targets):
+        for copy in core_copies(turn, pieces):
+            copy.wait()
+        for i, piece in enumerate(pieces):
+            piece[own_half, :] = piece[own_half, :] + core_land[turn % 2, i]
+        for copy in out_copies(turn, pieces, targets):
+            copy.start()
+
+    def core_done(turn, pieces, targets):
+        for copy in out_copies(turn, pieces, targets):
+            copy.wait()
+
+    sent = []
+
+    def settle():
+        if sent:
+            key, turn, pieces, targets = sent.pop()
+            core_add(turn, pieces, targets)
+            stage_of[key] = functools.partial(core_done, turn, pieces, targets)
+
+    def stage(turn, matrix, part, value, target):
+        key = (matrix, part)
+        last = [old for old, spot in staged_last.items() if spot == turn % 3]
+        for old in last:
+            staged_last.pop(old)
+            if old in stage_of:
+                stage_of.pop(old)()
+        staged[turn % 3] = value
+        settle()
+        pieces = thirds_of(staged.at[turn % 3])
+        core_send_off(turn, pieces)
+        sent.append((key, turn, pieces, thirds_of(target)))
+        staged_last[key] = turn % 3
+
     staged_last = {}
-
-    def stage(value, matrix, part, target):
-        nonlocal staged_count
-        spot = staged_count % 3
-        if spot in staged_last and staged_last[spot] in stage_of:
-            stage_of.pop(staged_last[spot]).wait()
-        staged[spot] = value
-        copy = pltpu.make_async_copy(staged.at[spot], target, stage_sem.at[staged_count])
-        copy.start()
-        stage_of[(matrix, part)] = copy
-        staged_last[spot] = (matrix, part)
-        staged_count += 1
 
     hops = gather_groups(sizes)
     every_s[tower, batch] = pooled[...]
+    if early:
+        every_u[tower, batch] = sums[...]
     deltas = set()
     for group in list(bit_groups(sizes).values()) + [hops]:
         for bits in group:
@@ -675,35 +767,64 @@
     for flips in sorted(deltas):
         pl.semaphore_signal(barrier, inc=1, device_id=place.partner(flips), device_id_type=MESH)
     pl.semaphore_wait(barrier, len(deltas))
-    for h, group in enumerate(hops):
+
+    def hop(h, kind=0):
+        group = hops[h]
         masks = [names[bit] for bit in group]
+        every = (every_s, every_u)[kind]
         if masks[0][0] == "tower":
-            held = every_s.at[tower]
+            held = every.at[tower]
         else:
             mask = masks[0][1]
-            held = every_s.at[tower, pl.ds(lax.div(batch, jnp.int32(mask)) * mask, mask)]
-        copies = [
+            held = every.at[tower, pl.ds(lax.div(batch, jnp.int32(mask)) * mask, mask)]
+        return [
             pltpu.make_async_remote_copy(
                 src_ref=held,
                 dst_ref=held,
-                send_sem=hop_send.at[h, turn],
-                recv_sem=hop_recv.at[h, turn],
+                send_sem=hop_send.at[h, 3 * kind + turn],
+                recv_sem=hop_recv.at[h, 3 * kind + turn],
                 device_id=place.partner(flips),
                 device_id_type=MESH,
             )
             for turn, flips in enumerate(flips_of(group))
         ]
-        for copy in copies:
-            copy.start()
-        for copy in copies:
+
+    def outer(part, right):
+        loads["act%d" % part].wait()
+        stage(part, 0, part, dot_tn(act_s[part][...], right[...]), grads[0].at[cut(part), :])
+
+    for copy in hop(0):
+        copy.start()
+    served = 0
+    if early:
+        loads["cot"].wait()
+        for part in range(parts):
+            outer(part, cot_s)
+            if part >= 1 and served < len(hops) - 1:
+                for copy in hop(served):
+                    copy.wait()
+                served += 1
+                for copy in hop(served):
+                    copy.start()
+            between()
+    while served < len(hops):
+        for copy in hop(served):
             copy.wait()
+        served += 1
+        if served < len(hops):
+            for copy in hop(served):
+                copy.start()
+    settle()
     between()
 
+    total = rows * sizes["batch"]
     for t in range(2):
         for b in range(sizes["batch"]):
-            staged[t, b * rows : (b + 1) * rows, :] = every_s[t, b]
-    total = rows * sizes["batch"]
-    loss, dpooled = contrast(staged[0, 0:total, :], staged[1, 0:total, :], doc_groups[...], positives[...])
+            first = t * total + b * rows
+            staged[3, first : first + rows, :] = every_s[t, b]
+    loss, dpooled = contrast(
+        staged[3, 0:total, :], staged[3, total : 2 * total, :], doc_groups[...], positives[...]
+    )
     loss_out[...] = loss
     mine = jnp.where(tower == 0, dpooled[0], dpooled[1])
     ids = lax.broadcasted_iota(jnp.int32, (mine.shape[0], 1), 0)
@@ -711,7 +832,13 @@
         jnp.sum(jnp.where(ids == batch * rows + row, mine, 0.0), 0, keepdims=True) / lengths[row].astype(FULL)
         for row in range(rows)
     ]
-    loads["cot"].wait()
+    dpooled_out[0:total, :] = dpooled[0]
+    dpooled_out[total : 2 * total, :] = dpooled[1]
+    if early:
+        for copy in hop(0, 1):
+            copy.start()
+    else:
+        loads["cot"].wait()
 
     def full_dout(row, i):
         at = pl.ds(pl.multiple_of(row * seq + i * block, block), block)
@@ -727,10 +854,10 @@
         loop(seq // block, round_dout)
     between()
 
-    for part in range(parts):
-        loads["act%d" % part].wait()
-        stage(dot_tn(act_s[part][...], dout_s[...]), 0, part, grads[0].at[cut(part), :])
-        between()
+    if not early:
+        for part in range(parts):
+            outer(part, dout_s)
+            between()
     for name, source, target in (("q", q, 0), ("k", k, 1), ("v", v, 2), ("n1", n1, 3)):
         load(name, source, narrow.at[target])
     loads["n2"].wait()
@@ -750,8 +877,17 @@
         loop(count // block, inner_back)
         if part + 2 < parts:
             wi_chunk(part + 2).start()
-        stage(dot_tn(n2_s[...], slope_s[part][...]), 1, part, grads[1].at[:, cut(part)])
+        stage(parts + part, 1, part, dot_tn(n2_s[...], slope_s[part][...]), grads[1].at[:, cut(part)])
+        if early and part < len(hops):
+            for copy in hop(part, 1):
+                copy.wait()
+            if part + 1 < len(hops):
+                for copy in hop(part + 1, 1):
+                    copy.start()
         between()
+    if early:
+        u_copy = pltpu.make_async_copy(every_u, u_out, last_sem.at[1])
+        u_copy.start()
     load("ho", ho, narrow.at[9])
     for name, source, target in (("wm", wm, 0), ("wq", wq, 1), ("wk", wk, 2), ("wv", wv, 3)):
         load(name, source, square.at[target])
@@ -774,15 +910,23 @@
             dh_s[at, :] = dot_nt(da, square[0]).astype(LOW)
 
         loop(seq // block, mix_back)
+    settle()
     between()
     loads["ho"].wait()
-    stage(dot_tn(narrow[9], cot_s[...]), 5, 0, grads[5])
+    third_refs = [thirds_s.at[i] for i in range(3)]
+    third_targets = [thirds_of(grads[5])] + [
+        [grads[2 + i].at[:, pl.ds(turn * UNIT_COLS, UNIT_COLS)] for i in range(3)] for turn in range(3)
+    ]
+    first_turn = 2 * parts
+    for i in range(3):
+        thirds_s[i] = dot_tn(narrow[9], cot_s[:, pl.ds(i * UNIT_COLS, UNIT_COLS)])
+    core_send_off(first_turn, third_refs)
     between()
-    for copy in list(stage_of.values()):
-        copy.wait()
+    for done in list(stage_of.values()):
+        done()
     stage_of.clear()
     load("x", tokens, narrow.at[9])
-    for name in ("q", "k", "v"):
+    for name in ("q", "k", "v", "n1"):
         loads[name].wait()
 
     blocks = seq // 128
@@ -796,6 +940,19 @@
             actions = order[first_item + 2 * index + side] if 2 * index + side < 24 else []
             if actions:
                 pl.when(step == index)(functools.partial(act_on, actions))
+
+    per_turn = 2 * rows
+
+    def third(turn):
+        for i, d_s in enumerate((dq_s, dk_s, dv_s)):
+            thirds_s[i] = dot_tn(n1_s[...], d_s[:, pl.ds(turn * UNIT_COLS, UNIT_COLS)])
+        core_send_off(first_turn + 1 + turn, third_refs)
+
+    def third_add(turn):
+        core_add(first_turn + 1 + turn, third_refs, third_targets[1 + turn])
+
+    def third_done(turn):
+        core_done(first_turn + 1 + turn, third_refs, third_targets[1 + turn])
 
     def attend_back(step):
         pair = lax.div(step, jnp.int32(rows))
@@ -803,6 +960,10 @@
         at = rows_of(row, seq)
         here = rows_of(pair, 2 * size)
         limit = lengths[row]
+        for turn in range(-1, steps // per_turn - 1):
+            ready = per_turn * (turn + 1) if turn >= 0 else 1
+            pl.when(step == ready)(functools.partial(third_add, turn))
+            pl.when(step == ready + 1)(functools.partial(third_done, turn))
 
         @pl.when(row == 0)
         def _():
@@ -866,6 +1027,8 @@
                     found = found + jnp.where(bucket == b, jnp.sum(share, 1, keepdims=True), 0.0)
                 sums_s[pair * 2 + side] = found
 
+        for turn in range(steps // per_turn):
+            pl.when(step == per_turn * (turn + 1) - 1)(functools.partial(third, turn))
         between_at(step, 1)
 
     loop(steps, attend_back)
@@ -873,10 +1036,10 @@
     for head in range(heads):
         small_out[8 + head : 9 + head, 0:128] = sums_s[head]
 
-    loads["n1"].wait()
-    for matrix, d_s in ((2, dq_s), (3, dk_s), (4, dv_s)):
-        stage(dot_tn(n1_s[...], d_s[...]), matrix, 0, grads[matrix])
-        between()
+    third_add(steps // per_turn - 1)
+    for i in range(3):
+        stage_of[(2 + i, steps // per_turn - 1)] = lambda: None
+    between()
     for name in ("wq", "wk", "wv", "x"):
         loads[name].wait()
 
@@ -887,8 +1050,14 @@
         small_out[0:1, :] = small_out[0:1, :] + dgain
         cot_s[at, :] = (h1_s[at, :] + dv).astype(LOW)
 
-    loop(count // block, input_back)
-    last = pltpu.make_async_copy(cot_s, tokens_grad, last_sem)
+    for i in range(4):
+        share = count // block // 4
+        loop(share, lambda j, i=i: input_back(j + i * share))
+        if i == 0:
+            third_done(steps // per_turn - 1)
+        if i < 3:
+            between()
+    last = pltpu.make_async_copy(cot_s, tokens_grad, last_sem.at[0])
     last.start()
 
     def small_copy(bit):
@@ -911,12 +1080,14 @@
             small_copy(bit + 1).start()
     act_on(actions[len(actions) * len(names) // (len(names) + 1) :])
     last.wait()
-    for copy in stage_of.values():
-        copy.wait()
+    if early:
+        u_copy.wait()
+    for done in stage_of.values():
+        done()
 
 
 def backward(
-    sizes, cot, pooled, lengths, doc_groups, positives, act, slope, wo, wi, n2, h1, ho, q, k, v, n1, tokens, lse,
+    sizes, cot, pooled, sums, lengths, doc_groups, positives, act, slope, wo, wi, n2, h1, ho, q, k, v, n1, tokens, lse,
     wq, wk, wv, wm, gain1, gain2, table,
 ):
     count, width = cot.shape
@@ -925,12 +1096,14 @@
     heads = table.shape[0]
     total = doc_groups.shape[0]
     names = bit_names(sizes)
-    units, items = make_units(sizes, hidden, width)
+    shape = jax.ShapeDtypeStruct
+    early = is_early(sizes, rows)
+    gathered = shape((2, sizes["batch"]) + sums.shape if early else (8, 128), FULL)
+    units, items = make_units(sizes, rows, hidden, width)
     counts = set_counts(sizes)
     order, _ = plan(units, names, counts, [time for _, time in items])
     steps = max(len(unit.steps) for unit in units)
     sets = sum(counts.values())
-    shape = jax.ShapeDtypeStruct
     any_spec = pl.BlockSpec(memory_space=pl.ANY)
     vmem_spec = pl.BlockSpec(memory_space=pltpu.VMEM)
     smem_spec = pl.BlockSpec(memory_space=pltpu.SMEM)
@@ -939,14 +1112,16 @@
     dma = pltpu.SemaphoreType.DMA
     return pl.pallas_call(
         functools.partial(backward_kernel, sizes, units, order, counts),
-        out_shape=squares + squares + [shape((count, width), LOW), shape((24, width), FULL), shape((1, 1), FULL)],
-        in_specs=[any_spec, vmem_spec, smem_spec, vmem_spec, vmem_spec]
+        out_shape=squares + squares
+        + [shape((count, width), LOW), gathered, shape((24, width), FULL), shape((1, 1), FULL)]
+        + [shape((2 * total, width), FULL)],
+        in_specs=[any_spec, vmem_spec, vmem_spec, smem_spec, vmem_spec, vmem_spec]
         + [any_spec] * 12
         + [vmem_spec]
         + [any_spec] * 4
         + [vmem_spec] * 2
         + [smem_spec],
-        out_specs=[any_spec] * 13 + [vmem_spec] * 2,
+        out_specs=[any_spec] * 14 + [vmem_spec] * 3,
         scratch_shapes=[
             pltpu.VMEM((11, count, width), LOW),
             pltpu.VMEM((6, width, width), LOW),
@@ -956,38 +1131,53 @@
             pltpu.VMEM((2, 5, 128, 128), FULL),
             pltpu.VMEM((heads, 1, 128), FULL),
             pltpu.VMEM((2, sizes["batch"], rows, width), FULL),
+            pltpu.VMEM(gathered.shape, FULL),
+            pltpu.VMEM((3, width, UNIT_COLS), FULL),
+            pltpu.VMEM((2, 3, width // 2, UNIT_COLS), FULL),
             pltpu.VMEM((len(names), 24, width), FULL),
-            pltpu.VMEM((sets, units[0].steps[0][2], width), FULL),
-            pltpu.VMEM((sets, max(unit.land for unit in units), width), FULL),
+            pltpu.VMEM((sets, max(unit.steps[0][2] for unit in units), UNIT_COLS), FULL),
+            pltpu.VMEM((sets, max(unit.land for unit in units), UNIT_COLS), FULL),
             dma((32,)),
             dma((8,)),
-            dma((16,)),
-            dma,
-            dma((hops, 3)),
-            dma((hops, 3)),
+            dma((16, 3)),
+            dma((2, 3)),
+            dma((2, 3)),
+            dma((2,)),
+            dma((hops, 6)),
+            dma((hops, 6)),
             dma((len(names),)),
             dma((len(names),)),
             dma((sets, steps, 3)),
             dma((sets, steps, 3)),
             dma((sets,)),
             dma((sets,)),
+            dma((len(units),)),
+            dma((len(units),)),
         ],
         compiler_params=pltpu.CompilerParams(
             collective_id=0, has_side_effects=True, vmem_limit_bytes=int(63.5 * 2**20)
         ),
     )(
-        cot, pooled, lengths, doc_groups.reshape(1, total), positives.reshape(1, total), act, slope, wo, wi, n2, h1,
+        cot, pooled, sums, lengths, doc_groups.reshape(1, total), positives.reshape(1, total), act, slope, wo, wi, n2, h1,
         ho, q, k, v, n1, tokens, lse, wq, wk, wv, wm, gain1, gain2, table,
     )
 
 
-def hand_out_kernel(blocks, count, heads, *refs):
-    sources, (small, loss_in) = refs[:count], refs[count : count + 2]
-    targets = refs[count + 2 : 2 * count + 2]
-    gain1, gain2, table, loss = refs[2 * count + 2 : 2 * count + 6]
-    full, low, in_sem, out_sem = refs[2 * count + 6 :]
+OUT_ROWS = 256
+
+
+def hand_out_kernel(blocks, count, heads, early, *refs):
+    sources, (u_in, small, loss_in, dpooled) = refs[:count], refs[count : count + 4]
+    targets = refs[count + 4 : 2 * count + 4]
+    gain1, gain2, table, loss = refs[2 * count + 4 : 2 * count + 8]
+    full, low, u_s, sums_s, in_sem, out_sem = refs[2 * count + 8 :]
+    width = full.shape[2]
     loads, stores = [], []
-    for i, (array, spot, at) in enumerate(blocks):
+    if early:
+        u_load = pltpu.make_async_copy(u_in, u_s, in_sem.at[len(blocks)])
+        u_load.start()
+    for i, (array, spot, row, col) in enumerate(blocks):
+        at = (pl.ds(row, OUT_ROWS), pl.ds(col, width))
         held = (low if sources[array].dtype == LOW else full).at[spot]
         loads.append(pltpu.make_async_copy(sources[array].at[at], held, in_sem.at[i]))
         stores.append(pltpu.make_async_copy(held, targets[array].at[at], out_sem.at[i]))
@@ -995,41 +1185,60 @@
         load.start()
     gain1[...] = small[0]
     gain2[...] = small[1]
+    table[...] = small[8 : 8 + heads, 0 : table.shape[1]]
     loss[...] = loss_in[...]
-    table[...] = small[8 : 8 + heads, 0 : table.shape[1]]
-    for load, store in zip(loads, stores):
+    if early:
+        u_load.wait()
+        towers, places, most, _ = u_s.shape
+        parts = targets[0].shape[0] // width
+        rows = most // parts
+        for part in range(parts):
+            for t in range(towers):
+                for b in range(places):
+                    first = (t * places + b) * rows
+                    sums_s[part, first : first + rows, :] = u_s[t, b, part * rows : (part + 1) * rows, :]
+    for i, (load, store) in enumerate(zip(loads, stores)):
         load.wait()
+        array, spot, row, _ = blocks[i]
+        if early and array == 0:
+            some = sums_s[row // width, :, row % width : row % width + OUT_ROWS]
+            full[spot] = full[spot] + lax.dot_general(
+                some, dpooled[...], (((0,), (0,)), ((), ())), precision=HIGHEST, preferred_element_type=FULL
+            )
         store.start()
     for store in stores:
         store.wait()
 
 
-def hand_out(arrays, small, loss, heads, buckets):
+def hand_out(arrays, sums, small, loss, dpooled, heads, buckets):
     width = small.shape[1]
+    early = len(sums.shape) == 4
     blocks, held = [], {FULL: 0, LOW: 0}
     for i, array in enumerate(arrays):
         for col in range(0, array.shape[1], width):
-            for row in range(0, array.shape[0], UNIT_ROWS):
+            for row in range(0, array.shape[0], OUT_ROWS):
                 kind = LOW if array.dtype == LOW else FULL
-                blocks.append((i, held[kind], (pl.ds(row, UNIT_ROWS), pl.ds(col, width))))
+                blocks.append((i, held[kind], row, col))
                 held[kind] += 1
     any_spec = pl.BlockSpec(memory_space=pl.ANY)
     vmem_spec = pl.BlockSpec(memory_space=pltpu.VMEM)
     shape = jax.ShapeDtypeStruct
     return pl.pallas_call(
-        functools.partial(hand_out_kernel, blocks, len(arrays), heads),
+        functools.partial(hand_out_kernel, blocks, len(arrays), heads, early),
         out_shape=[shape(a.shape, a.dtype) for a in arrays]
         + [shape((width,), FULL), shape((width,), FULL), shape((heads, buckets), FULL), shape((1, 1), FULL)],
-        in_specs=[any_spec] * len(arrays) + [vmem_spec] * 2,
+        in_specs=[any_spec] * (len(arrays) + 1) + [vmem_spec] * 3,
         out_specs=[any_spec] * len(arrays) + [vmem_spec] * 4,
         scratch_shapes=[
-            pltpu.VMEM((held[FULL], UNIT_ROWS, width), FULL),
-            pltpu.VMEM((held[LOW], UNIT_ROWS, width), LOW),
-            pltpu.SemaphoreType.DMA((len(blocks),)),
+            pltpu.VMEM((held[FULL], OUT_ROWS, width), FULL),
+            pltpu.VMEM((held[LOW], OUT_ROWS, width), LOW),
+            pltpu.VMEM(sums.shape, FULL),
+            pltpu.VMEM((arrays[0].shape[0] // width, dpooled.shape[0], width) if early else (8, 128), FULL),
+            pltpu.SemaphoreType.DMA((len(blocks) + 1,)),
             pltpu.SemaphoreType.DMA((len(blocks),)),
         ],
         compiler_params=pltpu.CompilerParams(vmem_limit_bytes=63 * 2**20),
-    )(*arrays, small, loss)
+    )(*arrays, sums, small, loss, dpooled)
 
 
 def shards(
@@ -1056,15 +1265,14 @@
     cot = cotangent.reshape(count, width)
     own_lengths = lengths.reshape(rows)
     table = rel_table.T
-    q, k, v, ho, n1, n2, h1, act, slope, result, lse, pooled = forward(
+    q, k, v, ho, n1, n2, h1, act, slope, result, lse, pooled, sums = forward(
         flat, own_lengths, w_query, w_key, w_value, w_mixed, w_inner, w_outer, gain_attn, gain_ffn, table
     )
     found = backward(
-        sizes, cot, pooled, own_lengths, doc_groups, positives, act, slope, w_outer, w_inner, n2, h1, ho, q, k, v, n1,
+        sizes, cot, pooled, sums, own_lengths, doc_groups, positives, act, slope, w_outer, w_inner, n2, h1, ho, q, k, v, n1,
         flat, lse, w_query, w_key, w_value, w_mixed, gain_attn, gain_ffn, table,
     )
-    small, loss = found[13:]
-    given = hand_out(found[6:13], small, loss, heads, buckets)
+    given = hand_out(found[6:13], *found[13:], heads, buckets)
     wo_grad, wi_grad, wq_grad, wk_grad, wv_grad, wm_grad, tokens_grad, gain1_grad, gain2_grad, table_grad, loss = given
     return (
         result.reshape(tokens.shape),

time: 345 us -> 331 us (0.959)
  Pallas kernels: 337 us -> 323 us
    pallas_call x1, Pallas kernels: 267 us -> 250 us  [backward(): pl.pallas_call(functools.partial(backward_kernel, sizes, units, order, co...]
where the time goes in v5:
time: 331 us; the launch traced here: 324 us
  Pallas kernels  323 us (98%)
    pallas_call x1, Pallas kernels, backward(): pl.pallas_call(functools.partial(backward_kernel, sizes, units, order, co...  250 us
    pallas_call x1, Pallas kernels, forward(): pl.pallas_call(forward_kernel, out_shape=[low, low, low, low, low, low, s...  49 us
    pallas_call x1, Pallas kernels, hand_out(): pl.pallas_call(functools.partial(hand_out_kernel, blocks, len(arrays), he...  24.1 us

profile of v5, /device:TPU:0, one launch (start us, length us, event | category | flops | bytes accessed | tf_op | source)
XLA Modules:
  0.0 324.3 jit_solution(11130736101563064698)
XLA Ops:
  0.6 49.0 %shard_map.237 = (bf16[1024,768]{1,0:T(8,128)(2,1)}, bf16[1024,768]{1,0:T(8,128)(2,1)}, bf16[1024,768]{1,0:T(8,128)(2,1)}, bf16[1024,768]{1,0:T(8,128)(2,1)}, bf...) custom-call(bf16[1024,768]{1,0:T(8,128)(2,1)} %bitcast.11, ...), custom_call_target="tpu_custom_call" | custom-call | tf_op jit(solution)/shard_map/pallas_call | solution.py:510
  49.6 250.0 %shard_map.238 = (f32[3072,768]{1,0:T(8,128)}, f32[768,3072]{1,0:T(8,128)}, f32[768,768]{1,0:T(8,128)}, f32[768,768]{1,0:T(8,128)}, f32[768,768]{1,0:T(8,128)}, ...) custom-call(bf16[1024,768]{1,0:T(8,128)(2,1)} %bitcast.13, ...), custom_call_target="tpu_custom_call" | custom-call | tf_op jit(solution)/shard_map/pallas_call | solution.py:1113
  299.6 24.1 %shard_map.239 = (f32[3072,768]{1,0:T(8,128)}, f32[768,3072]{1,0:T(8,128)}, f32[768,768]{1,0:T(8,128)}, f32[768,768]{1,0:T(8,128)}, f32[768,768]{1,0:T(8,128)}, ...) custom-call(f32[3072,768]{1,0:T(8,128)} %get-tuple-element.61.refs_0, ...), custom_call_target="tpu_custom_call" | custom-call | tf_op jit(solution)/shard_map/pallas_call | solution.py:1226

commit v6 on v5

--- a/solution.py
+++ b/solution.py
@@ -15,11 +15,13 @@
 
 
 MESH = pl.DeviceIdType.MESH
-LINK = 45.7e3
+LINK = 46.97e3
 CORE = 500e3
-FLIGHT = 4.0
+FLIGHT = 3.42
+DEPTH = 7.40
+PACE = 0.885
 CLASSES = "ABCD"
-PATTERN = "ABCABD"
+PATTERN = "ACBADBCABADBACBADBCBADBAAABBBCCDAAAB"
 UNIT_COLS = 256
 
 
@@ -34,7 +36,7 @@
 
 
 def set_counts(sizes):
-    return {"A": 7, "B": 7, "C": 4, "D": 4} if sizes["batch"] <= 16 else {"A": 2, "B": 2, "C": 1, "D": 1}
+    return {"A": 6, "B": 6, "C": 4, "D": 4} if sizes["batch"] <= 16 else {"A": 2, "B": 2, "C": 1, "D": 1}
 
 
 def bit_groups(sizes):
@@ -130,7 +132,7 @@
     return {mask: link * (2 ** len(group) - 1) for mask in masks}
 
 
-def plan(units, names, counts, items, depth=8.0):
+def plan(units, names, counts, items, depth=DEPTH):
     free, clock, flight, pending = {}, 0.0, [], []
     idle = {kind: [(kind, i) for i in range(counts[kind])] for kind in CLASSES}
     done, order = 0, [[] for _ in items]
@@ -306,7 +308,7 @@
 
 
 def rows_of(i, size):
-    return pl.ds(pl.multiple_of(i * size, size), size)
+    return pl.ds(i * size if isinstance(i, int) else pl.multiple_of(i * size, size), size)
 
 
 def offset_buckets(shift):
@@ -381,7 +383,8 @@
         scale = lax.rsqrt(jnp.mean(x * x, -1, keepdims=True) + EPSILON)
         n1_s[at, :] = (x * scale * gain1[...].reshape(1, width)).astype(LOW)
 
-    loop(count // block, norm1)
+    for i in range(count // block):
+        norm1(i)
     store(n1_s, n1_out)
     for i, (w_s, p_s, p_out) in enumerate(((wq_s, q_s, q_out), (wk_s, k_s, k_out), (wv_s, v_s, v_out))):
         loads[1 + i].wait()
@@ -390,48 +393,46 @@
             at = rows_of(m, 512)
             p_s[at, :] = dot_nn(n1_s[at, :], w_s[...]).astype(LOW)
 
-        loop(count // 512, project)
+        for m in range(count // 512):
+            project(m)
         store(p_s, p_out)
     blocks = seq // 128
     lanes = lax.broadcasted_iota(jnp.int32, (seq, 2 * size), 1)
     keys = lax.broadcasted_iota(jnp.int32, (128, seq), 0)
 
-    def attend(step):
-        pair = lax.div(step, jnp.int32(rows))
-        row = lax.rem(step, jnp.int32(rows))
-        at = rows_of(row, seq)
+    def attend(pair):
         here = rows_of(pair, 2 * size)
-        limit = lengths[row]
-
-        @pl.when(row == 0)
-        def _():
-            fill_bias(bias_s, table, pair * 2, 2)
-
-        q, k = q_s[at, here], k_s[at, here]
-        vt = v_s[at, here].T
-        found = []
-        for side in range(2):
-            head = pair * 2 + side
-            chosen = jnp.where((lanes >= size) == (side == 1), q, jnp.zeros_like(q))
-            score_s[side] = dot_nt(k, chosen)
-        for side in range(2):
-            head = pair * 2 + side
-            top = jnp.full((1, seq), NEGATIVE, FULL)
-            for jb in range(blocks):
-                strip = score_s[side, jb * 128 : (jb + 1) * 128, :] + bias_strip(bias_s, side, table, head, jb, blocks)
-                strip = jnp.where(keys + jb * 128 < limit, strip, NEGATIVE)
-                score_s[side, jb * 128 : (jb + 1) * 128, :] = strip
-                top = jnp.maximum(top, jnp.max(strip, 0, keepdims=True))
-            mass = jnp.zeros((1, seq), FULL)
-            for jb in range(blocks):
-                strip = jnp.exp(score_s[side, jb * 128 : (jb + 1) * 128, :] - top)
-                mass = mass + jnp.sum(strip, 0, keepdims=True)
-                prob_s[side, jb * 128 : (jb + 1) * 128, :] = strip.astype(LOW)
-            lse_out[row * heads + head] = top + jnp.log(mass)
-            found.append(dot_nn(vt[side * size : (side + 1) * size, :], prob_s[side]) / mass)
-        ho_s[at, here] = jnp.concatenate(found, 0).T.astype(LOW)
-
-    loop(rows * (heads // 2), attend)
+        fill_bias(bias_s, table, pair * 2, 2)
+        for row in range(rows):
+            at = slice(row * seq, (row + 1) * seq)
+            limit = lengths[row]
+            q, k = q_s[at, here], k_s[at, here]
+            vt = v_s[at, here].T
+            found = []
+            for side in range(2):
+                chosen = jnp.where((lanes >= size) == (side == 1), q, jnp.zeros_like(q))
+                score_s[row * 2 + side] = dot_nt(k, chosen)
+            for side in range(2):
+                head = pair * 2 + side
+                spot = row * 2 + side
+                top = jnp.full((1, seq), NEGATIVE, FULL)
+                for jb in range(blocks):
+                    some = slice(jb * 128, (jb + 1) * 128)
+                    strip = score_s[spot, some, :] + bias_strip(bias_s, side, table, head, jb, blocks)
+                    strip = jnp.where(keys + jb * 128 < limit, strip, NEGATIVE)
+                    score_s[spot, some, :] = strip
+                    top = jnp.maximum(top, jnp.max(strip, 0, keepdims=True))
+                mass = jnp.zeros((1, seq), FULL)
+                for jb in range(blocks):
+                    some = slice(jb * 128, (jb + 1) * 128)
+                    strip = jnp.exp(score_s[spot, some, :] - top)
+                    mass = mass + jnp.sum(strip, 0, keepdims=True)
+                    prob_s[spot, some, :] = strip.astype(LOW)
+                lse_out[row * heads + head] = top + jnp.log(mass)
+                found.append(dot_nn(vt[side * size : (side + 1) * size, :], prob_s[spot]) / mass)
+            ho_s[at, here] = jnp.concatenate(found, 0).T.astype(LOW)
+
+    loop(heads // 2, attend)
     store(ho_s, ho_out)
     loads[4].wait()
 
@@ -442,7 +443,8 @@
         scale = lax.rsqrt(jnp.mean(h1 * h1, -1, keepdims=True) + EPSILON)
         n2_s[at, :] = (h1 * scale * gain2[...].reshape(1, width)).astype(LOW)
 
-    loop(count // block, mix)
+    for i in range(count // block):
+        mix(i)
     store(h1_s, h1_out)
     store(n2_s, n2_out)
     loads[5].wait()
@@ -476,7 +478,8 @@
                 total_s[at, :] = output
                 result_s[at, :] = output.astype(LOW)
 
-        loop(count // block, feed)
+        for i in range(count // block):
+            feed(i)
         store(act_s.at[:, columns], act_out.at[:, columns])
         sums = dot_nn(marks, act_s[:, columns])
         for row in range(rows):
@@ -519,8 +522,8 @@
         + [narrow_s] * 6
         + [full_s, wide_s, wide_s, narrow_s, full_s]
         + [
-            pltpu.VMEM((2, seq, seq), FULL),
-            pltpu.VMEM((2, seq, seq), LOW),
+            pltpu.VMEM((2 * rows, seq, seq), FULL),
+            pltpu.VMEM((2 * rows, seq, seq), LOW),
             pltpu.VMEM((2, 3, 128, 128), FULL),
             pltpu.SemaphoreType.DMA((7,)),
             pltpu.SemaphoreType.DMA((24,)),
@@ -576,30 +579,31 @@
 
     def outer():
         for part in range(parts):
-            items.append(("outer", 2.6))
+            items.append(("outer", 4.5 if items else 6.0))
             add(0, part * width, 0, len(items))
 
     if early:
         outer()
-        items.append(("hop", 2.0))
+        items.append(("hop", 3.0))
     else:
         items.append(("hop", 12.0))
     items.append(("loss", 4.0))
     if not early:
         outer()
     for part in range(parts):
-        items.append(("inner", 6.4))
+        items.append(("inner", 6.0))
         add(1, 0, part * width, len(items))
-    items.append(("mix", 4.0))
-    items.append(("mixed", 1.8))
+    items.append(("mix", 3.6))
+    items.append(("mixed", 2.5))
     first = len(items)
-    items += [("attend", 2.5)] * 24
+    for turn in range(24):
+        items.append(("attend", 5.0 if turn % 8 == 7 else 3.5 if turn in (2, 8, 16) else 2.5))
     add(5, 0, 0, first + 4)
     for turn in range(3):
         item = first + 8 * turn + 10 if turn < 2 else first + 25
         blocks.extend((matrix, 0, turn * UNIT_COLS, item) for matrix in range(2, 5))
-    items.append(("flush", 3.0))
-    items += [("input", 1.6)] * 4
+    items.append(("flush", 4.0))
+    items += [("input", 1.4)] * 4
     units = []
     for i, (matrix, row, col, item) in enumerate(blocks):
         kind = PATTERN[i % len(PATTERN)]
@@ -841,7 +845,7 @@
         loads["cot"].wait()
 
     def full_dout(row, i):
-        at = pl.ds(pl.multiple_of(row * seq + i * block, block), block)
+        at = pl.ds(row * seq + i * block, block)
         slot = lax.broadcasted_iota(jnp.int32, (block, 1), 0) + i * block
         return at, cot_s[at, :].astype(FULL) + jnp.where(slot < lengths[row], spread[row], 0.0)
 
@@ -851,7 +855,8 @@
             at, dout = full_dout(row, i)
             dout_s[at, :] = dout.astype(LOW)
 
-        loop(seq // block, round_dout)
+        for i in range(seq // block):
+            round_dout(i)
     between()
 
     if not early:
@@ -874,7 +879,8 @@
             more = dot_nt(dinner, square[parts + part % 2])
             sum_s[at, :] = more if part == 0 else sum_s[at, :] + more
 
-        loop(count // block, inner_back)
+        for i in range(count // block):
+            inner_back(i)
         if part + 2 < parts:
             wi_chunk(part + 2).start()
         stage(parts + part, 1, part, dot_tn(n2_s[...], slope_s[part][...]), grads[1].at[:, cut(part)])
@@ -909,7 +915,8 @@
             cot_s[at, :] = da
             dh_s[at, :] = dot_nt(da, square[0]).astype(LOW)
 
-        loop(seq // block, mix_back)
+        for i in range(seq // block):
+            mix_back(i)
     settle()
     between()
     loads["ho"].wait()
@@ -1050,9 +1057,8 @@
         small_out[0:1, :] = small_out[0:1, :] + dgain
         cot_s[at, :] = (h1_s[at, :] + dv).astype(LOW)
 
-    for i in range(4):
-        share = count // block // 4
-        loop(share, lambda j, i=i: input_back(j + i * share))
+    for i in range(count // block):
+        input_back(i)
         if i == 0:
             third_done(steps // per_turn - 1)
         if i < 3:
@@ -1101,7 +1107,7 @@
     gathered = shape((2, sizes["batch"]) + sums.shape if early else (8, 128), FULL)
     units, items = make_units(sizes, rows, hidden, width)
     counts = set_counts(sizes)
-    order, _ = plan(units, names, counts, [time for _, time in items])
+    order, _ = plan(units, names, counts, [PACE * time for _, time in items])
     steps = max(len(unit.steps) for unit in units)
     sets = sum(counts.values())
     any_spec = pl.BlockSpec(memory_space=pl.ANY)

time: 331 us -> 310 us (0.937)
  Pallas kernels: 323 us -> 304 us
    pallas_call x1, Pallas kernels: 250 us -> 239 us  [backward(): pl.pallas_call(functools.partial(backward_kernel, sizes, units, order, co...]
    pallas_call x1, Pallas kernels: 49 us -> 40.2 us  [forward(): pl.pallas_call(forward_kernel, out_shape=[low, low, low, low, low, low, s...]
where the time goes in v6:
time: 310 us; the launch traced here: 305 us
  Pallas kernels  304 us (98%)
    pallas_call x1, Pallas kernels, backward(): pl.pallas_call(functools.partial(backward_kernel, sizes, units, order, co...  239 us
    pallas_call x1, Pallas kernels, forward(): pl.pallas_call(forward_kernel, out_shape=[low, low, low, low, low, low, s...  40.2 us
    pallas_call x1, Pallas kernels, hand_out(): pl.pallas_call(functools.partial(hand_out_kernel, blocks, len(arrays), he...  24.1 us

profile of v6, /device:TPU:0, one launch (start us, length us, event | category | flops | bytes accessed | tf_op | source)
XLA Modules:
  0.0 304.6 jit_solution(5008641675642840282)
XLA Ops:
  0.6 40.2 %shard_map.237 = (bf16[1024,768]{1,0:T(8,128)(2,1)}, bf16[1024,768]{1,0:T(8,128)(2,1)}, bf16[1024,768]{1,0:T(8,128)(2,1)}, bf16[1024,768]{1,0:T(8,128)(2,1)}, bf...) custom-call(bf16[1024,768]{1,0:T(8,128)(2,1)} %bitcast.11, ...), custom_call_target="tpu_custom_call" | custom-call | tf_op jit(solution)/shard_map/pallas_call | solution.py:513
  40.9 239.4 %shard_map.238 = (f32[3072,768]{1,0:T(8,128)}, f32[768,3072]{1,0:T(8,128)}, f32[768,768]{1,0:T(8,128)}, f32[768,768]{1,0:T(8,128)}, f32[768,768]{1,0:T(8,128)}, ...) custom-call(bf16[1024,768]{1,0:T(8,128)(2,1)} %bitcast.13, ...), custom_call_target="tpu_custom_call" | custom-call | tf_op jit(solution)/shard_map/pallas_call | solution.py:1119
  280.3 24.1 %shard_map.239 = (f32[3072,768]{1,0:T(8,128)}, f32[768,3072]{1,0:T(8,128)}, f32[768,768]{1,0:T(8,128)}, f32[768,768]{1,0:T(8,128)}, f32[768,768]{1,0:T(8,128)}, ...) custom-call(f32[3072,768]{1,0:T(8,128)} %get-tuple-element.61.refs_0, ...), custom_call_target="tpu_custom_call" | custom-call | tf_op jit(solution)/shard_map/pallas_call | solution.py:1232

commit v7 on v6

--- a/solution.py
+++ b/solution.py
@@ -328,11 +328,12 @@
 
 def fill_bias(bias, table, head, count):
     ids = [offset_buckets(shift) for shift, _ in NEAR]
-    for side in range(count):
-        for spot, (shift, members) in enumerate(NEAR):
-            block = jnp.zeros((128, 128), FULL)
-            for b in members:
-                block = jnp.where(ids[spot] == b, table[head + side, b], block)
+    for spot, (shift, members) in enumerate(NEAR):
+        found = [jnp.zeros((128, 128), FULL)] * count
+        for b in members:
+            here = ids[spot] == b
+            found = [jnp.where(here, table[head + side, b], block) for side, block in enumerate(found)]
+        for side, block in enumerate(found):
             bias[side, spot] = block
 
 
@@ -405,13 +406,15 @@
         fill_bias(bias_s, table, pair * 2, 2)
         for row in range(rows):
             at = slice(row * seq, (row + 1) * seq)
-            limit = lengths[row]
             q, k = q_s[at, here], k_s[at, here]
-            vt = v_s[at, here].T
-            found = []
             for side in range(2):
                 chosen = jnp.where((lanes >= size) == (side == 1), q, jnp.zeros_like(q))
                 score_s[row * 2 + side] = dot_nt(k, chosen)
+        for row in range(rows):
+            at = slice(row * seq, (row + 1) * seq)
+            limit = lengths[row]
+            vt = v_s[at, here].T
+            found = []
             for side in range(2):
                 head = pair * 2 + side
                 spot = row * 2 + side

time: 310 us -> 309 us (level)
  no operation moved by 1% of the time
where the time goes in v7:
time: 309 us; the launch traced here: 304 us
  Pallas kernels  303 us (98%)
    pallas_call x1, Pallas kernels, backward(): pl.pallas_call(functools.partial(backward_kernel, sizes, units, order, co...  239 us
    pallas_call x1, Pallas kernels, forward(): pl.pallas_call(forward_kernel, out_shape=[low, low, low, low, low, low, s...  39.9 us
    pallas_call x1, Pallas kernels, hand_out(): pl.pallas_call(functools.partial(hand_out_kernel, blocks, len(arrays), he...  24.1 us

profile of v7, /device:TPU:0, one launch (start us, length us, event | category | flops | bytes accessed | tf_op | source)
XLA Modules:
  0.0 304.4 jit_solution(17968215459329633906)
XLA Ops:
  0.6 39.9 %shard_map.237 = (bf16[1024,768]{1,0:T(8,128)(2,1)}, bf16[1024,768]{1,0:T(8,128)(2,1)}, bf16[1024,768]{1,0:T(8,128)(2,1)}, bf16[1024,768]{1,0:T(8,128)(2,1)}, bf...) custom-call(bf16[1024,768]{1,0:T(8,128)(2,1)} %bitcast.11, ...), custom_call_target="tpu_custom_call" | custom-call | tf_op jit(solution)/shard_map/pallas_call | solution.py:516
  40.6 239.4 %shard_map.238 = (f32[3072,768]{1,0:T(8,128)}, f32[768,3072]{1,0:T(8,128)}, f32[768,768]{1,0:T(8,128)}, f32[768,768]{1,0:T(8,128)}, f32[768,768]{1,0:T(8,128)}, ...) custom-call(bf16[1024,768]{1,0:T(8,128)(2,1)} %bitcast.13, ...), custom_call_target="tpu_custom_call" | custom-call | tf_op jit(solution)/shard_map/pallas_call | solution.py:1122
  280.0 24.1 %shard_map.239 = (f32[3072,768]{1,0:T(8,128)}, f32[768,3072]{1,0:T(8,128)}, f32[768,768]{1,0:T(8,128)}, f32[768,768]{1,0:T(8,128)}, f32[768,768]{1,0:T(8,128)}, ...) custom-call(f32[3072,768]{1,0:T(8,128)} %get-tuple-element.61.refs_0, ...), custom_call_target="tpu_custom_call" | custom-call | tf_op jit(solution)/shard_map/pallas_call | solution.py:1235
